TPU v7x, 32 devices: a whole 2x2x4 slice. The times are simulated.
32 devices in a mesh: grp: 4 (over z), seq: 8 (over y, x, core).
Axes of the slice: x: 2, y: 2, z: 4, core: 2. Of those that a mesh axis runs over, the one named last changes fastest.
Arguments:
- queries: bfloat16 [128, 8192], P(('grp', 'seq')), may hold values from -200 to 200
- new_kv: bfloat16 [128, 2, 1024], P(('grp', 'seq')), may hold values from -8 to 8
- suffix_kv: bfloat16 [128, 2, 128, 1024], P(('grp', 'seq')), may hold values from -8 to 8
- suffix_len: int32 [128], P(('grp', 'seq')), may hold values from 1 to 128, 8192 in all
- prefix_of: int32 [128, 1], P(('grp', 'seq')), may hold values from 0 to 3; in each aligned block of 4 rows (0 to 3, 4 to 7, ...) at most 2 rows name the same one
- prefix_kv: bfloat16 [4, 2, 1024, 1024], P('grp', None, 'seq'), may hold values from -16 to 16
Outputs:
- attended: bfloat16 [128, 8192], P(('grp', 'seq'))
Inputs may be any that keep to these rules, and one draw needn't show every extreme that they name: `prefix_of`: at most 2 of the 4 requests of one device name the same group, and that bound is reached on some device.
All inputs are finite; a program needn't handle non-finite values. No bound on the sum of `suffix_len` on one device may be relied on, other than what follows from the above.
Results may differ from a plain program's by a relative error of at most 0.0029.
Values may be sent and summed in bfloat16 or wider, within the bound.
No kernel may reach another device: no remote copies, remote signals or barrier semaphores. Data moves between devices by JAX's collectives and lax.ppermute only.
A program may use at most 128 MiB of HBM per device.

v0:
```python
import jax
import jax.numpy as jnp
from jax import lax
from jax.sharding import PartitionSpec as P

HEADS = 64
KVH = 8
HEAD = 128
CAP = 2


def suffix_attention(queries, new_kv, suffix_kv, suffix_len, score_scale):
    requests_here = queries.shape[0]
    suffix_span = suffix_kv.shape[2]
    per_group = HEADS // KVH
    query_heads = queries.reshape(requests_here, KVH, per_group, HEAD)
    suffix_keys = suffix_kv[:, 0].reshape(requests_here, suffix_span, KVH, HEAD)
    suffix_values = suffix_kv[:, 1].reshape(requests_here, suffix_span, KVH, HEAD)
    own_key = new_kv[:, 0].reshape(requests_here, KVH, HEAD)
    own_value = new_kv[:, 1].reshape(requests_here, KVH, HEAD)
    scores = (
        jnp.einsum("rkgd,rtkd->rkgt", query_heads, suffix_keys, preferred_element_type=jnp.float32)
        * score_scale
    )
    live_keys = jnp.arange(suffix_span)[None, :] < suffix_len[:, None]
    scores = jnp.where(live_keys[:, None, None, :], scores, -jnp.inf)
    own_score = (
        jnp.einsum("rkgd,rkd->rkg", query_heads, own_key, preferred_element_type=jnp.float32)
        * score_scale
    )
    suffix_max = jnp.maximum(jnp.max(scores, axis=3), own_score)
    expo_terms = jnp.exp(scores - suffix_max[..., None])
    own_expo = jnp.exp(own_score - suffix_max)
    suffix_out = jnp.einsum(
        "rkgt,rtkd->rkgd",
        expo_terms.astype(jnp.bfloat16),
        suffix_values,
        preferred_element_type=jnp.float32,
    )
    suffix_out = suffix_out + jnp.einsum(
        "rkg,rkd->rkgd",
        own_expo.astype(jnp.bfloat16),
        own_value,
        preferred_element_type=jnp.float32,
    )
    suffix_total = jnp.sum(expo_terms, axis=3) + own_expo
    return (
        suffix_out.reshape(requests_here, HEADS, HEAD),
        suffix_max.reshape(requests_here, HEADS),
        suffix_total.reshape(requests_here, HEADS),
    )


def on_device(queries, new_kv, suffix_kv, suffix_len, prefix_of, prefix_kv):
    group_count = lax.axis_size("grp")
    seq_count = lax.axis_size("seq")
    requests_here = queries.shape[0]
    per_group = HEADS // KVH
    width_all = HEADS * HEAD
    score_scale = HEAD ** (-0.5)
    local_slots = group_count * CAP
    all_slots = local_slots * seq_count
    if all_slots % 128 == 0:
        block_slots = 128
    elif all_slots % 64 == 0:
        block_slots = 64
    else:
        block_slots = all_slots
    block_total = all_slots // block_slots
    prefix_here = prefix_kv.shape[2]
    routes = prefix_of[:, 0]
    position = jnp.arange(requests_here)
    earlier = position[None, :] < position[:, None]
    same_group = routes[None, :] == routes[:, None]
    rank_within = jnp.sum((earlier & same_group).astype(jnp.int32), axis=1)
    slot_index = routes * CAP + rank_within
    slot_table = (jnp.arange(local_slots)[:, None] == slot_index[None, :]).astype(jnp.bfloat16)
    outgoing = jnp.dot(slot_table, queries, preferred_element_type=jnp.float32).astype(jnp.bfloat16)
    arrived = lax.all_to_all(
        outgoing.reshape(group_count, CAP, width_all),
        "grp",
        split_axis=0,
        concat_axis=0,
        tiled=True,
    )
    arrived = arrived.reshape(local_slots, width_all)
    suffix_out, suffix_max, suffix_total = suffix_attention(
        queries, new_kv, suffix_kv, suffix_len, score_scale
    )
    cache_here = prefix_kv[0]
    key_rows = cache_here[0].reshape(prefix_here, KVH, HEAD)
    value_rows = cache_here[1].reshape(prefix_here, KVH, HEAD)
    gathered = lax.all_gather(arrived, "seq", axis=0, tiled=True)
    query_blocks = gathered.reshape(block_total, block_slots, KVH, per_group, HEAD)

    def block_max(query_block):
        scores = (
            jnp.einsum("bkgd,tkd->bkgt", query_block, key_rows, preferred_element_type=jnp.float32)
            * score_scale
        )
        return jnp.max(scores, axis=3)

    local_max = lax.map(block_max, query_blocks).reshape(all_slots, KVH, per_group)
    prefix_max = lax.pmax(local_max, "seq")
    max_blocks = prefix_max.reshape(block_total, block_slots, KVH, per_group)

    def block_sums(inputs):
        query_block, max_block = inputs
        scores = (
            jnp.einsum("bkgd,tkd->bkgt", query_block, key_rows, preferred_element_type=jnp.float32)
            * score_scale
        )
        expo_terms = jnp.exp(scores - max_block[..., None])
        partial_value = jnp.einsum(
            "bkgt,tkd->bkgd",
            expo_terms.astype(jnp.bfloat16),
            value_rows,
            preferred_element_type=jnp.float32,
        )
        return (partial_value, jnp.sum(expo_terms, axis=3))

    partial_value, totals = lax.map(block_sums, (query_blocks, max_blocks))
    partial_value = partial_value.reshape(all_slots, width_all)
    totals = totals.reshape(all_slots, HEADS)
    prefix_out, prefix_total = (
        lax.psum_scatter(partial_value, "seq", scatter_dimension=0, tiled=True),
        lax.psum_scatter(totals, "seq", scatter_dimension=0, tiled=True),
    )
    own_max = lax.dynamic_slice_in_dim(
        prefix_max, lax.axis_index("seq") * local_slots, local_slots, 0
    )
    own_max = own_max.reshape(local_slots, HEADS)
    home_out, home_total, home_max = (
        lax.all_to_all(
            prefix_out.reshape(group_count, CAP, width_all),
            "grp",
            split_axis=0,
            concat_axis=0,
            tiled=True,
        ),
        lax.all_to_all(
            prefix_total.reshape(group_count, CAP, HEADS),
            "grp",
            split_axis=0,
            concat_axis=0,
            tiled=True,
        ),
        lax.all_to_all(
            own_max.reshape(group_count, CAP, HEADS), "grp", split_axis=0, concat_axis=0, tiled=True
        ),
    )
    prefix_part = jnp.take(home_out.reshape(local_slots, width_all), slot_index, axis=0)
    prefix_part = prefix_part.reshape(requests_here, HEADS, HEAD)
    prefix_sum = jnp.take(home_total.reshape(local_slots, HEADS), slot_index, axis=0)
    prefix_top = jnp.take(home_max.reshape(local_slots, HEADS), slot_index, axis=0)
    top_all = jnp.maximum(prefix_top, suffix_max)
    from_prefix = jnp.exp(prefix_top - top_all)
    from_suffix = jnp.exp(suffix_max - top_all)
    numer = from_prefix[..., None] * prefix_part + from_suffix[..., None] * suffix_out
    denom = from_prefix * prefix_sum + from_suffix * suffix_total
    return (numer / denom[..., None]).reshape(requests_here, width_all).astype(jnp.bfloat16)


def solution(mesh):
    in_specs = (
        P(("grp", "seq"), None),
        P(("grp", "seq"), None, None),
        P(("grp", "seq"), None, None, None),
        P(("grp", "seq")),
        P(("grp", "seq"), None),
        P("grp", None, "seq", None),
    )
    out_specs = P(("grp", "seq"), None)
    return jax.shard_map(
        on_device, mesh=mesh, in_specs=in_specs, out_specs=out_specs, check_vma=False
    )
```

profile of v0, /device:TPU:0, one launch (start us, length us, event | category | flops | bytes accessed | tf_op | source)
XLA Modules:
  0.0 149.0 jit_solution(11489451414866210028)
XLA Ops:
  6.5 0.9 convert_reduce_fusion
  7.5 1.3 compare_and_fusion
  8.7 1.0 convolution_convert_fusion
  9.7 0.1 reshape.112
  9.8 12.2 %all_to_all.20 = bf16[4,2,8192]{2,1,0:T(2,128)(2,1)S(1)} all-to-all(bf16[4,2,8192]{2,1,0:T(2,128)(2,1)S(1)} %reshape.112), channel_id=1, replica_groups=mesh['grp'=4,'seq'=8] {'grp'}, dimensions={0} | all-to-all | bytes 262144 | tf_op jit(solution)/shard_map/all_to_all | solution.py:79
  22.0 0.7 reshape.113
  22.7 0.0 all-gather.2.cloned.1.call-update
  22.8 0.0 reduce-scatter.3.cloned.1.call-start
  22.8 1.1 fusion.33
  23.9 0.8 copy.71
  24.7 0.2 copy.69
  24.9 1.8 %fusion.32 = (bf16[4,1,128,1024]{3,2,1,0:T(8,128)(2,1)S(1)}, bf16[4,1,128,1024]{3,2,1,0:T(8,128)(2,1)S(1)}) fusion(bf16[4,2,128,1024]{3,2,1,0:T(8,128)(2,1)} %param.10), kind=kLoop, calls=%fused_computation.66 | loop fusion | bytes 4194304 | tf_op jit(solution)/shard_map/slice | solution.py:18
  26.7 0.0 copy-start.8
  26.8 0.7 copy.72
  27.4 1.3 copy.70
  28.8 0.6 dynamic-slice.1
  30.0 15.5 %all-gather.2.cloned.1.call-done = bf16[64,8192]{1,0:T(8,128)(2,1)} async-done(((bf16[8,8192]{1,0:T(8,128)(2,1)}), bf16[64,8192]{1,0:T(8,128)(2,1)}) %all-gather.2.cloned.1.call-update) | async-done | bytes 1048592 | tf_op jit(solution)/shard_map/all_gather | solution.py:93
  45.5 1.5 %copy.73 = bf16[8,8,64,128]{3,2,1,0:T(8,128)(2,1)S(1)} copy(bf16[8,8,64,128]{3,1,2,0:T(8,128)(2,1)} %bitcast.108) | data formatting | bytes 2097152
  47.0 1.5 %bitcast_reduce_fusion = (f32[64,8,8]{2,0,1:T(8,128)}, f32[8,64,8,128]{3,2,1,0:T(8,128)S(1)}) fusion(bf16[128,8,128,1]{0,2,3,1:T(8,128)(2,1)S(1)} %bitcast.106, bf16[64,8,8,128]{3,2,1,0:T(8,128)(2,1)S(1)} %bitcast.103), kind=kOutput, calls=%fused_computation.6 | convolution fusion | flops 135262208 | bytes 3424256 | tf_op jit(solution)/shard_map/while/body/eval_jaxpr/bkgd,tkd->bkgt/dot_general | solution.py:98
  48.5 26.8 %pmax.7 = f32[64,8,8]{2,0,1:T(8,128)S(1)} all-reduce(f32[64,8,8]{2,0,1:T(8,128)} %get-tuple-element.52), channel_id=1, replica_groups=mesh['grp'=4,'seq'=8] {'seq'}, use_global_device_ids=true, to_apply=%region_2.3 | all-reduce | flops 4096 | bytes 32768 | tf_op jit(solution)/shard_map/pmax | solution.py:104
  75.3 1.9 %convolution_bitcast_fusion = f32[64,8,8,128]{3,2,0,1:T(8,128)S(1)} fusion(bf16[128,8,128,1]{0,2,3,1:T(8,128)(2,1)} %bitcast.107, f32[8,64,8,128]{3,2,1,0:T(8,128)S(1)} %get-tuple-element.53, f32[64,8,8]{2,0,1:T(8,128)S(1)} %pmax.7), kind=kOutput, calls=%fused_computation.10 | convolution fusion | flops 135790592 | bytes 4472832 | tf_op jit(solution)/shard_map/while/body/eval_jaxpr/bkgt,tkd->bkgd/dot_general | solution.py:114
  77.2 0.3 copy.52
  77.4 2.5 %copy.107 = f32[8,8,64,128]{3,1,2,0:T(8,128)} copy(f32[8,8,64,128]{3,2,1,0:T(8,128)S(1)} %bitcast.102) | data formatting | bytes 4194304
  80.0 0.0 reduce-scatter.3.cloned.1.call-update
  80.0 0.6 pad_clamp_fusion.1
  80.6 0.0 copy-done.7
  80.7 0.1 iota_compare_fusion.2
  80.7 0.1 copy-done
  80.9 0.1 fusion.15
  81.0 1.7 %fusion.34 = (f32[4,8,8]{2,1,0:T(8,128)S(1)}, f32[4,8,8,128]{3,2,1,0:T(8,128)S(1)}) fusion(bf16[4,128,8,128]{1,3,2,0:T(8,128)(2,1)} %bitcast.105, bf16[1,4,64,128]{3,1,2,0:T(4,128)(2,1)S(1)} %bitcast.110, pred[4,128]{1,0:T(4,128)(4,1)S(1)} %iota_compare_fusion.2), kind=kOutput, calls=%fused_computation.68 | convolution fusion | flops 8486656 | bytes 1246720 | tf_op jit(solution)/shard_map/rkgd,rtkd->rkgt/dot_general | solution.py:22
  82.7 0.2 fusion.12
  82.9 1.2 and_bitcast_fusion
  84.2 0.6 convert_convert_fusion
  84.8 0.7 fusion.3
  85.5 0.1 reshape_reshape.3
  85.6 0.7 reshape.165
  86.3 4.6 %all-to-all-start.1 = ((f32[4,1,128]{2,1,0:T(1,128)}), f32[4,1,128]{2,1,0:T(1,128)S(1)}, u32[]{:S(2)}, u32[]{:S(2)}) async-start(f32[4,1,128]{2,1,0:T(1,128)} %reshape.165), calls=%async_computation.1 | async-start | bytes 4096 | tf_op jit(solution)/shard_map/all_to_all | solution.py:148
  90.9 1.3 fusion.1
  92.2 0.1 copy.55
  92.3 22.6 %all-reduce = f32[64,64]{0,1:T(8,128)S(1)} all-reduce(f32[64,64]{0,1:T(8,128)S(1)} %bitcast.111), channel_id=3, replica_groups=mesh['grp'=4,'seq'=8] {'seq'}, use_global_device_ids=true, to_apply=%region_6.8.clone | all-reduce | flops 4096 | bytes 32768
  114.9 0.1 constant_dynamic-slice_fusion
  115.0 0.1 copy.56
  115.1 0.7 reshape.167
  115.8 0.0 all-to-all-done.1
  115.8 5.0 %all-to-all-start.3 = ((f32[4,1,128]{2,1,0:T(1,128)}), f32[4,1,128]{2,1,0:T(1,128)S(1)}, u32[]{:S(2)}, u32[]{:S(2)}) async-start(f32[4,1,128]{2,1,0:T(1,128)} %reshape.167), calls=%async_computation.4 | async-start | bytes 4096 | tf_op jit(solution)/shard_map/all_to_all | solution.py:141
  120.8 0.1 reshape.116
  120.9 0.1 reshape.125
  121.0 0.5 broadcast.116
  121.5 0.7 reduce.1
  122.1 0.1 reshape.166
  122.2 4.0 %all-to-all-done.3 = f32[4,1,128]{2,1,0:T(1,128)S(1)} async-done(((f32[4,1,128]{2,1,0:T(1,128)}), f32[4,1,128]{2,1,0:T(1,128)S(1)}, u32[]{:S(2)}, u32[]{:S(2)}) %all-to-all-start.3) | async-done | bytes 2080 | tf_op jit(solution)/shard_map/all_to_all | solution.py:141
  126.2 0.7 reduce
  126.9 0.1 reshape.168
  126.9 0.7 gather_fusion.1
  127.6 0.7 gather_fusion.2
  128.3 0.1 fusion.26
  128.4 1.8 %reshape.118 = f32[4,2,8192]{2,1,0:T(2,128)} reshape(f32[8,8192]{1,0:T(8,128)} %reduce-scatter.3.cloned.1.call-done) | data formatting | bytes 524288 | tf_op jit(solution)/shard_map/reshape | solution.py:135
  130.2 3.4 %all-to-all-start.2 = ((f32[4,2,8192]{2,1,0:T(2,128)}), f32[4,2,8192]{2,1,0:T(2,128)S(1)}, u32[]{:S(2)}, u32[]{:S(2)}) async-start(f32[4,2,8192]{2,1,0:T(2,128)} %reshape.118), calls=%async_computation.3 | async-start | bytes 524288 | tf_op jit(solution)/shard_map/all_to_all | solution.py:134
  133.6 0.1 broadcast_bitcast_fusion.2
  133.7 0.1 broadcast_bitcast_fusion
  133.8 6.5 %all-to-all-done.2 = f32[4,2,8192]{2,1,0:T(2,128)S(1)} async-done(((f32[4,2,8192]{2,1,0:T(2,128)}), f32[4,2,8192]{2,1,0:T(2,128)S(1)}, u32[]{:S(2)}, u32[]{:S(2)}) %all-to-all-start.2) | async-done | bytes 262176 | tf_op jit(solution)/shard_map/all_to_all | solution.py:134
  140.4 0.2 reshape.119
  140.5 0.6 gather_fusion
  141.2 0.9 fusion.11
  (23 shorter events, 0.1 us)
Async XLA Ops:
  6.5 39.0 %all-gather.2.cloned.1.call-start = ((), (), s32[]{:S(2)}) async-start(), calls=%async_computation.5 | async-start | bytes 1179648 | tf_op jit(solution)/shard_map/all_gather | solution.py:93
  7.4 1.3 copy-start.5
  22.8 105.6 %reduce-scatter.3.cloned.1.call-start = ((), (), s32[]{:S(2)}) async-start(), calls=%async_computation.6 | async-start | bytes 2359296 | tf_op jit(solution)/shard_map/reduce_scatter | solution.py:126
  26.7 2.0 %copy-start.8 = (u32[32]{0:T(128)S(1)}, u32[32]{0:T(128)}, u32[]{:S(2)}) copy-start(u32[32]{0:T(128)} %constant.79) | copy-start | bytes 388
  80.0 0.7 copy-start.7
  80.0 0.9 copy-start
  80.0 0.9 copy-start.2
  85.5 35.3 %copy-start.4 = (s32[4,1]{0,1:T(1,128)S(1)}, s32[4,1]{0,1:T(1,128)}, u32[]{:S(2)}) copy-start(s32[4,1]{0,1:T(1,128)} %get-tuple-element.31) | copy-start | bytes 52
  85.5 35.4 %copy-start.1 = (f32[4,8,8]{2,1,0:T(8,128)S(1)}, f32[4,8,8]{2,1,0:T(8,128)}, u32[]{:S(2)}) copy-start(f32[4,8,8]{2,1,0:T(8,128)} %get-tuple-element.51) | copy-start | bytes 3076
  85.5 42.8 %copy-start.6 = (pred[4]{0:T(512)(128)(4,1)S(1)}, pred[4]{0:T(512)(128)(4,1)}, u32[]{:S(2)}) copy-start(pred[4]{0:T(512)(128)(4,1)} %get-tuple-element.35) | copy-start | bytes 16
  86.3 29.4 %all-to-all-start.1 = ((f32[4,1,128]{2,1,0:T(1,128)}), f32[4,1,128]{2,1,0:T(1,128)S(1)}, u32[]{:S(2)}, u32[]{:S(2)}) async-start(f32[4,1,128]{2,1,0:T(1,128)} %reshape.165), calls=%async_computation.1 | async-start | bytes 4096 | tf_op jit(solution)/shard_map/all_to_all | solution.py:148
  92.2 49.0 %copy-start.3 = (pred[4]{0:T(512)(128)(4,1)S(1)}, pred[4]{0:T(512)(128)(4,1)}, u32[]{:S(2)}) copy-start(pred[4]{0:T(512)(128)(4,1)} %get-tuple-element.30) | copy-start | bytes 16
  115.8 10.4 %all-to-all-start.3 = ((f32[4,1,128]{2,1,0:T(1,128)}), f32[4,1,128]{2,1,0:T(1,128)S(1)}, u32[]{:S(2)}, u32[]{:S(2)}) async-start(f32[4,1,128]{2,1,0:T(1,128)} %reshape.167), calls=%async_computation.4 | async-start | bytes 4096 | tf_op jit(solution)/shard_map/all_to_all | solution.py:141
  130.2 10.2 %all-to-all-start.2 = ((f32[4,2,8192]{2,1,0:T(2,128)}), f32[4,2,8192]{2,1,0:T(2,128)S(1)}, u32[]{:S(2)}, u32[]{:S(2)}) async-start(f32[4,2,8192]{2,1,0:T(2,128)} %reshape.118), calls=%async_computation.3 | async-start | bytes 524288 | tf_op jit(solution)/shard_map/all_to_all | solution.py:134
Sparse Core Ops, SparseCore 0:
  22.9 22.5 all-gather.1
  80.1 41.3 reduce-scatter.2
where the time goes:
time: 150 us; the launch traced here: 149 us
  blocking collectives  61.6 us (41%)
  waiting for transfers between devices  26 us (17%)
  local copies, waits for them, and re-layouts  18.5 us (12%)
  between operations  14.3 us (10%)
  starting transfers between devices  13.1 us (9%)
  other arithmetic  8.59 us (6%)
  matrix products  6.9 us (5%)
    pmax x1, blocking collectives, on_device(): prefix_max = lax.pmax(local_max, 'seq')  26.8 us
    unnamed x1, blocking collectives  22.6 us
    all_gather x1, waiting for transfers between devices, on_device(): gathered = lax.all_gather(arrived, 'seq', axis=0, tiled=True)  15.5 us
    all_to_all x1, blocking collectives, on_device(): lax.all_to_all(outgoing.reshape(group_count, CAP, width_all), 'grp', spli...  12.2 us
    unnamed x32, local copies, waits for them, and re-layouts  9.62 us
    all_to_all x1, waiting for transfers between devices, on_device(): lax.all_to_all(prefix_out.reshape(group_count, CAP, width_all), 'grp', sp...  6.51 us
    all_to_all x1, starting transfers between devices, on_device(): lax.all_to_all(prefix_total.reshape(group_count, CAP, HEADS), 'grp', spli...  5.04 us
    all_to_all x1, starting transfers between devices, on_device(): lax.all_to_all(own_max.reshape(group_count, CAP, HEADS), 'grp', split_axi...  4.6 us
  transfers between devices with their start and end apart: 5, of which 3 were waited for; matrix products, arithmetic and copies ran while one was open for 12% of the time, Pallas kernels for 0%

commit v1 on v0

v1 whole, which is shorter than its diff:
```python
import functools
import math

import jax
import jax.numpy as jnp
from jax import lax
from jax.experimental import pallas as pl
from jax.experimental.pallas import tpu as pltpu
from jax.sharding import PartitionSpec as P

HEADS = 64
KVH = 8
HEAD = 128
CAP = 2
PER = HEADS // KVH
SCALE = HEAD ** (-0.5)
LOG2E = math.log2(math.e)
LN2 = math.log(2.0)
SEND = jnp.bfloat16
ROWS = CAP * PER
BACK = ROWS + PER
NT = (((1,), (1,)), ((), ()))
VMEM = pl.BlockSpec(memory_space=pltpu.VMEM)
SMEM = pl.BlockSpec(memory_space=pltpu.SMEM)
ANY = pl.BlockSpec(memory_space=pl.ANY)


def slots_of(routes_ref, requests):
    routes = [routes_ref[r, 0] for r in range(requests)]
    ranks = []
    for r in range(requests):
        rank = jnp.int32(0)
        for e in range(r):
            rank = rank + jnp.where(routes[e] == routes[r], 1, 0)
        ranks.append(rank)
    return routes, ranks


def pack_queries(groups, splits, routes_ref, q_ref, out_ref, rows_ref, x_ref):
    requests = q_ref.shape[0]
    routes, ranks = slots_of(routes_ref, requests)
    q = q_ref[...].astype(jnp.float32)
    for k in range(KVH):
        for h in range(PER):
            x_ref[h * requests:(h + 1) * requests, k * HEAD:(k + 1) * HEAD] = q[
                :, (k * PER + h) * HEAD:(k * PER + h + 1) * HEAD
            ]
    x = x_ref[...].astype(jnp.bfloat16)
    cols = PER * requests
    total = groups * ROWS
    row = lax.broadcasted_iota(jnp.int32, (total, cols), 0)
    col = lax.broadcasted_iota(jnp.int32, (total, cols), 1)
    wanted = jnp.full((total, cols), -1, jnp.int32)
    for r in range(requests):
        wanted = jnp.where(col % requests == r, routes[r] * CAP + ranks[r], wanted)
    pick = (row // PER == wanted) & (row % PER == col // requests)
    placed = jnp.dot(
        pick.astype(jnp.float32).astype(jnp.bfloat16), x, preferred_element_type=jnp.float32
    ).astype(jnp.bfloat16)
    for g in range(groups):
        for k in range(KVH):
            tile = placed[g * ROWS:(g + 1) * ROWS, k * HEAD:(k + 1) * HEAD]
            for t in range(splits):
                out_ref[g, t, k] = tile
    mine = requests * PER
    row = lax.broadcasted_iota(jnp.int32, (mine, cols), 0)
    col = lax.broadcasted_iota(jnp.int32, (mine, cols), 1)
    turn = (row // PER == col % requests) & (row % PER == col // requests)
    turned = jnp.dot(
        turn.astype(jnp.float32).astype(jnp.bfloat16), x, preferred_element_type=jnp.float32
    )
    for r in range(requests):
        for k in range(KVH):
            rows_ref[r, k * PER:(k + 1) * PER, :] = turned[
                r * PER:(r + 1) * PER, k * HEAD:(k + 1) * HEAD
            ]


def split_heads(kv_ref, *refs):
    outs, sems = refs[:-1], refs[-1]
    mine = lax.axis_index("seq") % KVH
    copies = []
    for j in range(KVH):
        head = jnp.bitwise_xor(mine, j)
        start = pl.multiple_of(head * HEAD, HEAD)
        copies.append(
            pltpu.make_async_copy(kv_ref.at[0, :, :, pl.ds(start, HEAD)], outs[j], sems.at[j])
        )
    for copy in copies:
        copy.start()
    for copy in copies:
        copy.wait()


def suffix_kernel(len_ref, rows_ref, new_ref, kv_ref, out_ref, stat_ref):
    r = pl.program_id(0)
    span = kv_ref.shape[2]
    q = rows_ref[0]
    new = new_ref[pl.ds(r, 1)][0].astype(jnp.float32)
    zero = jnp.zeros((PER, HEAD), jnp.float32)
    wide = jnp.concatenate(
        [
            jnp.concatenate(
                [q[k * PER:(k + 1) * PER] if j == k else zero for j in range(KVH)], axis=1
            )
            for k in range(KVH)
        ],
        axis=0,
    ).astype(jnp.bfloat16)
    raw = lax.dot_general(wide, kv_ref[0, 0], NT, preferred_element_type=jnp.float32)
    live = lax.broadcasted_iota(jnp.int32, raw.shape, 1) < len_ref[r]
    raw = jnp.where(live, raw, -jnp.inf)
    own = jnp.concatenate(
        [
            jnp.sum(
                q[k * PER:(k + 1) * PER] * new[0:1, k * HEAD:(k + 1) * HEAD],
                axis=1,
                keepdims=True,
            )
            for k in range(KVH)
        ],
        axis=0,
    )
    top = jnp.maximum(jnp.max(raw, axis=1, keepdims=True), own)
    weight = jnp.exp2((raw - top) * (SCALE * LOG2E))
    own_weight = jnp.exp2((own - top) * (SCALE * LOG2E))
    total = jnp.sum(weight, axis=1, keepdims=True) + own_weight
    full = jnp.dot(weight.astype(jnp.bfloat16), kv_ref[0, 1], preferred_element_type=jnp.float32)
    own_rounded = own_weight.astype(jnp.bfloat16).astype(jnp.float32)
    for k in range(KVH):
        rows = slice(k * PER, (k + 1) * PER)
        cols = slice(k * HEAD, (k + 1) * HEAD)
        out_ref[0, rows, :] = full[rows, cols] + own_rounded[rows] * new[1:2, cols]
    lane = lax.broadcasted_iota(jnp.int32, (HEADS, HEAD), 1)
    stat_ref[0] = jnp.where(lane == 0, top * SCALE, total)


def prefix_kernel(q_ref, *refs):
    parts, out_ref = refs[:-1], refs[-1]
    keys = jnp.concatenate([part[0] for part in parts], axis=0)
    values = jnp.concatenate([part[1] for part in parts], axis=0)
    sources = q_ref.shape[0]
    step = 8
    lane = lax.broadcasted_iota(jnp.int32, (step * ROWS, HEAD), 1)

    def block(i):
        q = q_ref[pl.ds(i * step, step)].reshape(step * ROWS, HEAD)
        raw = lax.dot_general(q, keys, NT, preferred_element_type=jnp.float32)
        top = jnp.max(raw, axis=1, keepdims=True)
        weight = jnp.exp2((raw - top) * (SCALE * LOG2E))
        total = jnp.sum(weight, axis=1, keepdims=True)
        out = jnp.dot(weight.astype(jnp.bfloat16), values, preferred_element_type=jnp.float32)
        out = (out / total).astype(SEND)
        level = top * SCALE + jnp.log(total)
        first = level.astype(SEND).astype(jnp.float32)
        rest = level - first
        second = rest.astype(SEND).astype(jnp.float32)
        third = rest - second
        stat = jnp.where(
            lane == 0, first, jnp.where(lane == 1, second, jnp.where(lane == 2, third, 0.0))
        )
        for s in range(step):
            at = i * step + s
            out_ref[at, 0:ROWS, :] = out[s * ROWS:(s + 1) * ROWS]
            two = stat[s * ROWS:(s + 1) * ROWS]
            joined = two[0:PER]
            for c in range(1, CAP):
                joined = joined + pltpu.roll(two[c * PER:(c + 1) * PER], c * (HEAD // CAP), 1)
            out_ref[at, ROWS:BACK, :] = joined.astype(SEND)

    if sources // step <= 4:
        for i in range(sources // step):
            block(i)
    else:
        lax.fori_loop(0, sources // step, lambda i, c: (block(i), c)[1], 0)


def join_kernel(splits, routes_ref, back_ref, suffix_ref, stat_ref, out_ref):
    requests = out_ref.shape[0]
    routes, ranks = slots_of(routes_ref, requests)
    lane = lax.broadcasted_iota(jnp.int32, (PER, HEAD), 1) // (HEAD // CAP)
    pieces = [[None] * requests for _ in range(KVH)]
    for r in range(requests):
        stats = stat_ref[r]
        for k in range(KVH):
            rows = slice(k * PER, (k + 1) * PER)
            levels, parts = [], []
            for t in range(splits):
                both = back_ref[routes[r], t, k, 0:ROWS, :].astype(jnp.float32)
                part = both[0:PER]
                for c in range(1, CAP):
                    part = jnp.where(ranks[r] == c, both[c * PER:(c + 1) * PER], part)
                parts.append(part)
                stat = back_ref[routes[r], t, k, ROWS:BACK, :].astype(jnp.float32)
                levels.append(
                    jnp.sum(jnp.where(lane == ranks[r], stat, 0.0), axis=1, keepdims=True)
                )
            suffix_top = stats[rows, 0:1]
            top = suffix_top
            for level in levels:
                top = jnp.maximum(top, level)
            from_suffix = jnp.exp(suffix_top - top)
            numer = from_suffix * suffix_ref[r, rows, :]
            denom = from_suffix * stats[rows, 1:2]
            for level, part in zip(levels, parts):
                from_prefix = jnp.exp(level - top)
                numer = numer + from_prefix * part
                denom = denom + from_prefix
            pieces[k][r] = numer / denom
    stacked = jnp.concatenate(
        [jnp.concatenate(pieces[k], axis=0) for k in range(KVH)], axis=1
    ).astype(jnp.bfloat16)
    mine = requests * PER
    row = lax.broadcasted_iota(jnp.int32, (PER * 8, mine), 0)
    col = lax.broadcasted_iota(jnp.int32, (PER * 8, mine), 1)
    turn = (row % 8 == col // PER) & (row // 8 == col % PER)
    turned = jnp.dot(
        turn.astype(jnp.float32).astype(jnp.bfloat16), stacked, preferred_element_type=jnp.float32
    ).astype(jnp.bfloat16)
    turned = turned.astype(jnp.float32)
    for k in range(KVH):
        for h in range(PER):
            out_ref[:, (k * PER + h) * HEAD:(k * PER + h + 1) * HEAD] = turned[
                h * 8:h * 8 + requests, k * HEAD:(k + 1) * HEAD
            ].astype(jnp.bfloat16)


def on_device(queries, new_kv, suffix_kv, suffix_len, prefix_of, prefix_kv):
    groups = lax.axis_size("grp")
    seq = lax.axis_size("seq")
    splits = seq // KVH
    requests = queries.shape[0]
    span = suffix_kv.shape[2]
    here = prefix_kv.shape[2]
    everyone = ("grp", "seq")

    outgoing, rows = pl.pallas_call(
        functools.partial(pack_queries, groups, splits),
        out_shape=(
            jax.ShapeDtypeStruct((groups, splits, KVH, ROWS, HEAD), jnp.bfloat16),
            jax.ShapeDtypeStruct((requests, HEADS, HEAD), jnp.float32),
        ),
        in_specs=[SMEM, VMEM],
        out_specs=(VMEM, VMEM),
        scratch_shapes=[pltpu.VMEM((PER * requests, KVH * HEAD), jnp.float32)],
        name="pack_queries",
    )(prefix_of, queries)

    blocks = pl.pallas_call(
        split_heads,
        out_shape=[jax.ShapeDtypeStruct((2, here, HEAD), jnp.bfloat16)] * KVH,
        in_specs=[ANY],
        out_specs=[ANY] * KVH,
        scratch_shapes=[pltpu.SemaphoreType.DMA((KVH,))],
        name="split_heads",
    )(prefix_kv)
    parts = [blocks[0]]
    for j in range(1, KVH):
        parts.append(lax.ppermute(blocks[j], "seq", [(s, s ^ j) for s in range(seq)]))

    arrived = lax.all_to_all(
        outgoing.reshape(groups * seq, ROWS, HEAD), everyone, split_axis=0, concat_axis=0, tiled=True
    )

    suffix_out, suffix_stat = pl.pallas_call(
        suffix_kernel,
        grid=(requests,),
        out_shape=(
            jax.ShapeDtypeStruct((requests, HEADS, HEAD), jnp.float32),
            jax.ShapeDtypeStruct((requests, HEADS, HEAD), jnp.float32),
        ),
        in_specs=[
            SMEM,
            pl.BlockSpec((1, HEADS, HEAD), lambda r: (r, 0, 0)),
            pl.BlockSpec((requests, 2, KVH * HEAD), lambda r: (0, 0, 0)),
            pl.BlockSpec((1, 2, span, KVH * HEAD), lambda r: (r, 0, 0, 0)),
        ],
        out_specs=(
            pl.BlockSpec((1, HEADS, HEAD), lambda r: (r, 0, 0)),
            pl.BlockSpec((1, HEADS, HEAD), lambda r: (r, 0, 0)),
        ),
        cost_estimate=pl.CostEstimate(
            flops=4 * requests * HEADS * KVH * HEAD * span,
            bytes_accessed=2 * suffix_kv.size,
            transcendentals=requests * HEADS * span,
        ),
        name="suffix_attention",
    )(suffix_len, rows, new_kv, suffix_kv)

    back = pl.pallas_call(
        prefix_kernel,
        out_shape=jax.ShapeDtypeStruct((groups * seq, BACK, HEAD), SEND),
        in_specs=[VMEM] * (1 + KVH),
        out_specs=VMEM,
        compiler_params=pltpu.CompilerParams(vmem_limit_bytes=32 * 1024 * 1024),
        name="prefix_attention",
    )(arrived, *parts)

    home = lax.all_to_all(back, everyone, split_axis=0, concat_axis=0, tiled=True)

    return pl.pallas_call(
        functools.partial(join_kernel, splits),
        out_shape=jax.ShapeDtypeStruct((requests, HEADS * HEAD), jnp.bfloat16),
        in_specs=[SMEM, VMEM, VMEM, VMEM],
        out_specs=VMEM,
        name="join",
    )(prefix_of, home.reshape(groups, splits, KVH, BACK, HEAD), suffix_out, suffix_stat)


def solution(mesh):
    in_specs = (
        P(("grp", "seq"), None),
        P(("grp", "seq"), None, None),
        P(("grp", "seq"), None, None, None),
        P(("grp", "seq")),
        P(("grp", "seq"), None),
        P("grp", None, "seq", None),
    )
    out_specs = P(("grp", "seq"), None)
    return jax.shard_map(
        on_device, mesh=mesh, in_specs=in_specs, out_specs=out_specs, check_vma=False
    )
```

time: 150 us -> 59.7 us (0.40)
  blocking collectives: 61.6 us -> 0 us
  Pallas kernels: 0 us -> 28.2 us
  waiting for transfers between devices: 26 us -> 9.33 us
  local copies, waits for them, and re-layouts: 18.5 us -> 2.83 us
  between operations: 14.3 us -> 0.04 us
  other arithmetic: 8.59 us -> 0 us
  matrix products: 6.9 us -> 0 us
  starting transfers between devices: 13.1 us -> 18.8 us
    pallas_call x0 -> x5, Pallas kernels: none -> 28.2 us  [the longest x1 17.1 us: on_device(): pl.pallas_call(split_heads, out_shape=[jax.ShapeDtypeStruct((2, here, HEA...]
    pmax x1 -> x0, blocking collectives: 26.8 us -> none  [on_device(): prefix_max = lax.pmax(local_max, 'seq')]
    unnamed x1 -> x0, blocking collectives: 22.6 us -> none
    all_gather x1 -> x0, waiting for transfers between devices: 15.5 us -> none  [on_device(): gathered = lax.all_gather(arrived, 'seq', axis=0, tiled=True)]
    all_to_all x1 -> x0, blocking collectives: 12.2 us -> none  [on_device(): lax.all_to_all(outgoing.reshape(group_count, CAP, width_all), 'grp', spli...]
    dot_general x6 -> x0, matrix products: 6.9 us -> none  [the longest x1 1.87 us: block_sums(): jnp.einsum('bkgt,tkd->bkgd', expo_terms.astype(jnp.bfloat16), value_rows,...]
    unnamed x32 -> x5, local copies, waits for them, and re-layouts: 9.62 us -> 2.83 us
    ppermute x0 -> x7, starting transfers between devices: none -> 6.59 us  [on_device(): lax.ppermute(blocks[j], 'seq', [(s, s ^ j) for s in range(seq)])]
  transfers between devices with their start and end apart: 5 -> 9, of which waited for: 3 -> 5; matrix products, arithmetic and copies ran while one was open for 12% -> 0% of each run, Pallas kernels for 0% -> 37%
where the time goes in v1:
time: 59.7 us; the launch traced here: 59.1 us
  Pallas kernels  28.2 us (47%)
  starting transfers between devices  18.8 us (31%)
  waiting for transfers between devices  9.33 us (16%)
  local copies, waits for them, and re-layouts  2.83 us (5%)
    pallas_call x1, Pallas kernels, on_device(): pl.pallas_call(split_heads, out_shape=[jax.ShapeDtypeStruct((2, here, HEA...  17.1 us
    all_to_all x1, starting transfers between devices, on_device(): lax.all_to_all(outgoing.reshape(groups * seq, ROWS, HEAD), everyone, spli...  7.3 us
    ppermute x7, starting transfers between devices, on_device(): lax.ppermute(blocks[j], 'seq', [(s, s ^ j) for s in range(seq)])  6.59 us
    ppermute x7, waiting for transfers between devices, on_device(): lax.ppermute(blocks[j], 'seq', [(s, s ^ j) for s in range(seq)])  5.05 us
    all_to_all x1, starting transfers between devices, on_device(): lax.all_to_all(back, everyone, split_axis=0, concat_axis=0, tiled=True)  4.87 us
    pallas_call x1, Pallas kernels, on_device(): pl.pallas_call(suffix_kernel, grid=(requests,), out_shape=(jax.ShapeDtype...  4.61 us
    all_to_all x1, waiting for transfers between devices, on_device(): lax.all_to_all(back, everyone, split_axis=0, concat_axis=0, tiled=True)  4.27 us
    unnamed x5, local copies, waits for them, and re-layouts  2.83 us
  transfers between devices with their start and end apart: 9, of which 5 were waited for; matrix products, arithmetic and copies ran while one was open for 0% of the time, Pallas kernels for 37%

profile of v1, /device:TPU:0, one launch (start us, length us, event | category | flops | bytes accessed | tf_op | source)
XLA Modules:
  0.0 59.1 jit_solution(10405718189946263387)
XLA Ops:
  0.0 1.3 %copy.8.routes_ref = s32[4,1]{1,0:T(4,128)} copy(s32[4,1]{0,1:T(1,128)} %param.10) | data formatting | bytes 32 | tf_op args[4]
  1.3 1.7 %pack_queries.1 = (bf16[4,1,8,16,128]{4,3,2,1,0:T(8,128)(2,1)}, f32[4,64,128]{2,1,0:T(8,128)}) custom-call(s32[4,1]{1,0:T(4,128)} %copy.8.routes_ref, bf16[4,8192]{1,0:T(4,128)(2,1)} %q_ref.1), custom_call_target="tpu_custom_call" | custom-call | tf_op jit(solution)/shard_map/pack_queries/pallas_call | solution.py:237
  3.0 7.3 %all-to-all-start = ((bf16[32,16,128]{2,1,0:T(8,128)(2,1)}), bf16[32,16,128]{2,1,0:T(8,128)(2,1)S(1)}, u32[]{:S(2)}, u32[]{:S(2)}) async-start(bf16[32,16,128]{2,1,0:T(8,128)(2,1)} %bitcast.3), calls=%async_computation | async-start | bytes 262144 | tf_op jit(solution)/shard_map/all_to_all | solution.py:261
  10.3 17.1 %split_heads.1 = (bf16[2,128,128]{2,1,0:T(8,128)(2,1)}, bf16[2,128,128]{2,1,0:T(8,128)(2,1)}, bf16[2,128,128]{2,1,0:T(8,128)(2,1)}, bf16[2,128,128]{2,1,0:T(8,12...) custom-call(bf16[1,2,128,1024]{3,2,1,0:T(8,128)(2,1)} %kv_ref.2), custom_call_target="tpu_custom_call" | custom-call | tf_op jit(solution)/shard_map/split_heads/pallas_call | solution.py:249
  27.4 0.3 collective-permute-start
  27.7 1.7 %collective-permute-start.1 = (bf16[2,128,128]{2,1,0:T(8,128)(2,1)}, bf16[2,128,128]{2,1,0:T(8,128)(2,1)S(1)}, u32[]{:S(2)}, u32[]{:S(2)}) collective-permute-start(bf16[2,128,128]{2,1,0:T(8,128)(2,1)} %get-tuple-element.20), channel_id=1, source_target_pairs={{0,2},{1,3},{2,0},{3,1},{4,6},{5,7},{6,4},{7,5},{8,10},{9,11},{10,... | collective-permute-start | bytes 196616 | tf_op jit(solution)/shard_map/ppermute | solution.py:259
  29.4 0.0 collective-permute-start.2
  29.4 1.7 %collective-permute-start.3 = (bf16[2,128,128]{2,1,0:T(8,128)(2,1)}, bf16[2,128,128]{2,1,0:T(8,128)(2,1)S(1)}, u32[]{:S(2)}, u32[]{:S(2)}) collective-permute-start(bf16[2,128,128]{2,1,0:T(8,128)(2,1)} %get-tuple-element.22), channel_id=1, source_target_pairs={{0,4},{1,5},{2,6},{3,7},{4,0},{5,1},{6,2},{7,3},{8,12},{9,13},{10,... | collective-permute-start | bytes 196616 | tf_op jit(solution)/shard_map/ppermute | solution.py:259
  31.1 0.1 collective-permute-start.4
  31.2 0.0 collective-permute-done.refs_1_
  31.2 2.6 %collective-permute-start.5 = (bf16[2,128,128]{2,1,0:T(8,128)(2,1)}, bf16[2,128,128]{2,1,0:T(8,128)(2,1)S(1)}, u32[]{:S(2)}, u32[]{:S(2)}) collective-permute-start(bf16[2,128,128]{2,1,0:T(8,128)(2,1)} %get-tuple-element.24), channel_id=1, source_target_pairs={{0,6},{1,7},{2,4},{3,5},{4,2},{5,3},{6,0},{7,1},{8,14},{9,15},{10,... | collective-permute-start | bytes 196616 | tf_op jit(solution)/shard_map/ppermute | solution.py:259
  33.8 0.0 collective-permute-done.1.refs_2_
  33.8 0.2 collective-permute-start.6
  34.0 0.0 collective-permute-done.2.refs_3_
  34.0 0.1 collective-permute-done.3.refs_4_
  34.1 1.3 %collective-permute-done.4.refs_5_ = bf16[2,128,128]{2,1,0:T(8,128)(2,1)S(1)} collective-permute-done((bf16[2,128,128]{2,1,0:T(8,128)(2,1)}, bf16[2,128,128]{2,1,0:T(8,128)(2,1)S(1)}, u32[]{:S(2)}, u32[]{:S(2)}) %collective-permute-start.4) | collective-permute-done | bytes 65568 | tf_op jit(solution)/shard_map/ppermute | solution.py:259
  35.4 1.4 %collective-permute-done.5.refs_6_ = bf16[2,128,128]{2,1,0:T(8,128)(2,1)S(1)} collective-permute-done((bf16[2,128,128]{2,1,0:T(8,128)(2,1)}, bf16[2,128,128]{2,1,0:T(8,128)(2,1)S(1)}, u32[]{:S(2)}, u32[]{:S(2)}) %collective-permute-start.5) | collective-permute-done | bytes 65568 | tf_op jit(solution)/shard_map/ppermute | solution.py:259
  36.8 2.3 %collective-permute-done.6.refs_7_ = bf16[2,128,128]{2,1,0:T(8,128)(2,1)S(1)} collective-permute-done((bf16[2,128,128]{2,1,0:T(8,128)(2,1)}, bf16[2,128,128]{2,1,0:T(8,128)(2,1)S(1)}, u32[]{:S(2)}, u32[]{:S(2)}) %collective-permute-start.6) | collective-permute-done | bytes 65568 | tf_op jit(solution)/shard_map/ppermute | solution.py:259
  39.1 0.0 all-to-all-done.q_ref
  39.1 0.0 copy-start
  39.1 0.8 %copy-done = bf16[2,128,128]{2,1,0:T(8,128)(2,1)S(1)} copy-done((bf16[2,128,128]{2,1,0:T(8,128)(2,1)S(1)}, bf16[2,128,128]{2,1,0:T(8,128)(2,1)}, u32[]{:S(2)}) %copy-start) | copy-done | bytes 65560
  39.9 2.3 %prefix_attention.1 = bf16[32,24,128]{2,1,0:T(8,128)(2,1)} custom-call(bf16[32,16,128]{2,1,0:T(8,128)(2,1)S(1)} %all-to-all-done.q_ref, bf16[2,128,128]{2,1,0:T(8,128)(2,1)S(1)} %copy-done, bf16[2,128,128]{2,1,0:T(8,128)(2,1)S(1)} %collective-permute-done.refs_1_, bf16[2,128,128]{2,1,0:T(8,128)(2,1)S(1)} %collective-permute-done.1.refs_2_, ...), custom_call_target="tpu_custom_call" | custom-call | tf_op jit(solution)/shard_map/prefix_attention/pallas_call | solution.py:290
  42.3 4.9 %all-to-all-start.1 = ((bf16[32,24,128]{2,1,0:T(8,128)(2,1)}), bf16[32,24,128]{2,1,0:T(8,128)(2,1)S(1)}, u32[]{:S(2)}, u32[]{:S(2)}) async-start(bf16[32,24,128]{2,1,0:T(8,128)(2,1)} %prefix_attention.1), calls=%async_computation.1 | async-start | bytes 393216 | tf_op jit(solution)/shard_map/all_to_all | solution.py:299
  47.1 4.6 %suffix_attention.1 = (f32[4,64,128]{2,1,0:T(8,128)}, f32[4,64,128]{2,1,0:T(8,128)}) custom-call(s32[4]{0:T(128)} %len_ref.1, f32[4,64,128]{2,1,0:T(8,128)} %get-tuple-element.26.rows_ref, bf16[4,2,1024]{2,1,0:T(2,128)(2,1)} %new_ref.1, bf16[4,2,128,1024]{3,2,1,0:T(8,128)(2,1)} %kv_ref.3), custom_call_target="tpu_custom_call" | custom-call | flops 134217728 | bytes 2097152 | tf_op jit(solution)/shard_map/suffix_attention/pallas_call | solution.py:265
  51.8 4.3 %all-to-all-done.1 = bf16[32,24,128]{2,1,0:T(8,128)(2,1)S(1)} async-done(((bf16[32,24,128]{2,1,0:T(8,128)(2,1)}), bf16[32,24,128]{2,1,0:T(8,128)(2,1)S(1)}, u32[]{:S(2)}, u32[]{:S(2)}) %all-to-all-start.1) | async-done | bytes 196640 | tf_op jit(solution)/shard_map/all_to_all | solution.py:299
  56.0 0.0 copy-start.1
  56.0 0.7 %copy-done.1 = bf16[32,24,128]{2,1,0:T(8,128)(2,1)} copy-done((bf16[32,24,128]{2,1,0:T(8,128)(2,1)}, bf16[32,24,128]{2,1,0:T(8,128)(2,1)S(1)}, u32[]{:S(2)}) %copy-start.1) | copy-done | bytes 196632
  56.7 2.4 %join.1 = bf16[4,8192]{1,0:T(4,128)(2,1)} custom-call(s32[4,1]{1,0:T(4,128)} %copy.8.routes_ref, bf16[4,1,8,24,128]{4,3,2,1,0:T(8,128)(2,1)} %bitcast.2, f32[4,64,128]{2,1,0:T(8,128)} %get-tuple-element.27.suffix_ref, f32[4,64,128]{2,1,0:T(8,128)} %get-tuple-element.28.stat_ref), custom_call_target="tpu_custom_call" | custom-call | tf_op jit(solution)/shard_map/join/pallas_call | solution.py:301
Async XLA Ops:
  3.0 36.0 %all-to-all-start = ((bf16[32,16,128]{2,1,0:T(8,128)(2,1)}), bf16[32,16,128]{2,1,0:T(8,128)(2,1)S(1)}, u32[]{:S(2)}, u32[]{:S(2)}) async-start(bf16[32,16,128]{2,1,0:T(8,128)(2,1)} %bitcast.3), calls=%async_computation | async-start | bytes 262144 | tf_op jit(solution)/shard_map/all_to_all | solution.py:261
  27.4 3.8 %collective-permute-start = (bf16[2,128,128]{2,1,0:T(8,128)(2,1)}, bf16[2,128,128]{2,1,0:T(8,128)(2,1)S(1)}, u32[]{:S(2)}, u32[]{:S(2)}) collective-permute-start(bf16[2,128,128]{2,1,0:T(8,128)(2,1)} %get-tuple-element.19), channel_id=1, source_target_pairs={{0,1},{1,0},{2,3},{3,2},{4,5},{5,4},{6,7},{7,6},{8,9},{9,8},{10,11... | collective-permute-start | bytes 196616 | tf_op jit(solution)/shard_map/ppermute | solution.py:259
  27.7 6.1 %collective-permute-start.1 = (bf16[2,128,128]{2,1,0:T(8,128)(2,1)}, bf16[2,128,128]{2,1,0:T(8,128)(2,1)S(1)}, u32[]{:S(2)}, u32[]{:S(2)}) collective-permute-start(bf16[2,128,128]{2,1,0:T(8,128)(2,1)} %get-tuple-element.20), channel_id=1, source_target_pairs={{0,2},{1,3},{2,0},{3,1},{4,6},{5,7},{6,4},{7,5},{8,10},{9,11},{10,... | collective-permute-start | bytes 196616 | tf_op jit(solution)/shard_map/ppermute | solution.py:259
  29.4 4.6 %collective-permute-start.2 = (bf16[2,128,128]{2,1,0:T(8,128)(2,1)}, bf16[2,128,128]{2,1,0:T(8,128)(2,1)S(1)}, u32[]{:S(2)}, u32[]{:S(2)}) collective-permute-start(bf16[2,128,128]{2,1,0:T(8,128)(2,1)} %get-tuple-element.21), channel_id=1, source_target_pairs={{0,3},{1,2},{2,1},{3,0},{4,7},{5,6},{6,5},{7,4},{8,11},{9,10},{10,... | collective-permute-start | bytes 196616 | tf_op jit(solution)/shard_map/ppermute | solution.py:259
  29.4 4.7 %collective-permute-start.3 = (bf16[2,128,128]{2,1,0:T(8,128)(2,1)}, bf16[2,128,128]{2,1,0:T(8,128)(2,1)S(1)}, u32[]{:S(2)}, u32[]{:S(2)}) collective-permute-start(bf16[2,128,128]{2,1,0:T(8,128)(2,1)} %get-tuple-element.22), channel_id=1, source_target_pairs={{0,4},{1,5},{2,6},{3,7},{4,0},{5,1},{6,2},{7,3},{8,12},{9,13},{10,... | collective-permute-start | bytes 196616 | tf_op jit(solution)/shard_map/ppermute | solution.py:259
  31.1 4.3 %collective-permute-start.4 = (bf16[2,128,128]{2,1,0:T(8,128)(2,1)}, bf16[2,128,128]{2,1,0:T(8,128)(2,1)S(1)}, u32[]{:S(2)}, u32[]{:S(2)}) collective-permute-start(bf16[2,128,128]{2,1,0:T(8,128)(2,1)} %get-tuple-element.23), channel_id=1, source_target_pairs={{0,5},{1,4},{2,7},{3,6},{4,1},{5,0},{6,3},{7,2},{8,13},{9,12},{10,... | collective-permute-start | bytes 196616 | tf_op jit(solution)/shard_map/ppermute | solution.py:259
  31.2 5.6 %collective-permute-start.5 = (bf16[2,128,128]{2,1,0:T(8,128)(2,1)}, bf16[2,128,128]{2,1,0:T(8,128)(2,1)S(1)}, u32[]{:S(2)}, u32[]{:S(2)}) collective-permute-start(bf16[2,128,128]{2,1,0:T(8,128)(2,1)} %get-tuple-element.24), channel_id=1, source_target_pairs={{0,6},{1,7},{2,4},{3,5},{4,2},{5,3},{6,0},{7,1},{8,14},{9,15},{10,... | collective-permute-start | bytes 196616 | tf_op jit(solution)/shard_map/ppermute | solution.py:259
  33.8 5.3 %collective-permute-start.6 = (bf16[2,128,128]{2,1,0:T(8,128)(2,1)}, bf16[2,128,128]{2,1,0:T(8,128)(2,1)S(1)}, u32[]{:S(2)}, u32[]{:S(2)}) collective-permute-start(bf16[2,128,128]{2,1,0:T(8,128)(2,1)} %get-tuple-element.25), channel_id=1, source_target_pairs={{0,7},{1,6},{2,5},{3,4},{4,3},{5,2},{6,1},{7,0},{8,15},{9,14},{10,... | collective-permute-start | bytes 196616 | tf_op jit(solution)/shard_map/ppermute | solution.py:259
  39.1 0.8 %copy-start = (bf16[2,128,128]{2,1,0:T(8,128)(2,1)S(1)}, bf16[2,128,128]{2,1,0:T(8,128)(2,1)}, u32[]{:S(2)}) copy-start(bf16[2,128,128]{2,1,0:T(8,128)(2,1)} %get-tuple-element.18.refs_0_) | copy-start | bytes 196612
  42.3 13.8 %all-to-all-start.1 = ((bf16[32,24,128]{2,1,0:T(8,128)(2,1)}), bf16[32,24,128]{2,1,0:T(8,128)(2,1)S(1)}, u32[]{:S(2)}, u32[]{:S(2)}) async-start(bf16[32,24,128]{2,1,0:T(8,128)(2,1)} %prefix_attention.1), calls=%async_computation.1 | async-start | bytes 393216 | tf_op jit(solution)/shard_map/all_to_all | solution.py:299
  56.0 0.7 %copy-start.1 = (bf16[32,24,128]{2,1,0:T(8,128)(2,1)}, bf16[32,24,128]{2,1,0:T(8,128)(2,1)S(1)}, u32[]{:S(2)}) copy-start(bf16[32,24,128]{2,1,0:T(8,128)(2,1)S(1)} %all-to-all-done.1) | copy-start | bytes 589828

commit v2 on v1

--- a/solution.py
+++ b/solution.py
@@ -26,7 +26,7 @@
 
 
 def slots_of(routes_ref, requests):
-    routes = [routes_ref[r, 0] for r in range(requests)]
+    routes = [routes_ref[r] for r in range(requests)]
     ranks = []
     for r in range(requests):
         rank = jnp.int32(0)
@@ -76,69 +76,74 @@
             ]
 
 
-def split_heads(kv_ref, *refs):
-    outs, sems = refs[:-1], refs[-1]
+def prepare(groups, splits, routes_ref, q_ref, kv_ref, out_ref, rows_ref, *refs):
+    blocks, (x_ref, sems) = refs[:KVH], refs[KVH:]
     mine = lax.axis_index("seq") % KVH
     copies = []
     for j in range(KVH):
-        head = jnp.bitwise_xor(mine, j)
-        start = pl.multiple_of(head * HEAD, HEAD)
+        start = pl.multiple_of(jnp.bitwise_xor(mine, j) * HEAD, HEAD)
         copies.append(
-            pltpu.make_async_copy(kv_ref.at[0, :, :, pl.ds(start, HEAD)], outs[j], sems.at[j])
+            pltpu.make_async_copy(kv_ref.at[0, :, :, pl.ds(start, HEAD)], blocks[j], sems.at[j])
         )
     for copy in copies:
         copy.start()
+    pack_queries(groups, splits, routes_ref, q_ref, out_ref, rows_ref, x_ref)
     for copy in copies:
         copy.wait()
 
 
 def suffix_kernel(len_ref, rows_ref, new_ref, kv_ref, out_ref, stat_ref):
-    r = pl.program_id(0)
-    span = kv_ref.shape[2]
-    q = rows_ref[0]
-    new = new_ref[pl.ds(r, 1)][0].astype(jnp.float32)
+    requests = rows_ref.shape[0]
     zero = jnp.zeros((PER, HEAD), jnp.float32)
-    wide = jnp.concatenate(
-        [
-            jnp.concatenate(
-                [q[k * PER:(k + 1) * PER] if j == k else zero for j in range(KVH)], axis=1
-            )
-            for k in range(KVH)
-        ],
-        axis=0,
-    ).astype(jnp.bfloat16)
-    raw = lax.dot_general(wide, kv_ref[0, 0], NT, preferred_element_type=jnp.float32)
-    live = lax.broadcasted_iota(jnp.int32, raw.shape, 1) < len_ref[r]
-    raw = jnp.where(live, raw, -jnp.inf)
-    own = jnp.concatenate(
-        [
-            jnp.sum(
-                q[k * PER:(k + 1) * PER] * new[0:1, k * HEAD:(k + 1) * HEAD],
-                axis=1,
-                keepdims=True,
-            )
-            for k in range(KVH)
-        ],
-        axis=0,
-    )
-    top = jnp.maximum(jnp.max(raw, axis=1, keepdims=True), own)
-    weight = jnp.exp2((raw - top) * (SCALE * LOG2E))
-    own_weight = jnp.exp2((own - top) * (SCALE * LOG2E))
-    total = jnp.sum(weight, axis=1, keepdims=True) + own_weight
-    full = jnp.dot(weight.astype(jnp.bfloat16), kv_ref[0, 1], preferred_element_type=jnp.float32)
-    own_rounded = own_weight.astype(jnp.bfloat16).astype(jnp.float32)
-    for k in range(KVH):
-        rows = slice(k * PER, (k + 1) * PER)
-        cols = slice(k * HEAD, (k + 1) * HEAD)
-        out_ref[0, rows, :] = full[rows, cols] + own_rounded[rows] * new[1:2, cols]
     lane = lax.broadcasted_iota(jnp.int32, (HEADS, HEAD), 1)
-    stat_ref[0] = jnp.where(lane == 0, top * SCALE, total)
-
-
-def prefix_kernel(q_ref, *refs):
-    parts, out_ref = refs[:-1], refs[-1]
-    keys = jnp.concatenate([part[0] for part in parts], axis=0)
-    values = jnp.concatenate([part[1] for part in parts], axis=0)
+    for r in range(requests):
+        q = rows_ref[r]
+        new = new_ref[r].astype(jnp.float32)
+        wide = jnp.concatenate(
+            [
+                jnp.concatenate(
+                    [q[k * PER:(k + 1) * PER] if j == k else zero for j in range(KVH)], axis=1
+                )
+                for k in range(KVH)
+            ],
+            axis=0,
+        ).astype(jnp.bfloat16)
+        raw = lax.dot_general(wide, kv_ref[r, 0], NT, preferred_element_type=jnp.float32)
+        live = lax.broadcasted_iota(jnp.int32, raw.shape, 1) < len_ref[r]
+        raw = jnp.where(live, raw, -jnp.inf)
+        own = jnp.concatenate(
+            [
+                jnp.sum(
+                    q[k * PER:(k + 1) * PER] * new[0:1, k * HEAD:(k + 1) * HEAD],
+                    axis=1,
+                    keepdims=True,
+                )
+                for k in range(KVH)
+            ],
+            axis=0,
+        )
+        top = jnp.maximum(jnp.max(raw, axis=1, keepdims=True), own)
+        weight = jnp.exp2((raw - top) * (SCALE * LOG2E))
+        own_weight = jnp.exp2((own - top) * (SCALE * LOG2E))
+        total = jnp.sum(weight, axis=1, keepdims=True) + own_weight
+        full = jnp.dot(
+            weight.astype(jnp.bfloat16), kv_ref[r, 1], preferred_element_type=jnp.float32
+        )
+        own_rounded = own_weight.astype(jnp.bfloat16).astype(jnp.float32)
+        for k in range(KVH):
+            rows = slice(k * PER, (k + 1) * PER)
+            cols = slice(k * HEAD, (k + 1) * HEAD)
+            out_ref[r, rows, :] = full[rows, cols] + own_rounded[rows] * new[1:2, cols]
+        stat_ref[r] = jnp.where(lane == 0, top * SCALE, total)
+
+
+def prefix_kernel(q_ref, own_ref, *refs):
+    parts, (out_ref, own, sem) = refs[:-3], refs[-3:]
+    copy = pltpu.make_async_copy(own_ref, own, sem)
+    copy.start()
+    copy.wait()
+    keys = jnp.concatenate([part[0] for part in parts] + [own[0]], axis=0)
+    values = jnp.concatenate([part[1] for part in parts] + [own[1]], axis=0)
     sources = q_ref.shape[0]
     step = 8
     lane = lax.broadcasted_iota(jnp.int32, (step * ROWS, HEAD), 1)
@@ -186,12 +191,13 @@
             rows = slice(k * PER, (k + 1) * PER)
             levels, parts = [], []
             for t in range(splits):
-                both = back_ref[routes[r], t, k, 0:ROWS, :].astype(jnp.float32)
+                at = (routes[r] * splits + t) * KVH + k
+                both = back_ref[at, 0:ROWS, :].astype(jnp.float32)
                 part = both[0:PER]
                 for c in range(1, CAP):
                     part = jnp.where(ranks[r] == c, both[c * PER:(c + 1) * PER], part)
                 parts.append(part)
-                stat = back_ref[routes[r], t, k, ROWS:BACK, :].astype(jnp.float32)
+                stat = back_ref[at, ROWS:BACK, :].astype(jnp.float32)
                 levels.append(
                     jnp.sum(jnp.where(lane == ranks[r], stat, 0.0), axis=1, keepdims=True)
                 )
@@ -233,27 +239,23 @@
     span = suffix_kv.shape[2]
     here = prefix_kv.shape[2]
     everyone = ("grp", "seq")
-
-    outgoing, rows = pl.pallas_call(
-        functools.partial(pack_queries, groups, splits),
-        out_shape=(
+    routes = prefix_of.reshape(requests)
+
+    outgoing, rows, *blocks = pl.pallas_call(
+        functools.partial(prepare, groups, splits),
+        out_shape=[
             jax.ShapeDtypeStruct((groups, splits, KVH, ROWS, HEAD), jnp.bfloat16),
             jax.ShapeDtypeStruct((requests, HEADS, HEAD), jnp.float32),
-        ),
-        in_specs=[SMEM, VMEM],
-        out_specs=(VMEM, VMEM),
-        scratch_shapes=[pltpu.VMEM((PER * requests, KVH * HEAD), jnp.float32)],
-        name="pack_queries",
-    )(prefix_of, queries)
-
-    blocks = pl.pallas_call(
-        split_heads,
-        out_shape=[jax.ShapeDtypeStruct((2, here, HEAD), jnp.bfloat16)] * KVH,
-        in_specs=[ANY],
-        out_specs=[ANY] * KVH,
-        scratch_shapes=[pltpu.SemaphoreType.DMA((KVH,))],
-        name="split_heads",
-    )(prefix_kv)
+        ]
+        + [jax.ShapeDtypeStruct((2, here, HEAD), jnp.bfloat16)] * KVH,
+        in_specs=[SMEM, VMEM, ANY],
+        out_specs=[VMEM] * (2 + KVH),
+        scratch_shapes=[
+            pltpu.VMEM((PER * requests, KVH * HEAD), jnp.float32),
+            pltpu.SemaphoreType.DMA((KVH,)),
+        ],
+        name="prepare",
+    )(routes, queries, prefix_kv)
     parts = [blocks[0]]
     for j in range(1, KVH):
         parts.append(lax.ppermute(blocks[j], "seq", [(s, s ^ j) for s in range(seq)]))
@@ -264,21 +266,12 @@
 
     suffix_out, suffix_stat = pl.pallas_call(
         suffix_kernel,
-        grid=(requests,),
         out_shape=(
             jax.ShapeDtypeStruct((requests, HEADS, HEAD), jnp.float32),
             jax.ShapeDtypeStruct((requests, HEADS, HEAD), jnp.float32),
         ),
-        in_specs=[
-            SMEM,
-            pl.BlockSpec((1, HEADS, HEAD), lambda r: (r, 0, 0)),
-            pl.BlockSpec((requests, 2, KVH * HEAD), lambda r: (0, 0, 0)),
-            pl.BlockSpec((1, 2, span, KVH * HEAD), lambda r: (r, 0, 0, 0)),
-        ],
-        out_specs=(
-            pl.BlockSpec((1, HEADS, HEAD), lambda r: (r, 0, 0)),
-            pl.BlockSpec((1, HEADS, HEAD), lambda r: (r, 0, 0)),
-        ),
+        in_specs=[SMEM, VMEM, VMEM, VMEM],
+        out_specs=(VMEM, VMEM),
         cost_estimate=pl.CostEstimate(
             flops=4 * requests * HEADS * KVH * HEAD * span,
             bytes_accessed=2 * suffix_kv.size,
@@ -287,11 +280,19 @@
         name="suffix_attention",
     )(suffix_len, rows, new_kv, suffix_kv)
 
+    arrived, suffix_out, suffix_stat = lax.optimization_barrier(
+        (arrived, suffix_out, suffix_stat)
+    )
+
     back = pl.pallas_call(
         prefix_kernel,
         out_shape=jax.ShapeDtypeStruct((groups * seq, BACK, HEAD), SEND),
-        in_specs=[VMEM] * (1 + KVH),
+        in_specs=[VMEM, ANY] + [VMEM] * (KVH - 1),
         out_specs=VMEM,
+        scratch_shapes=[
+            pltpu.VMEM((2, here, HEAD), jnp.bfloat16),
+            pltpu.SemaphoreType.DMA,
+        ],
         compiler_params=pltpu.CompilerParams(vmem_limit_bytes=32 * 1024 * 1024),
         name="prefix_attention",
     )(arrived, *parts)
@@ -304,7 +305,7 @@
         in_specs=[SMEM, VMEM, VMEM, VMEM],
         out_specs=VMEM,
         name="join",
-    )(prefix_of, home.reshape(groups, splits, KVH, BACK, HEAD), suffix_out, suffix_stat)
+    )(routes, home, suffix_out, suffix_stat)
 
 
 def solution(mesh):

time: 59.7 us -> 40.4 us (0.68)
  Pallas kernels: 28.2 us -> 11.4 us
  blocking collectives: 0 us -> 13.8 us
  waiting for transfers between devices: 9.33 us -> 0.1 us
  starting transfers between devices: 18.8 us -> 14.4 us
  local copies, waits for them, and re-layouts: 2.83 us -> 0.01 us
    pallas_call x3 -> x2, Pallas kernels: 23.4 us -> 7.28 us  [the longest x1 4.38 us: on_device(): pl.pallas_call(suffix_kernel, out_shape=(jax.ShapeDtypeStruct((requests,...]
    all_to_all x0 -> x1, blocking collectives: none -> 13.8 us  [on_device(): lax.all_to_all(back, everyone, split_axis=0, concat_axis=0, tiled=True)]
    ppermute x7, waiting for transfers between devices: 5.05 us -> 0.1 us  [on_device(): lax.ppermute(blocks[j], 'seq', [(s, s ^ j) for s in range(seq)])]
    all_to_all x1 -> x0, starting transfers between devices: 4.87 us -> none  [on_device(): lax.all_to_all(back, everyone, split_axis=0, concat_axis=0, tiled=True)]
    all_to_all x1 -> x0, waiting for transfers between devices: 4.27 us -> none  [on_device(): lax.all_to_all(back, everyone, split_axis=0, concat_axis=0, tiled=True)]
    unnamed x5 -> x2, local copies, waits for them, and re-layouts: 2.83 us -> 0.01 us
    pallas_call x1, Pallas kernels: 2.34 us -> 1.73 us  [on_device(): pl.pallas_call(prefix_kernel, out_shape=jax.ShapeDtypeStruct((groups * se...]
  transfers between devices with their start and end apart: 9 -> 8, of which waited for: 5 -> 1; matrix products, arithmetic and copies ran while one was open for 0% -> 0% of each run, Pallas kernels for 37% -> 11%
where the time goes in v2:
time: 40.4 us; the launch traced here: 39.9 us
  starting transfers between devices  14.4 us (36%)
  blocking collectives  13.8 us (34%)
  Pallas kernels  11.4 us (28%)
    all_to_all x1, blocking collectives, on_device(): lax.all_to_all(back, everyone, split_axis=0, concat_axis=0, tiled=True)  13.8 us
    all_to_all x1, starting transfers between devices, on_device(): lax.all_to_all(outgoing.reshape(groups * seq, ROWS, HEAD), everyone, spli...  7.3 us
    ppermute x7, starting transfers between devices, on_device(): lax.ppermute(blocks[j], 'seq', [(s, s ^ j) for s in range(seq)])  7.14 us
    pallas_call x1, Pallas kernels, on_device(): pl.pallas_call(suffix_kernel, out_shape=(jax.ShapeDtypeStruct((requests,...  4.38 us
    pallas_call x1, Pallas kernels, on_device(): pl.pallas_call(functools.partial(prepare, groups, splits), out_shape=[jax...  2.9 us
    pallas_call x1, Pallas kernels, on_device(): pl.pallas_call(functools.partial(join_kernel, splits), out_shape=jax.Shap...  2.42 us
    pallas_call x1, Pallas kernels, on_device(): pl.pallas_call(prefix_kernel, out_shape=jax.ShapeDtypeStruct((groups * se...  1.73 us
  transfers between devices with their start and end apart: 8, of which 1 were waited for; matrix products, arithmetic and copies ran while one was open for 0% of the time, Pallas kernels for 11%

profile of v2, /device:TPU:0, one launch (start us, length us, event | category | flops | bytes accessed | tf_op | source)
XLA Modules:
  0.0 39.9 jit_solution(15119925691373211072)
XLA Ops:
  0.0 2.9 %prepare.1 = (bf16[4,1,8,16,128]{4,3,2,1,0:T(8,128)(2,1)}, f32[4,64,128]{2,1,0:T(8,128)}, bf16[2,128,128]{2,1,0:T(8,128)(2,1)}, bf16[2,128,128]{2,1,0:T(8,128)(2...) custom-call(s32[4]{0:T(128)} %bitcast.3, ...), custom_call_target="tpu_custom_call" | custom-call | tf_op jit(solution)/shard_map/prepare/pallas_call | solution.py:244
  2.9 0.0 copy-start
  2.9 7.3 %all-to-all-start = ((bf16[32,16,128]{2,1,0:T(8,128)(2,1)}), bf16[32,16,128]{2,1,0:T(8,128)(2,1)S(1)}, u32[]{:S(2)}, u32[]{:S(2)}) async-start(bf16[32,16,128]{2,1,0:T(8,128)(2,1)} %bitcast.2), calls=%async_computation | async-start | bytes 262144 | tf_op jit(solution)/shard_map/all_to_all | solution.py:263
  10.2 0.3 collective-permute-start
  10.5 1.7 %collective-permute-start.1 = (bf16[2,128,128]{2,1,0:T(8,128)(2,1)}, bf16[2,128,128]{2,1,0:T(8,128)(2,1)S(1)}, u32[]{:S(2)}, u32[]{:S(2)}) collective-permute-start(bf16[2,128,128]{2,1,0:T(8,128)(2,1)} %get-tuple-element.27), channel_id=1, source_target_pairs={{0,2},{1,3},{2,0},{3,1},{4,6},{5,7},{6,4},{7,5},{8,10},{9,11},{10,... | collective-permute-start | bytes 196616 | tf_op jit(solution)/shard_map/ppermute | solution.py:261
  12.2 0.0 collective-permute-start.2
  12.2 1.7 %collective-permute-start.3 = (bf16[2,128,128]{2,1,0:T(8,128)(2,1)}, bf16[2,128,128]{2,1,0:T(8,128)(2,1)S(1)}, u32[]{:S(2)}, u32[]{:S(2)}) collective-permute-start(bf16[2,128,128]{2,1,0:T(8,128)(2,1)} %get-tuple-element.29), channel_id=1, source_target_pairs={{0,4},{1,5},{2,6},{3,7},{4,0},{5,1},{6,2},{7,3},{8,12},{9,13},{10,... | collective-permute-start | bytes 196616 | tf_op jit(solution)/shard_map/ppermute | solution.py:261
  13.9 0.1 collective-permute-start.4
  14.0 0.0 collective-permute-done.refs_0_
  14.0 2.6 %collective-permute-start.5 = (bf16[2,128,128]{2,1,0:T(8,128)(2,1)}, bf16[2,128,128]{2,1,0:T(8,128)(2,1)S(1)}, u32[]{:S(2)}, u32[]{:S(2)}) collective-permute-start(bf16[2,128,128]{2,1,0:T(8,128)(2,1)} %get-tuple-element.31), channel_id=1, source_target_pairs={{0,6},{1,7},{2,4},{3,5},{4,2},{5,3},{6,0},{7,1},{8,14},{9,15},{10,... | collective-permute-start | bytes 196616 | tf_op jit(solution)/shard_map/ppermute | solution.py:261
  16.6 0.0 collective-permute-done.1.refs_1_
  16.6 0.8 %collective-permute-start.6 = (bf16[2,128,128]{2,1,0:T(8,128)(2,1)}, bf16[2,128,128]{2,1,0:T(8,128)(2,1)S(1)}, u32[]{:S(2)}, u32[]{:S(2)}) collective-permute-start(bf16[2,128,128]{2,1,0:T(8,128)(2,1)} %get-tuple-element.32), channel_id=1, source_target_pairs={{0,7},{1,6},{2,5},{3,4},{4,3},{5,2},{6,1},{7,0},{8,15},{9,14},{10,... | collective-permute-start | bytes 196616 | tf_op jit(solution)/shard_map/ppermute | solution.py:261
  17.4 4.4 %suffix_attention.1 = (f32[4,64,128]{2,1,0:T(8,128)}, f32[4,64,128]{2,1,0:T(8,128)}) custom-call(s32[4]{0:T(128)} %len_ref.1, f32[4,64,128]{2,1,0:T(8,128)} %get-tuple-element.21.rows_ref, bf16[4,2,1024]{2,1,0:T(2,128)(2,1)} %new_ref.1, bf16[4,2,128,1024]{3,2,1,0:T(8,128)(2,1)} %kv_ref.3), custom_call_target="tpu_custom_call" | custom-call | flops 134217728 | bytes 2097152 | tf_op jit(solution)/shard_map/suffix_attention/pallas_call | solution.py:267
  21.8 0.0 all-to-all-done.q_ref
  21.8 0.0 collective-permute-done.2.refs_2_
  21.8 0.0 collective-permute-done.3.refs_3_
  21.8 0.0 collective-permute-done.4.refs_4_
  21.8 0.0 collective-permute-done.5.refs_5_
  21.8 0.1 collective-permute-done.6.refs_6_
  21.9 0.0 copy-done
  21.9 1.7 %prefix_attention.1 = bf16[32,24,128]{2,1,0:T(8,128)(2,1)S(1)} custom-call(bf16[32,16,128]{2,1,0:T(8,128)(2,1)S(1)} %all-to-all-done.q_ref, bf16[2,128,128]{2,1,0:T(8,128)(2,1)S(1)} %copy-done, bf16[2,128,128]{2,1,0:T(8,128)(2,1)S(1)} %collective-permute-done.refs_0_, bf16[2,128,128]{2,1,0:T(8,128)(2,1)S(1)} %collective-permute-done.1.refs_1_, ...), custom_call_target="tpu_custom_call" | custom-call | tf_op jit(solution)/shard_map/prefix_attention/pallas_call | solution.py:287
  23.6 13.8 %all_to_all.10.back_ref = bf16[32,24,128]{2,1,0:T(8,128)(2,1)} all-to-all(bf16[32,24,128]{2,1,0:T(8,128)(2,1)S(1)} %prefix_attention.1), channel_id=1, replica_groups=mesh['grp'=4,'seq'=8] {'grp','seq'}, dimensions={0} | all-to-all | bytes 393216 | tf_op jit(solution)/shard_map/all_to_all | solution.py:300
  37.4 2.4 %join.1 = bf16[4,8192]{1,0:T(4,128)(2,1)} custom-call(s32[4]{0:T(128)} %bitcast.4, bf16[32,24,128]{2,1,0:T(8,128)(2,1)} %all_to_all.10.back_ref, f32[4,64,128]{2,1,0:T(8,128)} %get-tuple-element.33.suffix_ref, f32[4,64,128]{2,1,0:T(8,128)} %get-tuple-element.34.stat_ref), custom_call_target="tpu_custom_call" | custom-call | tf_op jit(solution)/shard_map/join/pallas_call | solution.py:302
Async XLA Ops:
  2.9 19.0 %copy-start = (bf16[2,128,128]{2,1,0:T(8,128)(2,1)S(1)}, bf16[2,128,128]{2,1,0:T(8,128)(2,1)}, u32[]{:S(2)}) copy-start(bf16[2,128,128]{2,1,0:T(8,128)(2,1)} %get-tuple-element.25.own_ref) | copy-start | bytes 196612
  2.9 18.8 %all-to-all-start = ((bf16[32,16,128]{2,1,0:T(8,128)(2,1)}), bf16[32,16,128]{2,1,0:T(8,128)(2,1)S(1)}, u32[]{:S(2)}, u32[]{:S(2)}) async-start(bf16[32,16,128]{2,1,0:T(8,128)(2,1)} %bitcast.2), calls=%async_computation | async-start | bytes 262144 | tf_op jit(solution)/shard_map/all_to_all | solution.py:263
  10.2 3.8 %collective-permute-start = (bf16[2,128,128]{2,1,0:T(8,128)(2,1)}, bf16[2,128,128]{2,1,0:T(8,128)(2,1)S(1)}, u32[]{:S(2)}, u32[]{:S(2)}) collective-permute-start(bf16[2,128,128]{2,1,0:T(8,128)(2,1)} %get-tuple-element.26), channel_id=1, source_target_pairs={{0,1},{1,0},{2,3},{3,2},{4,5},{5,4},{6,7},{7,6},{8,9},{9,8},{10,11... | collective-permute-start | bytes 196616 | tf_op jit(solution)/shard_map/ppermute | solution.py:261
  10.5 6.1 %collective-permute-start.1 = (bf16[2,128,128]{2,1,0:T(8,128)(2,1)}, bf16[2,128,128]{2,1,0:T(8,128)(2,1)S(1)}, u32[]{:S(2)}, u32[]{:S(2)}) collective-permute-start(bf16[2,128,128]{2,1,0:T(8,128)(2,1)} %get-tuple-element.27), channel_id=1, source_target_pairs={{0,2},{1,3},{2,0},{3,1},{4,6},{5,7},{6,4},{7,5},{8,10},{9,11},{10,... | collective-permute-start | bytes 196616 | tf_op jit(solution)/shard_map/ppermute | solution.py:261
  12.2 9.5 %collective-permute-start.2 = (bf16[2,128,128]{2,1,0:T(8,128)(2,1)}, bf16[2,128,128]{2,1,0:T(8,128)(2,1)S(1)}, u32[]{:S(2)}, u32[]{:S(2)}) collective-permute-start(bf16[2,128,128]{2,1,0:T(8,128)(2,1)} %get-tuple-element.28), channel_id=1, source_target_pairs={{0,3},{1,2},{2,1},{3,0},{4,7},{5,6},{6,5},{7,4},{8,11},{9,10},{10,... | collective-permute-start | bytes 196616 | tf_op jit(solution)/shard_map/ppermute | solution.py:261
  12.2 9.5 %collective-permute-start.3 = (bf16[2,128,128]{2,1,0:T(8,128)(2,1)}, bf16[2,128,128]{2,1,0:T(8,128)(2,1)S(1)}, u32[]{:S(2)}, u32[]{:S(2)}) collective-permute-start(bf16[2,128,128]{2,1,0:T(8,128)(2,1)} %get-tuple-element.29), channel_id=1, source_target_pairs={{0,4},{1,5},{2,6},{3,7},{4,0},{5,1},{6,2},{7,3},{8,12},{9,13},{10,... | collective-permute-start | bytes 196616 | tf_op jit(solution)/shard_map/ppermute | solution.py:261
  13.9 7.9 %collective-permute-start.4 = (bf16[2,128,128]{2,1,0:T(8,128)(2,1)}, bf16[2,128,128]{2,1,0:T(8,128)(2,1)S(1)}, u32[]{:S(2)}, u32[]{:S(2)}) collective-permute-start(bf16[2,128,128]{2,1,0:T(8,128)(2,1)} %get-tuple-element.30), channel_id=1, source_target_pairs={{0,5},{1,4},{2,7},{3,6},{4,1},{5,0},{6,3},{7,2},{8,13},{9,12},{10,... | collective-permute-start | bytes 196616 | tf_op jit(solution)/shard_map/ppermute | solution.py:261
  14.0 7.8 %collective-permute-start.5 = (bf16[2,128,128]{2,1,0:T(8,128)(2,1)}, bf16[2,128,128]{2,1,0:T(8,128)(2,1)S(1)}, u32[]{:S(2)}, u32[]{:S(2)}) collective-permute-start(bf16[2,128,128]{2,1,0:T(8,128)(2,1)} %get-tuple-element.31), channel_id=1, source_target_pairs={{0,6},{1,7},{2,4},{3,5},{4,2},{5,3},{6,0},{7,1},{8,14},{9,15},{10,... | collective-permute-start | bytes 196616 | tf_op jit(solution)/shard_map/ppermute | solution.py:261
  16.6 5.3 %collective-permute-start.6 = (bf16[2,128,128]{2,1,0:T(8,128)(2,1)}, bf16[2,128,128]{2,1,0:T(8,128)(2,1)S(1)}, u32[]{:S(2)}, u32[]{:S(2)}) collective-permute-start(bf16[2,128,128]{2,1,0:T(8,128)(2,1)} %get-tuple-element.32), channel_id=1, source_target_pairs={{0,7},{1,6},{2,5},{3,4},{4,3},{5,2},{6,1},{7,0},{8,15},{9,14},{10,... | collective-permute-start | bytes 196616 | tf_op jit(solution)/shard_map/ppermute | solution.py:261

commit v3 on v2

--- a/solution.py
+++ b/solution.py
@@ -18,11 +18,15 @@
 LN2 = math.log(2.0)
 SEND = jnp.bfloat16
 ROWS = CAP * PER
-BACK = ROWS + PER
+PAIRS = ROWS // 2
+BACK = PAIRS + 1
+HALF = HEAD // 2
 NT = (((1,), (1,)), ((), ()))
 VMEM = pl.BlockSpec(memory_space=pltpu.VMEM)
 SMEM = pl.BlockSpec(memory_space=pltpu.SMEM)
 ANY = pl.BlockSpec(memory_space=pl.ANY)
+in_smem = functools.partial(pltpu.with_memory_space_constraint, memory_space=pltpu.SMEM)
+in_vmem = functools.partial(pltpu.with_memory_space_constraint, memory_space=pltpu.VMEM)
 
 
 def slots_of(routes_ref, requests):
@@ -76,29 +80,50 @@
             ]
 
 
-def prepare(groups, splits, routes_ref, q_ref, kv_ref, out_ref, rows_ref, *refs):
-    blocks, (x_ref, sems) = refs[:KVH], refs[KVH:]
+def prepare(groups, splits, routes_in, q_in, kv_ref, out_ref, rows_ref, routes_ref, *refs):
+    blocks, (q_ref, x_ref, sems) = refs[:KVH], refs[KVH:]
     mine = lax.axis_index("seq") % KVH
-    copies = []
+    first = [
+        pltpu.make_async_copy(routes_in, routes_ref, sems.at[KVH]),
+        pltpu.make_async_copy(q_in, q_ref, sems.at[KVH + 1]),
+    ]
+    later = []
     for j in range(KVH):
         start = pl.multiple_of(jnp.bitwise_xor(mine, j) * HEAD, HEAD)
-        copies.append(
+        later.append(
             pltpu.make_async_copy(kv_ref.at[0, :, :, pl.ds(start, HEAD)], blocks[j], sems.at[j])
         )
-    for copy in copies:
+    for copy in first + later:
         copy.start()
+    for copy in first:
+        copy.wait()
     pack_queries(groups, splits, routes_ref, q_ref, out_ref, rows_ref, x_ref)
-    for copy in copies:
+    for copy in later:
         copy.wait()
 
 
-def suffix_kernel(len_ref, rows_ref, new_ref, kv_ref, out_ref, stat_ref):
+def suffix_kernel(len_in, rows_ref, new_in, kv_in, out_ref, stat_ref, len_ref, new_ref, kv_ref, sems):
     requests = rows_ref.shape[0]
+    small = [
+        pltpu.make_async_copy(len_in, len_ref, sems.at[2 * requests]),
+        pltpu.make_async_copy(new_in, new_ref, sems.at[2 * requests + 1]),
+    ]
+    cached = [
+        [
+            pltpu.make_async_copy(kv_in.at[r, j], kv_ref.at[r, j], sems.at[2 * r + j])
+            for r in range(requests)
+        ]
+        for j in range(2)
+    ]
+    for copy in small + cached[0] + cached[1]:
+        copy.start()
     zero = jnp.zeros((PER, HEAD), jnp.float32)
     lane = lax.broadcasted_iota(jnp.int32, (HEADS, HEAD), 1)
+    for copy in small:
+        copy.wait()
+    news, owns, raws = [], [], []
     for r in range(requests):
         q = rows_ref[r]
-        new = new_ref[r].astype(jnp.float32)
         wide = jnp.concatenate(
             [
                 jnp.concatenate(
@@ -108,48 +133,55 @@
             ],
             axis=0,
         ).astype(jnp.bfloat16)
+        new = new_ref[r].astype(jnp.float32)
+        news.append(new)
+        owns.append(
+            jnp.concatenate(
+                [
+                    jnp.sum(
+                        q[k * PER:(k + 1) * PER] * new[0:1, k * HEAD:(k + 1) * HEAD],
+                        axis=1,
+                        keepdims=True,
+                    )
+                    for k in range(KVH)
+                ],
+                axis=0,
+            )
+        )
+        cached[0][r].wait()
         raw = lax.dot_general(wide, kv_ref[r, 0], NT, preferred_element_type=jnp.float32)
         live = lax.broadcasted_iota(jnp.int32, raw.shape, 1) < len_ref[r]
-        raw = jnp.where(live, raw, -jnp.inf)
-        own = jnp.concatenate(
-            [
-                jnp.sum(
-                    q[k * PER:(k + 1) * PER] * new[0:1, k * HEAD:(k + 1) * HEAD],
-                    axis=1,
-                    keepdims=True,
-                )
-                for k in range(KVH)
-            ],
-            axis=0,
-        )
-        top = jnp.maximum(jnp.max(raw, axis=1, keepdims=True), own)
-        weight = jnp.exp2((raw - top) * (SCALE * LOG2E))
-        own_weight = jnp.exp2((own - top) * (SCALE * LOG2E))
+        raws.append(jnp.where(live, raw, -jnp.inf))
+    weights, own_weights = [], []
+    for r in range(requests):
+        top = jnp.maximum(jnp.max(raws[r], axis=1, keepdims=True), owns[r])
+        weight = jnp.exp2((raws[r] - top) * (SCALE * LOG2E))
+        own_weight = jnp.exp2((owns[r] - top) * (SCALE * LOG2E))
         total = jnp.sum(weight, axis=1, keepdims=True) + own_weight
-        full = jnp.dot(
-            weight.astype(jnp.bfloat16), kv_ref[r, 1], preferred_element_type=jnp.float32
-        )
-        own_rounded = own_weight.astype(jnp.bfloat16).astype(jnp.float32)
+        stat_ref[r] = jnp.where(lane == 0, top * SCALE, total)
+        weights.append(weight.astype(jnp.bfloat16))
+        own_weights.append(own_weight.astype(jnp.bfloat16).astype(jnp.float32))
+    for r in range(requests):
+        cached[1][r].wait()
+        full = jnp.dot(weights[r], kv_ref[r, 1], preferred_element_type=jnp.float32)
         for k in range(KVH):
             rows = slice(k * PER, (k + 1) * PER)
             cols = slice(k * HEAD, (k + 1) * HEAD)
-            out_ref[r, rows, :] = full[rows, cols] + own_rounded[rows] * new[1:2, cols]
-        stat_ref[r] = jnp.where(lane == 0, top * SCALE, total)
-
-
-def prefix_kernel(q_ref, own_ref, *refs):
-    parts, (out_ref, own, sem) = refs[:-3], refs[-3:]
-    copy = pltpu.make_async_copy(own_ref, own, sem)
-    copy.start()
-    copy.wait()
-    keys = jnp.concatenate([part[0] for part in parts] + [own[0]], axis=0)
-    values = jnp.concatenate([part[1] for part in parts] + [own[1]], axis=0)
+            out_ref[r, rows, :] = full[rows, cols] + own_weights[r][rows] * news[r][1:2, cols]
+
+
+def prefix_kernel(q_ref, *refs):
+    parts, out_ref = refs[:-1], refs[-1]
+    keys = jnp.concatenate([part[0] for part in parts], axis=0)
+    values = jnp.concatenate([part[1] for part in parts], axis=0)
     sources = q_ref.shape[0]
-    step = 8
-    lane = lax.broadcasted_iota(jnp.int32, (step * ROWS, HEAD), 1)
+    step = HEAD // ROWS
+    shape = (step * ROWS, HEAD)
+    diagonal = lax.broadcasted_iota(jnp.int32, shape, 0) == lax.broadcasted_iota(jnp.int32, shape, 1)
+    low = lax.broadcasted_iota(jnp.int32, (1, HEAD), 1) < HALF
 
     def block(i):
-        q = q_ref[pl.ds(i * step, step)].reshape(step * ROWS, HEAD)
+        q = q_ref[pl.ds(i * step, step)].reshape(shape)
         raw = lax.dot_general(q, keys, NT, preferred_element_type=jnp.float32)
         top = jnp.max(raw, axis=1, keepdims=True)
         weight = jnp.exp2((raw - top) * (SCALE * LOG2E))
@@ -157,21 +189,20 @@
         out = jnp.dot(weight.astype(jnp.bfloat16), values, preferred_element_type=jnp.float32)
         out = (out / total).astype(SEND)
         level = top * SCALE + jnp.log(total)
+        level = jnp.sum(jnp.where(diagonal, level, 0.0), axis=0, keepdims=True)
         first = level.astype(SEND).astype(jnp.float32)
         rest = level - first
         second = rest.astype(SEND).astype(jnp.float32)
         third = rest - second
-        stat = jnp.where(
-            lane == 0, first, jnp.where(lane == 1, second, jnp.where(lane == 2, third, 0.0))
-        )
+        turned = [pltpu.roll(piece, HALF, 1) for piece in (first, second, third)]
+        halves = [
+            jnp.concatenate([jnp.where(low, first, turned[1]), third], axis=0).astype(SEND),
+            jnp.concatenate([jnp.where(low, turned[0], second), turned[2]], axis=0).astype(SEND),
+        ]
         for s in range(step):
-            at = i * step + s
-            out_ref[at, 0:ROWS, :] = out[s * ROWS:(s + 1) * ROWS]
-            two = stat[s * ROWS:(s + 1) * ROWS]
-            joined = two[0:PER]
-            for c in range(1, CAP):
-                joined = joined + pltpu.roll(two[c * PER:(c + 1) * PER], c * (HEAD // CAP), 1)
-            out_ref[at, ROWS:BACK, :] = joined.astype(SEND)
+            at = (i * step + s) * BACK
+            out_ref[pl.ds(at, PAIRS)] = out[s * ROWS:(s + 1) * ROWS].reshape(PAIRS, 2, HEAD)
+            out_ref[at + PAIRS] = halves[s // (step // 2)]
 
     if sources // step <= 4:
         for i in range(sources // step):
@@ -183,24 +214,25 @@
 def join_kernel(splits, routes_ref, back_ref, suffix_ref, stat_ref, out_ref):
     requests = out_ref.shape[0]
     routes, ranks = slots_of(routes_ref, requests)
-    lane = lax.broadcasted_iota(jnp.int32, (PER, HEAD), 1) // (HEAD // CAP)
+    step = HEAD // ROWS // 2
+    place = lax.axis_index("seq") % step * ROWS
+    lane = lax.broadcasted_iota(jnp.int32, (PER, HEAD), 1)
+    head = lax.broadcasted_iota(jnp.int32, (PER, HEAD), 0)
     pieces = [[None] * requests for _ in range(KVH)]
     for r in range(requests):
         stats = stat_ref[r]
+        once = lane == head + (place + ranks[r] * PER)
+        twice = lane % HALF == head + (place + ranks[r] * PER)
         for k in range(KVH):
             rows = slice(k * PER, (k + 1) * PER)
             levels, parts = [], []
             for t in range(splits):
-                at = (routes[r] * splits + t) * KVH + k
-                both = back_ref[at, 0:ROWS, :].astype(jnp.float32)
-                part = both[0:PER]
-                for c in range(1, CAP):
-                    part = jnp.where(ranks[r] == c, both[c * PER:(c + 1) * PER], part)
-                parts.append(part)
-                stat = back_ref[at, ROWS:BACK, :].astype(jnp.float32)
-                levels.append(
-                    jnp.sum(jnp.where(lane == ranks[r], stat, 0.0), axis=1, keepdims=True)
-                )
+                at = ((routes[r] * splits + t) * KVH + k) * BACK
+                pair = back_ref[pl.ds(at + ranks[r] * (PER // 2), PER // 2)]
+                parts.append(pair.reshape(PER, HEAD).astype(jnp.float32))
+                stat = back_ref[at + PAIRS].astype(jnp.float32)
+                stat = jnp.where(twice, stat[0:1], 0.0) + jnp.where(once, stat[1:2], 0.0)
+                levels.append(jnp.sum(stat, axis=1, keepdims=True))
             suffix_top = stats[rows, 0:1]
             top = suffix_top
             for level in levels:
@@ -241,23 +273,25 @@
     everyone = ("grp", "seq")
     routes = prefix_of.reshape(requests)
 
-    outgoing, rows, *blocks = pl.pallas_call(
+    outgoing, rows, routes, *blocks = pl.pallas_call(
         functools.partial(prepare, groups, splits),
         out_shape=[
             jax.ShapeDtypeStruct((groups, splits, KVH, ROWS, HEAD), jnp.bfloat16),
-            jax.ShapeDtypeStruct((requests, HEADS, HEAD), jnp.float32),
+            pltpu.VMEM((requests, HEADS, HEAD), jnp.float32),
+            pltpu.SMEM((requests,), jnp.int32),
         ]
-        + [jax.ShapeDtypeStruct((2, here, HEAD), jnp.bfloat16)] * KVH,
-        in_specs=[SMEM, VMEM, ANY],
-        out_specs=[VMEM] * (2 + KVH),
+        + [pltpu.VMEM((2, here, HEAD), jnp.bfloat16)] * KVH,
+        in_specs=[ANY, ANY, ANY],
+        out_specs=[VMEM, VMEM, SMEM] + [VMEM] * KVH,
         scratch_shapes=[
+            pltpu.VMEM((requests, HEADS * HEAD), jnp.bfloat16),
             pltpu.VMEM((PER * requests, KVH * HEAD), jnp.float32),
-            pltpu.SemaphoreType.DMA((KVH,)),
+            pltpu.SemaphoreType.DMA((KVH + 2,)),
         ],
         name="prepare",
     )(routes, queries, prefix_kv)
     parts = [blocks[0]]
-    for j in range(1, KVH):
+    for j in reversed(range(1, KVH)):
         parts.append(lax.ppermute(blocks[j], "seq", [(s, s ^ j) for s in range(seq)]))
 
     arrived = lax.all_to_all(
@@ -267,18 +301,24 @@
     suffix_out, suffix_stat = pl.pallas_call(
         suffix_kernel,
         out_shape=(
-            jax.ShapeDtypeStruct((requests, HEADS, HEAD), jnp.float32),
-            jax.ShapeDtypeStruct((requests, HEADS, HEAD), jnp.float32),
+            pltpu.VMEM((requests, HEADS, HEAD), jnp.float32),
+            pltpu.VMEM((requests, HEADS, HEAD), jnp.float32),
         ),
-        in_specs=[SMEM, VMEM, VMEM, VMEM],
+        in_specs=[ANY, VMEM, ANY, ANY],
         out_specs=(VMEM, VMEM),
+        scratch_shapes=[
+            pltpu.SMEM((requests,), jnp.int32),
+            pltpu.VMEM(new_kv.shape, jnp.bfloat16),
+            pltpu.VMEM(suffix_kv.shape, jnp.bfloat16),
+            pltpu.SemaphoreType.DMA((2 * requests + 2,)),
+        ],
         cost_estimate=pl.CostEstimate(
             flops=4 * requests * HEADS * KVH * HEAD * span,
             bytes_accessed=2 * suffix_kv.size,
             transcendentals=requests * HEADS * span,
         ),
         name="suffix_attention",
-    )(suffix_len, rows, new_kv, suffix_kv)
+    )(suffix_len, in_vmem(rows), new_kv, suffix_kv)
 
     arrived, suffix_out, suffix_stat = lax.optimization_barrier(
         (arrived, suffix_out, suffix_stat)
@@ -286,18 +326,14 @@
 
     back = pl.pallas_call(
         prefix_kernel,
-        out_shape=jax.ShapeDtypeStruct((groups * seq, BACK, HEAD), SEND),
-        in_specs=[VMEM, ANY] + [VMEM] * (KVH - 1),
+        out_shape=pltpu.VMEM((groups * seq * BACK, 2, HEAD), SEND),
+        in_specs=[VMEM] * (1 + KVH),
         out_specs=VMEM,
-        scratch_shapes=[
-            pltpu.VMEM((2, here, HEAD), jnp.bfloat16),
-            pltpu.SemaphoreType.DMA,
-        ],
         compiler_params=pltpu.CompilerParams(vmem_limit_bytes=32 * 1024 * 1024),
         name="prefix_attention",
     )(arrived, *parts)
 
-    home = lax.all_to_all(back, everyone, split_axis=0, concat_axis=0, tiled=True)
+    home = in_vmem(lax.all_to_all(back, everyone, split_axis=0, concat_axis=0, tiled=True))
 
     return pl.pallas_call(
         functools.partial(join_kernel, splits),
@@ -305,7 +341,7 @@
         in_specs=[SMEM, VMEM, VMEM, VMEM],
         out_specs=VMEM,
         name="join",
-    )(routes, home, suffix_out, suffix_stat)
+    )(in_smem(routes), home, in_vmem(suffix_out), in_vmem(suffix_stat))
 
 
 def solution(mesh):

time: 40.4 us -> 37 us (0.916)
  Pallas kernels: 11.4 us -> 8.21 us
  blocking collectives: 13.8 us -> 13 us
  waiting for transfers between devices: 0.1 us -> 0.72 us
    pallas_call x2, Pallas kernels: 6.11 us -> 5 us  [the longest x1 3.39 us: on_device(): pl.pallas_call(suffix_kernel, out_shape=(pltpu.VMEM((requests, HEADS, HEA...]
    pallas_call x1, Pallas kernels: 2.9 us -> 1.84 us  [on_device(): pl.pallas_call(functools.partial(prepare, groups, splits), out_shape=[jax...]
    pallas_call x1, Pallas kernels: 2.42 us -> 1.37 us  [on_device(): pl.pallas_call(functools.partial(join_kernel, splits), out_shape=jax.Shap...]
    all_to_all x1, blocking collectives: 13.8 us -> 13 us  [on_device(): lax.all_to_all(back, everyone, split_axis=0, concat_axis=0, tiled=True)]
    ppermute x7, waiting for transfers between devices: 0.1 us -> 0.72 us  [on_device(): lax.ppermute(blocks[j], 'seq', [(s, s ^ j) for s in range(seq)])]
  transfers between devices with their start and end apart: 8 -> 8, of which waited for: 1 -> 1; matrix products, arithmetic and copies ran while one was open for 0% -> 0% of each run, Pallas kernels for 11% -> 9%
where the time goes in v3:
time: 37 us; the launch traced here: 36.7 us
  starting transfers between devices  14.8 us (40%)
  blocking collectives  13 us (35%)
  Pallas kernels  8.21 us (22%)
  waiting for transfers between devices  0.72 us (2%)
    all_to_all x1, blocking collectives, on_device(): lax.all_to_all(back, everyone, split_axis=0, concat_axis=0, tiled=True)  13 us
    ppermute x7, starting transfers between devices, on_device(): lax.ppermute(blocks[j], 'seq', [(s, s ^ j) for s in range(seq)])  7.46 us
    all_to_all x1, starting transfers between devices, on_device(): lax.all_to_all(outgoing.reshape(groups * seq, ROWS, HEAD), everyone, spli...  7.3 us
    pallas_call x1, Pallas kernels, on_device(): pl.pallas_call(suffix_kernel, out_shape=(pltpu.VMEM((requests, HEADS, HEA...  3.39 us
    pallas_call x1, Pallas kernels, on_device(): pl.pallas_call(functools.partial(prepare, groups, splits), out_shape=[jax...  1.84 us
    pallas_call x1, Pallas kernels, on_device(): pl.pallas_call(prefix_kernel, out_shape=pltpu.VMEM((groups * seq * BACK,...  1.61 us
    pallas_call x1, Pallas kernels, on_device(): pl.pallas_call(functools.partial(join_kernel, splits), out_shape=jax.Shap...  1.37 us
  transfers between devices with their start and end apart: 8, of which 1 were waited for; matrix products, arithmetic and copies ran while one was open for 0% of the time, Pallas kernels for 9%

profile of v3, /device:TPU:0, one launch (start us, length us, event | category | flops | bytes accessed | tf_op | source)
XLA Modules:
  0.0 36.7 jit_solution(16208831439737035978)
XLA Ops:
  0.0 1.8 %prepare.1 = (bf16[4,1,8,16,128]{4,3,2,1,0:T(8,128)(2,1)}, f32[4,64,128]{2,1,0:T(8,128)S(1)}, s32[4]{0:T(128)S(4)}, bf16[2,128,128]{2,1,0:T(8,128)(2,1)S(1)}, bf...) custom-call(s32[4]{0:T(128)} %bitcast.3, ...), custom_call_target="tpu_custom_call" | custom-call | tf_op jit(solution)/shard_map/prepare/pallas_call | solution.py:276
  1.8 7.3 %all-to-all-start = ((bf16[32,16,128]{2,1,0:T(8,128)(2,1)}), bf16[32,16,128]{2,1,0:T(8,128)(2,1)S(1)}, u32[]{:S(2)}, u32[]{:S(2)}) async-start(bf16[32,16,128]{2,1,0:T(8,128)(2,1)} %bitcast.2), calls=%async_computation | async-start | bytes 262144 | tf_op jit(solution)/shard_map/all_to_all | solution.py:297
  9.2 2.5 %collective-permute-start = (bf16[2,128,128]{2,1,0:T(8,128)(2,1)S(1)}, bf16[2,128,128]{2,1,0:T(8,128)(2,1)S(1)}, u32[]{:S(2)}, u32[]{:S(2)}) collective-permute-start(bf16[2,128,128]{2,1,0:T(8,128)(2,1)S(1)} %get-tuple-element.28), channel_id=1, source_target_pairs={{0,7},{1,6},{2,5},{3,4},{4,3},{5,2},{6,1},{7,0},{8,15},{9,14},{10,... | collective-permute-start | bytes 196616 | tf_op jit(solution)/shard_map/ppermute | solution.py:295
  11.6 0.4 collective-permute-start.1
  12.0 1.4 %collective-permute-start.2 = (bf16[2,128,128]{2,1,0:T(8,128)(2,1)S(1)}, bf16[2,128,128]{2,1,0:T(8,128)(2,1)S(1)}, u32[]{:S(2)}, u32[]{:S(2)}) collective-permute-start(bf16[2,128,128]{2,1,0:T(8,128)(2,1)S(1)} %get-tuple-element.30), channel_id=1, source_target_pairs={{0,5},{1,4},{2,7},{3,6},{4,1},{5,0},{6,3},{7,2},{8,13},{9,12},{10,... | collective-permute-start | bytes 196616 | tf_op jit(solution)/shard_map/ppermute | solution.py:295
  13.4 0.4 collective-permute-start.3
  13.7 1.4 %collective-permute-start.4 = (bf16[2,128,128]{2,1,0:T(8,128)(2,1)S(1)}, bf16[2,128,128]{2,1,0:T(8,128)(2,1)S(1)}, u32[]{:S(2)}, u32[]{:S(2)}) collective-permute-start(bf16[2,128,128]{2,1,0:T(8,128)(2,1)S(1)} %get-tuple-element.32), channel_id=1, source_target_pairs={{0,3},{1,2},{2,1},{3,0},{4,7},{5,6},{6,5},{7,4},{8,11},{9,10},{10,... | collective-permute-start | bytes 196616 | tf_op jit(solution)/shard_map/ppermute | solution.py:295
  15.2 0.0 collective-permute-done.refs_1_
  15.2 1.5 %collective-permute-start.5 = (bf16[2,128,128]{2,1,0:T(8,128)(2,1)S(1)}, bf16[2,128,128]{2,1,0:T(8,128)(2,1)S(1)}, u32[]{:S(2)}, u32[]{:S(2)}) collective-permute-start(bf16[2,128,128]{2,1,0:T(8,128)(2,1)S(1)} %get-tuple-element.33), channel_id=1, source_target_pairs={{0,2},{1,3},{2,0},{3,1},{4,6},{5,7},{6,4},{7,5},{8,10},{9,11},{10,... | collective-permute-start | bytes 196616 | tf_op jit(solution)/shard_map/ppermute | solution.py:295
  16.6 0.7 %collective-permute-done.1.refs_2_ = bf16[2,128,128]{2,1,0:T(8,128)(2,1)S(1)} collective-permute-done((bf16[2,128,128]{2,1,0:T(8,128)(2,1)S(1)}, bf16[2,128,128]{2,1,0:T(8,128)(2,1)S(1)}, u32[]{:S(2)}, u32[]{:S(2)}) %collective-permute-start.1) | collective-permute-done | bytes 65568 | tf_op jit(solution)/shard_map/ppermute | solution.py:295
  17.3 0.0 collective-permute-start.6
  17.3 3.4 %suffix_attention.1 = (f32[4,64,128]{2,1,0:T(8,128)S(1)}, f32[4,64,128]{2,1,0:T(8,128)S(1)}) custom-call(s32[4]{0:T(128)} %len_in.1, f32[4,64,128]{2,1,0:T(8,128)S(1)} %get-tuple-element.23.rows_ref, bf16[4,2,1024]{2,1,0:T(2,128)(2,1)} %new_in.1, bf16[4,2,128,1024]{3,2,1,0:T(8,128)(2,1)} %kv_in.1), custom_call_target="tpu_custom_call" | custom-call | flops 134217728 | bytes 2097152 | tf_op jit(solution)/shard_map/suffix_attention/pallas_call | solution.py:301
  20.7 0.0 all-to-all-done.q_ref
  20.7 0.0 collective-permute-done.2.refs_3_
  20.7 0.0 collective-permute-done.3.refs_4_
  20.8 0.0 collective-permute-done.4.refs_5_
  20.8 0.0 collective-permute-done.5.refs_6_
  20.8 0.0 collective-permute-done.6.refs_7_
  20.8 1.6 %prefix_attention.1 = bf16[288,2,128]{2,1,0:T(2,128)(2,1)S(1)} custom-call(bf16[32,16,128]{2,1,0:T(8,128)(2,1)S(1)} %all-to-all-done.q_ref, bf16[2,128,128]{2,1,0:T(8,128)(2,1)S(1)} %get-tuple-element.27.refs_0_, bf16[2,128,128]{2,1,0:T(8,128)(2,1)S(1)} %collective-permute-done.refs_1_, bf16[2,128,128]{2,1,0:T(8,128)(2,1)S(1)} %collective-permute-done.1.refs_2_, ...), custom_call_target="tpu_custom_call" | custom-call | tf_op jit(solution)/shard_map/prefix_attention/pallas_call | solution.py:327
  22.4 13.0 %all_to_all.10.back_ref = bf16[288,2,128]{2,1,0:T(2,128)(2,1)S(1)} all-to-all(bf16[288,2,128]{2,1,0:T(2,128)(2,1)S(1)} %prefix_attention.1), channel_id=1, replica_groups=mesh['grp'=4,'seq'=8] {'grp','seq'}, dimensions={0} | all-to-all | bytes 294912 | tf_op jit(solution)/shard_map/all_to_all | solution.py:336
  35.4 1.4 %join.1 = bf16[4,8192]{1,0:T(4,128)(2,1)} custom-call(s32[4]{0:T(128)S(4)} %get-tuple-element.21.routes_ref, bf16[288,2,128]{2,1,0:T(2,128)(2,1)S(1)} %all_to_all.10.back_ref, f32[4,64,128]{2,1,0:T(8,128)S(1)} %get-tuple-element.35.suffix_ref, f32[4,64,128]{2,1,0:T(8,128)S(1)} %get-tuple-element.36.stat_ref), custom_call_target="tpu_custom_call" | custom-call | tf_op jit(solution)/shard_map/join/pallas_call | solution.py:338
Async XLA Ops:
  1.8 18.9 %all-to-all-start = ((bf16[32,16,128]{2,1,0:T(8,128)(2,1)}), bf16[32,16,128]{2,1,0:T(8,128)(2,1)S(1)}, u32[]{:S(2)}, u32[]{:S(2)}) async-start(bf16[32,16,128]{2,1,0:T(8,128)(2,1)} %bitcast.2), calls=%async_computation | async-start | bytes 262144 | tf_op jit(solution)/shard_map/all_to_all | solution.py:297
  9.2 6.0 %collective-permute-start = (bf16[2,128,128]{2,1,0:T(8,128)(2,1)S(1)}, bf16[2,128,128]{2,1,0:T(8,128)(2,1)S(1)}, u32[]{:S(2)}, u32[]{:S(2)}) collective-permute-start(bf16[2,128,128]{2,1,0:T(8,128)(2,1)S(1)} %get-tuple-element.28), channel_id=1, source_target_pairs={{0,7},{1,6},{2,5},{3,4},{4,3},{5,2},{6,1},{7,0},{8,15},{9,14},{10,... | collective-permute-start | bytes 196616 | tf_op jit(solution)/shard_map/ppermute | solution.py:295
  11.6 5.7 %collective-permute-start.1 = (bf16[2,128,128]{2,1,0:T(8,128)(2,1)S(1)}, bf16[2,128,128]{2,1,0:T(8,128)(2,1)S(1)}, u32[]{:S(2)}, u32[]{:S(2)}) collective-permute-start(bf16[2,128,128]{2,1,0:T(8,128)(2,1)S(1)} %get-tuple-element.29), channel_id=1, source_target_pairs={{0,6},{1,7},{2,4},{3,5},{4,2},{5,3},{6,0},{7,1},{8,14},{9,15},{10,... | collective-permute-start | bytes 196616 | tf_op jit(solution)/shard_map/ppermute | solution.py:295
  12.0 8.7 %collective-permute-start.2 = (bf16[2,128,128]{2,1,0:T(8,128)(2,1)S(1)}, bf16[2,128,128]{2,1,0:T(8,128)(2,1)S(1)}, u32[]{:S(2)}, u32[]{:S(2)}) collective-permute-start(bf16[2,128,128]{2,1,0:T(8,128)(2,1)S(1)} %get-tuple-element.30), channel_id=1, source_target_pairs={{0,5},{1,4},{2,7},{3,6},{4,1},{5,0},{6,3},{7,2},{8,13},{9,12},{10,... | collective-permute-start | bytes 196616 | tf_op jit(solution)/shard_map/ppermute | solution.py:295
  13.4 7.4 %collective-permute-start.3 = (bf16[2,128,128]{2,1,0:T(8,128)(2,1)S(1)}, bf16[2,128,128]{2,1,0:T(8,128)(2,1)S(1)}, u32[]{:S(2)}, u32[]{:S(2)}) collective-permute-start(bf16[2,128,128]{2,1,0:T(8,128)(2,1)S(1)} %get-tuple-element.31), channel_id=1, source_target_pairs={{0,4},{1,5},{2,6},{3,7},{4,0},{5,1},{6,2},{7,3},{8,12},{9,13},{10,... | collective-permute-start | bytes 196616 | tf_op jit(solution)/shard_map/ppermute | solution.py:295
  13.7 7.0 %collective-permute-start.4 = (bf16[2,128,128]{2,1,0:T(8,128)(2,1)S(1)}, bf16[2,128,128]{2,1,0:T(8,128)(2,1)S(1)}, u32[]{:S(2)}, u32[]{:S(2)}) collective-permute-start(bf16[2,128,128]{2,1,0:T(8,128)(2,1)S(1)} %get-tuple-element.32), channel_id=1, source_target_pairs={{0,3},{1,2},{2,1},{3,0},{4,7},{5,6},{6,5},{7,4},{8,11},{9,10},{10,... | collective-permute-start | bytes 196616 | tf_op jit(solution)/shard_map/ppermute | solution.py:295
  15.2 5.6 %collective-permute-start.5 = (bf16[2,128,128]{2,1,0:T(8,128)(2,1)S(1)}, bf16[2,128,128]{2,1,0:T(8,128)(2,1)S(1)}, u32[]{:S(2)}, u32[]{:S(2)}) collective-permute-start(bf16[2,128,128]{2,1,0:T(8,128)(2,1)S(1)} %get-tuple-element.33), channel_id=1, source_target_pairs={{0,2},{1,3},{2,0},{3,1},{4,6},{5,7},{6,4},{7,5},{8,10},{9,11},{10,... | collective-permute-start | bytes 196616 | tf_op jit(solution)/shard_map/ppermute | solution.py:295
  17.3 3.5 %collective-permute-start.6 = (bf16[2,128,128]{2,1,0:T(8,128)(2,1)S(1)}, bf16[2,128,128]{2,1,0:T(8,128)(2,1)S(1)}, u32[]{:S(2)}, u32[]{:S(2)}) collective-permute-start(bf16[2,128,128]{2,1,0:T(8,128)(2,1)S(1)} %get-tuple-element.34), channel_id=1, source_target_pairs={{0,1},{1,0},{2,3},{3,2},{4,5},{5,4},{6,7},{7,6},{8,9},{9,8},{10,11... | collective-permute-start | bytes 196616 | tf_op jit(solution)/shard_map/ppermute | solution.py:295

commit v4 on v3

--- a/solution.py
+++ b/solution.py
@@ -65,7 +65,7 @@
         for k in range(KVH):
             tile = placed[g * ROWS:(g + 1) * ROWS, k * HEAD:(k + 1) * HEAD]
             for t in range(splits):
-                out_ref[g, t, k] = tile
+                out_ref[(g * splits + t) * KVH + k] = tile
     mine = requests * PER
     row = lax.broadcasted_iota(jnp.int32, (mine, cols), 0)
     col = lax.broadcasted_iota(jnp.int32, (mine, cols), 1)
@@ -117,22 +117,24 @@
     ]
     for copy in small + cached[0] + cached[1]:
         copy.start()
-    zero = jnp.zeros((PER, HEAD), jnp.float32)
     lane = lax.broadcasted_iota(jnp.int32, (HEADS, HEAD), 1)
+    upper = lax.broadcasted_iota(jnp.int32, (2 * PER, HEAD), 0) < PER
+    wides = []
+    for r in range(requests):
+        q = rows_ref[r]
+        wides.append([])
+        for pair in range(KVH // 2):
+            two = q[2 * pair * PER:2 * (pair + 1) * PER]
+            wides[r].append(
+                jnp.concatenate(
+                    [jnp.where(upper, two, 0.0), jnp.where(upper, 0.0, two)], axis=1
+                ).astype(jnp.bfloat16)
+            )
     for copy in small:
         copy.wait()
     news, owns, raws = [], [], []
     for r in range(requests):
         q = rows_ref[r]
-        wide = jnp.concatenate(
-            [
-                jnp.concatenate(
-                    [q[k * PER:(k + 1) * PER] if j == k else zero for j in range(KVH)], axis=1
-                )
-                for k in range(KVH)
-            ],
-            axis=0,
-        ).astype(jnp.bfloat16)
         new = new_ref[r].astype(jnp.float32)
         news.append(new)
         owns.append(
@@ -148,8 +150,20 @@
                 axis=0,
             )
         )
+    for r in range(requests):
         cached[0][r].wait()
-        raw = lax.dot_general(wide, kv_ref[r, 0], NT, preferred_element_type=jnp.float32)
+        raw = jnp.concatenate(
+            [
+                lax.dot_general(
+                    wides[r][pair],
+                    kv_ref[r, 0, :, 2 * pair * HEAD:2 * (pair + 1) * HEAD],
+                    NT,
+                    preferred_element_type=jnp.float32,
+                )
+                for pair in range(KVH // 2)
+            ],
+            axis=0,
+        )
         live = lax.broadcasted_iota(jnp.int32, raw.shape, 1) < len_ref[r]
         raws.append(jnp.where(live, raw, -jnp.inf))
     weights, own_weights = [], []
@@ -163,11 +177,20 @@
         own_weights.append(own_weight.astype(jnp.bfloat16).astype(jnp.float32))
     for r in range(requests):
         cached[1][r].wait()
-        full = jnp.dot(weights[r], kv_ref[r, 1], preferred_element_type=jnp.float32)
-        for k in range(KVH):
-            rows = slice(k * PER, (k + 1) * PER)
-            cols = slice(k * HEAD, (k + 1) * HEAD)
-            out_ref[r, rows, :] = full[rows, cols] + own_weights[r][rows] * news[r][1:2, cols]
+        for pair in range(KVH // 2):
+            both = jnp.dot(
+                weights[r][2 * pair * PER:2 * (pair + 1) * PER],
+                kv_ref[r, 1, :, 2 * pair * HEAD:2 * (pair + 1) * HEAD],
+                preferred_element_type=jnp.float32,
+            )
+            for j in range(2):
+                k = 2 * pair + j
+                rows = slice(k * PER, (k + 1) * PER)
+                cols = slice(k * HEAD, (k + 1) * HEAD)
+                out_ref[r, rows, :] = (
+                    both[j * PER:(j + 1) * PER, j * HEAD:(j + 1) * HEAD]
+                    + own_weights[r][rows] * news[r][1:2, cols]
+                )
 
 
 def prefix_kernel(q_ref, *refs):
@@ -180,13 +203,18 @@
     diagonal = lax.broadcasted_iota(jnp.int32, shape, 0) == lax.broadcasted_iota(jnp.int32, shape, 1)
     low = lax.broadcasted_iota(jnp.int32, (1, HEAD), 1) < HALF
 
-    def block(i):
+    def score(i):
         q = q_ref[pl.ds(i * step, step)].reshape(shape)
-        raw = lax.dot_general(q, keys, NT, preferred_element_type=jnp.float32)
+        return lax.dot_general(q, keys, NT, preferred_element_type=jnp.float32)
+
+    def weigh(raw):
         top = jnp.max(raw, axis=1, keepdims=True)
         weight = jnp.exp2((raw - top) * (SCALE * LOG2E))
         total = jnp.sum(weight, axis=1, keepdims=True)
-        out = jnp.dot(weight.astype(jnp.bfloat16), values, preferred_element_type=jnp.float32)
+        return top, weight.astype(jnp.bfloat16), total
+
+    def store(i, top, weight, total):
+        out = jnp.dot(weight, values, preferred_element_type=jnp.float32)
         out = (out / total).astype(SEND)
         level = top * SCALE + jnp.log(total)
         level = jnp.sum(jnp.where(diagonal, level, 0.0), axis=0, keepdims=True)
@@ -204,11 +232,24 @@
             out_ref[pl.ds(at, PAIRS)] = out[s * ROWS:(s + 1) * ROWS].reshape(PAIRS, 2, HEAD)
             out_ref[at + PAIRS] = halves[s // (step // 2)]
 
-    if sources // step <= 4:
-        for i in range(sources // step):
-            block(i)
+    def several(start, count):
+        ahead, done = score(start), None
+        for i in range(count):
+            raw = ahead
+            if i + 1 < count:
+                ahead = score(start + i + 1)
+            ready = weigh(raw)
+            if done is not None:
+                store(start + i - 1, *done)
+            done = ready
+        store(start + count - 1, *done)
+
+    blocks = sources // step
+    count = 4 if blocks % 4 == 0 else 1
+    if blocks == count:
+        several(0, count)
     else:
-        lax.fori_loop(0, sources // step, lambda i, c: (block(i), c)[1], 0)
+        lax.fori_loop(0, blocks // count, lambda i, c: (several(i * count, count), c)[1], 0)
 
 
 def join_kernel(splits, routes_ref, back_ref, suffix_ref, stat_ref, out_ref):
@@ -276,7 +317,7 @@
     outgoing, rows, routes, *blocks = pl.pallas_call(
         functools.partial(prepare, groups, splits),
         out_shape=[
-            jax.ShapeDtypeStruct((groups, splits, KVH, ROWS, HEAD), jnp.bfloat16),
+            pltpu.VMEM((groups * seq, ROWS, HEAD), jnp.bfloat16),
             pltpu.VMEM((requests, HEADS, HEAD), jnp.float32),
             pltpu.SMEM((requests,), jnp.int32),
         ]
@@ -295,7 +336,7 @@
         parts.append(lax.ppermute(blocks[j], "seq", [(s, s ^ j) for s in range(seq)]))
 
     arrived = lax.all_to_all(
-        outgoing.reshape(groups * seq, ROWS, HEAD), everyone, split_axis=0, concat_axis=0, tiled=True
+        in_vmem(outgoing), everyone, split_axis=0, concat_axis=0, tiled=True
     )
 
     suffix_out, suffix_stat = pl.pallas_call(

time: 37 us -> 36.1 us (0.976)
  Pallas kernels: 8.21 us -> 7.22 us
    pallas_call x1, Pallas kernels: 1.61 us -> 1 us  [on_device(): pl.pallas_call(prefix_kernel, out_shape=pltpu.VMEM((groups * seq * BACK,...]
    pallas_call x1, Pallas kernels: 3.39 us -> 3.01 us  [on_device(): pl.pallas_call(suffix_kernel, out_shape=(pltpu.VMEM((requests, HEADS, HEA...]
  transfers between devices with their start and end apart: 8 -> 8, of which waited for: 1 -> 1; matrix products, arithmetic and copies ran while one was open for 0% -> 0% of each run, Pallas kernels for 9% -> 8%
where the time goes in v4:
time: 36.1 us; the launch traced here: 35.8 us
  starting transfers between devices  14.8 us (41%)
  blocking collectives  13.1 us (36%)
  Pallas kernels  7.22 us (20%)
  waiting for transfers between devices  0.72 us (2%)
    all_to_all x1, blocking collectives, on_device(): lax.all_to_all(back, everyone, split_axis=0, concat_axis=0, tiled=True)  13.1 us
    ppermute x7, starting transfers between devices, on_device(): lax.ppermute(blocks[j], 'seq', [(s, s ^ j) for s in range(seq)])  7.46 us
    all_to_all x1, starting transfers between devices, on_device(): lax.all_to_all(in_vmem(outgoing), everyone, split_axis=0, concat_axis=0,...  7.3 us
    pallas_call x1, Pallas kernels, on_device(): pl.pallas_call(suffix_kernel, out_shape=(pltpu.VMEM((requests, HEADS, HEA...  3.01 us
    pallas_call x1, Pallas kernels, on_device(): pl.pallas_call(functools.partial(prepare, groups, splits), out_shape=[plt...  1.84 us
    pallas_call x1, Pallas kernels, on_device(): pl.pallas_call(functools.partial(join_kernel, splits), out_shape=jax.Shap...  1.37 us
    pallas_call x1, Pallas kernels, on_device(): pl.pallas_call(prefix_kernel, out_shape=pltpu.VMEM((groups * seq * BACK,...  1 us
  transfers between devices with their start and end apart: 8, of which 1 were waited for; matrix products, arithmetic and copies ran while one was open for 0% of the time, Pallas kernels for 8%

profile of v4, /device:TPU:0, one launch (start us, length us, event | category | flops | bytes accessed | tf_op | source)
XLA Modules:
  0.0 35.8 jit_solution(13244907797346627192)
XLA Ops:
  0.0 1.8 %prepare.1 = (bf16[32,16,128]{2,1,0:T(8,128)(2,1)}, f32[4,64,128]{2,1,0:T(8,128)S(1)}, s32[4]{0:T(128)S(4)}, bf16[2,128,128]{2,1,0:T(8,128)(2,1)S(1)}, bf16[2,12...) custom-call(s32[4]{0:T(128)} %bitcast.1, ...), custom_call_target="tpu_custom_call" | custom-call | tf_op jit(solution)/shard_map/prepare/pallas_call | solution.py:317
  1.8 7.3 %all-to-all-start = ((bf16[32,16,128]{2,1,0:T(8,128)(2,1)}), bf16[32,16,128]{2,1,0:T(8,128)(2,1)S(1)}, u32[]{:S(2)}, u32[]{:S(2)}) async-start(bf16[32,16,128]{2,1,0:T(8,128)(2,1)} %get-tuple-element.22), calls=%async_computation | async-start | bytes 262144 | tf_op jit(solution)/shard_map/all_to_all | solution.py:338
  9.2 2.5 %collective-permute-start = (bf16[2,128,128]{2,1,0:T(8,128)(2,1)S(1)}, bf16[2,128,128]{2,1,0:T(8,128)(2,1)S(1)}, u32[]{:S(2)}, u32[]{:S(2)}) collective-permute-start(bf16[2,128,128]{2,1,0:T(8,128)(2,1)S(1)} %get-tuple-element.28), channel_id=1, source_target_pairs={{0,7},{1,6},{2,5},{3,4},{4,3},{5,2},{6,1},{7,0},{8,15},{9,14},{10,... | collective-permute-start | bytes 196616 | tf_op jit(solution)/shard_map/ppermute | solution.py:336
  11.6 0.4 %collective-permute-start.1 = (bf16[2,128,128]{2,1,0:T(8,128)(2,1)S(1)}, bf16[2,128,128]{2,1,0:T(8,128)(2,1)S(1)}, u32[]{:S(2)}, u32[]{:S(2)}) collective-permute-start(bf16[2,128,128]{2,1,0:T(8,128)(2,1)S(1)} %get-tuple-element.29), channel_id=1, source_target_pairs={{0,6},{1,7},{2,4},{3,5},{4,2},{5,3},{6,0},{7,1},{8,14},{9,15},{10,... | collective-permute-start | bytes 196616 | tf_op jit(solution)/shard_map/ppermute | solution.py:336
  12.0 1.4 %collective-permute-start.2 = (bf16[2,128,128]{2,1,0:T(8,128)(2,1)S(1)}, bf16[2,128,128]{2,1,0:T(8,128)(2,1)S(1)}, u32[]{:S(2)}, u32[]{:S(2)}) collective-permute-start(bf16[2,128,128]{2,1,0:T(8,128)(2,1)S(1)} %get-tuple-element.30), channel_id=1, source_target_pairs={{0,5},{1,4},{2,7},{3,6},{4,1},{5,0},{6,3},{7,2},{8,13},{9,12},{10,... | collective-permute-start | bytes 196616 | tf_op jit(solution)/shard_map/ppermute | solution.py:336
  13.4 0.4 %collective-permute-start.3 = (bf16[2,128,128]{2,1,0:T(8,128)(2,1)S(1)}, bf16[2,128,128]{2,1,0:T(8,128)(2,1)S(1)}, u32[]{:S(2)}, u32[]{:S(2)}) collective-permute-start(bf16[2,128,128]{2,1,0:T(8,128)(2,1)S(1)} %get-tuple-element.31), channel_id=1, source_target_pairs={{0,4},{1,5},{2,6},{3,7},{4,0},{5,1},{6,2},{7,3},{8,12},{9,13},{10,... | collective-permute-start | bytes 196616 | tf_op jit(solution)/shard_map/ppermute | solution.py:336
  13.7 1.4 %collective-permute-start.4 = (bf16[2,128,128]{2,1,0:T(8,128)(2,1)S(1)}, bf16[2,128,128]{2,1,0:T(8,128)(2,1)S(1)}, u32[]{:S(2)}, u32[]{:S(2)}) collective-permute-start(bf16[2,128,128]{2,1,0:T(8,128)(2,1)S(1)} %get-tuple-element.32), channel_id=1, source_target_pairs={{0,3},{1,2},{2,1},{3,0},{4,7},{5,6},{6,5},{7,4},{8,11},{9,10},{10,... | collective-permute-start | bytes 196616 | tf_op jit(solution)/shard_map/ppermute | solution.py:336
  15.2 0.0 collective-permute-done.refs_1_
  15.2 1.5 %collective-permute-start.5 = (bf16[2,128,128]{2,1,0:T(8,128)(2,1)S(1)}, bf16[2,128,128]{2,1,0:T(8,128)(2,1)S(1)}, u32[]{:S(2)}, u32[]{:S(2)}) collective-permute-start(bf16[2,128,128]{2,1,0:T(8,128)(2,1)S(1)} %get-tuple-element.33), channel_id=1, source_target_pairs={{0,2},{1,3},{2,0},{3,1},{4,6},{5,7},{6,4},{7,5},{8,10},{9,11},{10,... | collective-permute-start | bytes 196616 | tf_op jit(solution)/shard_map/ppermute | solution.py:336
  16.6 0.7 %collective-permute-done.1.refs_2_ = bf16[2,128,128]{2,1,0:T(8,128)(2,1)S(1)} collective-permute-done((bf16[2,128,128]{2,1,0:T(8,128)(2,1)S(1)}, bf16[2,128,128]{2,1,0:T(8,128)(2,1)S(1)}, u32[]{:S(2)}, u32[]{:S(2)}) %collective-permute-start.1) | collective-permute-done | bytes 65568 | tf_op jit(solution)/shard_map/ppermute | solution.py:336
  17.3 0.0 collective-permute-start.6
  17.3 3.0 %suffix_attention.1 = (f32[4,64,128]{2,1,0:T(8,128)S(1)}, f32[4,64,128]{2,1,0:T(8,128)S(1)}) custom-call(s32[4]{0:T(128)} %len_in.1, f32[4,64,128]{2,1,0:T(8,128)S(1)} %get-tuple-element.23.rows_ref, bf16[4,2,1024]{2,1,0:T(2,128)(2,1)} %new_in.1, bf16[4,2,128,1024]{3,2,1,0:T(8,128)(2,1)} %kv_in.1), custom_call_target="tpu_custom_call" | custom-call | flops 134217728 | bytes 2097152 | tf_op jit(solution)/shard_map/suffix_attention/pallas_call | solution.py:342
  20.3 0.0 all-to-all-done.q_ref
  20.4 0.0 collective-permute-done.2.refs_3_
  20.4 0.0 collective-permute-done.3.refs_4_
  20.4 0.0 collective-permute-done.4.refs_5_
  20.4 0.0 collective-permute-done.5.refs_6_
  20.4 0.0 collective-permute-done.6.refs_7_
  20.4 1.0 %prefix_attention.1 = bf16[288,2,128]{2,1,0:T(2,128)(2,1)S(1)} custom-call(bf16[32,16,128]{2,1,0:T(8,128)(2,1)S(1)} %all-to-all-done.q_ref, bf16[2,128,128]{2,1,0:T(8,128)(2,1)S(1)} %get-tuple-element.27.refs_0_, bf16[2,128,128]{2,1,0:T(8,128)(2,1)S(1)} %collective-permute-done.refs_1_, bf16[2,128,128]{2,1,0:T(8,128)(2,1)S(1)} %collective-permute-done.1.refs_2_, ...), custom_call_target="tpu_custom_call" | custom-call | tf_op jit(solution)/shard_map/prefix_attention/pallas_call | solution.py:368
  21.4 13.1 %all_to_all.10.back_ref = bf16[288,2,128]{2,1,0:T(2,128)(2,1)S(1)} all-to-all(bf16[288,2,128]{2,1,0:T(2,128)(2,1)S(1)} %prefix_attention.1), channel_id=1, replica_groups=mesh['grp'=4,'seq'=8] {'grp','seq'}, dimensions={0} | all-to-all | bytes 294912 | tf_op jit(solution)/shard_map/all_to_all | solution.py:377
  34.5 1.4 %join.1 = bf16[4,8192]{1,0:T(4,128)(2,1)} custom-call(s32[4]{0:T(128)S(4)} %get-tuple-element.21.routes_ref, bf16[288,2,128]{2,1,0:T(2,128)(2,1)S(1)} %all_to_all.10.back_ref, f32[4,64,128]{2,1,0:T(8,128)S(1)} %get-tuple-element.35.suffix_ref, f32[4,64,128]{2,1,0:T(8,128)S(1)} %get-tuple-element.36.stat_ref), custom_call_target="tpu_custom_call" | custom-call | tf_op jit(solution)/shard_map/join/pallas_call | solution.py:379
Async XLA Ops:
  1.8 18.5 %all-to-all-start = ((bf16[32,16,128]{2,1,0:T(8,128)(2,1)}), bf16[32,16,128]{2,1,0:T(8,128)(2,1)S(1)}, u32[]{:S(2)}, u32[]{:S(2)}) async-start(bf16[32,16,128]{2,1,0:T(8,128)(2,1)} %get-tuple-element.22), calls=%async_computation | async-start | bytes 262144 | tf_op jit(solution)/shard_map/all_to_all | solution.py:338
  9.2 6.0 %collective-permute-start = (bf16[2,128,128]{2,1,0:T(8,128)(2,1)S(1)}, bf16[2,128,128]{2,1,0:T(8,128)(2,1)S(1)}, u32[]{:S(2)}, u32[]{:S(2)}) collective-permute-start(bf16[2,128,128]{2,1,0:T(8,128)(2,1)S(1)} %get-tuple-element.28), channel_id=1, source_target_pairs={{0,7},{1,6},{2,5},{3,4},{4,3},{5,2},{6,1},{7,0},{8,15},{9,14},{10,... | collective-permute-start | bytes 196616 | tf_op jit(solution)/shard_map/ppermute | solution.py:336
  11.6 5.7 %collective-permute-start.1 = (bf16[2,128,128]{2,1,0:T(8,128)(2,1)S(1)}, bf16[2,128,128]{2,1,0:T(8,128)(2,1)S(1)}, u32[]{:S(2)}, u32[]{:S(2)}) collective-permute-start(bf16[2,128,128]{2,1,0:T(8,128)(2,1)S(1)} %get-tuple-element.29), channel_id=1, source_target_pairs={{0,6},{1,7},{2,4},{3,5},{4,2},{5,3},{6,0},{7,1},{8,14},{9,15},{10,... | collective-permute-start | bytes 196616 | tf_op jit(solution)/shard_map/ppermute | solution.py:336
  12.0 8.4 %collective-permute-start.2 = (bf16[2,128,128]{2,1,0:T(8,128)(2,1)S(1)}, bf16[2,128,128]{2,1,0:T(8,128)(2,1)S(1)}, u32[]{:S(2)}, u32[]{:S(2)}) collective-permute-start(bf16[2,128,128]{2,1,0:T(8,128)(2,1)S(1)} %get-tuple-element.30), channel_id=1, source_target_pairs={{0,5},{1,4},{2,7},{3,6},{4,1},{5,0},{6,3},{7,2},{8,13},{9,12},{10,... | collective-permute-start | bytes 196616 | tf_op jit(solution)/shard_map/ppermute | solution.py:336
  13.4 7.0 %collective-permute-start.3 = (bf16[2,128,128]{2,1,0:T(8,128)(2,1)S(1)}, bf16[2,128,128]{2,1,0:T(8,128)(2,1)S(1)}, u32[]{:S(2)}, u32[]{:S(2)}) collective-permute-start(bf16[2,128,128]{2,1,0:T(8,128)(2,1)S(1)} %get-tuple-element.31), channel_id=1, source_target_pairs={{0,4},{1,5},{2,6},{3,7},{4,0},{5,1},{6,2},{7,3},{8,12},{9,13},{10,... | collective-permute-start | bytes 196616 | tf_op jit(solution)/shard_map/ppermute | solution.py:336
  13.7 6.7 %collective-permute-start.4 = (bf16[2,128,128]{2,1,0:T(8,128)(2,1)S(1)}, bf16[2,128,128]{2,1,0:T(8,128)(2,1)S(1)}, u32[]{:S(2)}, u32[]{:S(2)}) collective-permute-start(bf16[2,128,128]{2,1,0:T(8,128)(2,1)S(1)} %get-tuple-element.32), channel_id=1, source_target_pairs={{0,3},{1,2},{2,1},{3,0},{4,7},{5,6},{6,5},{7,4},{8,11},{9,10},{10,... | collective-permute-start | bytes 196616 | tf_op jit(solution)/shard_map/ppermute | solution.py:336
  15.2 5.2 %collective-permute-start.5 = (bf16[2,128,128]{2,1,0:T(8,128)(2,1)S(1)}, bf16[2,128,128]{2,1,0:T(8,128)(2,1)S(1)}, u32[]{:S(2)}, u32[]{:S(2)}) collective-permute-start(bf16[2,128,128]{2,1,0:T(8,128)(2,1)S(1)} %get-tuple-element.33), channel_id=1, source_target_pairs={{0,2},{1,3},{2,0},{3,1},{4,6},{5,7},{6,4},{7,5},{8,10},{9,11},{10,... | collective-permute-start | bytes 196616 | tf_op jit(solution)/shard_map/ppermute | solution.py:336
  17.3 3.1 %collective-permute-start.6 = (bf16[2,128,128]{2,1,0:T(8,128)(2,1)S(1)}, bf16[2,128,128]{2,1,0:T(8,128)(2,1)S(1)}, u32[]{:S(2)}, u32[]{:S(2)}) collective-permute-start(bf16[2,128,128]{2,1,0:T(8,128)(2,1)S(1)} %get-tuple-element.34), channel_id=1, source_target_pairs={{0,1},{1,0},{2,3},{3,2},{4,5},{5,4},{6,7},{7,6},{8,9},{9,8},{10,11... | collective-permute-start | bytes 196616 | tf_op jit(solution)/shard_map/ppermute | solution.py:336

commit v5 on v4

--- a/solution.py
+++ b/solution.py
@@ -81,7 +81,7 @@
 
 
 def prepare(groups, splits, routes_in, q_in, kv_ref, out_ref, rows_ref, routes_ref, *refs):
-    blocks, (q_ref, x_ref, sems) = refs[:KVH], refs[KVH:]
+    blocks, (q_ref, x_ref, sems) = refs[:5], refs[5:]
     mine = lax.axis_index("seq") % KVH
     first = [
         pltpu.make_async_copy(routes_in, routes_ref, sems.at[KVH]),
@@ -91,7 +91,11 @@
     for j in range(KVH):
         start = pl.multiple_of(jnp.bitwise_xor(mine, j) * HEAD, HEAD)
         later.append(
-            pltpu.make_async_copy(kv_ref.at[0, :, :, pl.ds(start, HEAD)], blocks[j], sems.at[j])
+            pltpu.make_async_copy(
+                kv_ref.at[0, :, :, pl.ds(start, HEAD)],
+                blocks[j] if j < 2 else blocks[1 + j // 2].at[j % 2],
+                sems.at[j],
+            )
         )
     for copy in first + later:
         copy.start()
@@ -195,8 +199,10 @@
 
 def prefix_kernel(q_ref, *refs):
     parts, out_ref = refs[:-1], refs[-1]
-    keys = jnp.concatenate([part[0] for part in parts], axis=0)
-    values = jnp.concatenate([part[1] for part in parts], axis=0)
+    views = [part for part in parts[:2]]
+    views += [part.at[0] for part in parts[2:5]] + [part.at[1] for part in parts[5:]]
+    keys = jnp.concatenate([view[0] for view in views], axis=0)
+    values = jnp.concatenate([view[1] for view in views], axis=0)
     sources = q_ref.shape[0]
     step = HEAD // ROWS
     shape = (step * ROWS, HEAD)
@@ -321,9 +327,10 @@
             pltpu.VMEM((requests, HEADS, HEAD), jnp.float32),
             pltpu.SMEM((requests,), jnp.int32),
         ]
-        + [pltpu.VMEM((2, here, HEAD), jnp.bfloat16)] * KVH,
+        + [pltpu.VMEM((2, here, HEAD), jnp.bfloat16)] * 2
+        + [pltpu.VMEM((2, 2, here, HEAD), jnp.bfloat16)] * 3,
         in_specs=[ANY, ANY, ANY],
-        out_specs=[VMEM, VMEM, SMEM] + [VMEM] * KVH,
+        out_specs=[VMEM, VMEM, SMEM] + [VMEM] * 5,
         scratch_shapes=[
             pltpu.VMEM((requests, HEADS * HEAD), jnp.bfloat16),
             pltpu.VMEM((PER * requests, KVH * HEAD), jnp.float32),
@@ -331,9 +338,12 @@
         ],
         name="prepare",
     )(routes, queries, prefix_kv)
-    parts = [blocks[0]]
-    for j in reversed(range(1, KVH)):
-        parts.append(lax.ppermute(blocks[j], "seq", [(s, s ^ j) for s in range(seq)]))
+    def swap(block, j):
+        return lax.ppermute(block, "seq", [(s, s ^ j) for s in range(seq)])
+
+    parts = [blocks[0], swap(blocks[1], 1)]
+    pairs = [swap(blocks[1 + j // 2], j) for j in (6, 4, 2)]
+    parts += pairs + [swap(pair, 1) for pair in pairs]
 
     arrived = lax.all_to_all(
         in_vmem(outgoing), everyone, split_axis=0, concat_axis=0, tiled=True

time: 36.1 us -> 33.8 us (0.936)
  waiting for transfers between devices: 0.72 us -> 4.12 us
  blocking collectives: 13.1 us -> 10.2 us
  starting transfers between devices: 14.8 us -> 11.9 us
    all_to_all x1, waiting for transfers between devices: 0.01 us -> 4.1 us  [on_device(): lax.all_to_all(in_vmem(outgoing), everyone, split_axis=0, concat_axis=0,...]
    all_to_all x1, blocking collectives: 13.1 us -> 10.2 us  [on_device(): lax.all_to_all(back, everyone, split_axis=0, concat_axis=0, tiled=True)]
    ppermute x7, starting transfers between devices: 7.46 us -> 5.69 us  [swap(): return lax.ppermute(block, 'seq', [(s, s ^ j) for s in range(seq)])]
    all_to_all x1, starting transfers between devices: 7.3 us -> 6.25 us  [on_device(): lax.all_to_all(in_vmem(outgoing), everyone, split_axis=0, concat_axis=0,...]
    ppermute x7, waiting for transfers between devices: 0.72 us -> 0.02 us  [swap(): return lax.ppermute(block, 'seq', [(s, s ^ j) for s in range(seq)])]
  transfers between devices with their start and end apart: 8 -> 8, of which waited for: 1 -> 1; matrix products, arithmetic and copies ran while one was open for 0% -> 0% of each run, Pallas kernels for 8% -> 9%
where the time goes in v5:
time: 33.8 us; the launch traced here: 33.5 us
  starting transfers between devices  11.9 us (35%)
  blocking collectives  10.2 us (30%)
  Pallas kernels  7.22 us (21%)
  waiting for transfers between devices  4.12 us (12%)
    all_to_all x1, blocking collectives, on_device(): lax.all_to_all(back, everyone, split_axis=0, concat_axis=0, tiled=True)  10.2 us
    all_to_all x1, starting transfers between devices, on_device(): lax.all_to_all(in_vmem(outgoing), everyone, split_axis=0, concat_axis=0,...  6.25 us
    ppermute x7, starting transfers between devices, swap(): return lax.ppermute(block, 'seq', [(s, s ^ j) for s in range(seq)])  5.69 us
    all_to_all x1, waiting for transfers between devices, on_device(): lax.all_to_all(in_vmem(outgoing), everyone, split_axis=0, concat_axis=0,...  4.1 us
    pallas_call x1, Pallas kernels, on_device(): pl.pallas_call(suffix_kernel, out_shape=(pltpu.VMEM((requests, HEADS, HEA...  3.01 us
    pallas_call x1, Pallas kernels, on_device(): pl.pallas_call(functools.partial(prepare, groups, splits), out_shape=[plt...  1.84 us
    pallas_call x1, Pallas kernels, on_device(): pl.pallas_call(functools.partial(join_kernel, splits), out_shape=jax.Shap...  1.37 us
    pallas_call x1, Pallas kernels, on_device(): pl.pallas_call(prefix_kernel, out_shape=pltpu.VMEM((groups * seq * BACK,...  1 us
  transfers between devices with their start and end apart: 8, of which 1 were waited for; matrix products, arithmetic and copies ran while one was open for 0% of the time, Pallas kernels for 9%

profile of v5, /device:TPU:0, one launch (start us, length us, event | category | flops | bytes accessed | tf_op | source)
XLA Modules:
  0.0 33.5 jit_solution(16374578376938753980)
XLA Ops:
  0.0 1.8 %prepare.1 = (bf16[32,16,128]{2,1,0:T(8,128)(2,1)}, f32[4,64,128]{2,1,0:T(8,128)S(1)}, s32[4]{0:T(128)S(4)}, bf16[2,128,128]{2,1,0:T(8,128)(2,1)S(1)}, bf16[2,12...) custom-call(s32[4]{0:T(128)} %bitcast.1, ...), custom_call_target="tpu_custom_call" | custom-call | tf_op jit(solution)/shard_map/prepare/pallas_call | solution.py:323
  1.8 4.0 %collective-permute-start.1 = (bf16[2,2,128,128]{3,2,1,0:T(8,128)(2,1)S(1)}, bf16[2,2,128,128]{3,2,1,0:T(8,128)(2,1)S(1)}, u32[]{:S(2)}, u32[]{:S(2)}) collective-permute-start(bf16[2,2,128,128]{3,2,1,0:T(8,128)(2,1)S(1)} %get-tuple-element.26), channel_id=1, source_target_pairs={{0,6},{1,7},{2,4},{3,5},{4,2},{5,3},{6,0},{7,1},{8,14},{9,15},{10,... | collective-permute-start | bytes 393224 | tf_op jit(solution)/shard_map/ppermute | solution.py:342
  5.8 0.5 %collective-permute-start.2 = (bf16[2,2,128,128]{3,2,1,0:T(8,128)(2,1)S(1)}, bf16[2,2,128,128]{3,2,1,0:T(8,128)(2,1)S(1)}, u32[]{:S(2)}, u32[]{:S(2)}) collective-permute-start(bf16[2,2,128,128]{3,2,1,0:T(8,128)(2,1)S(1)} %get-tuple-element.27), channel_id=1, source_target_pairs={{0,4},{1,5},{2,6},{3,7},{4,0},{5,1},{6,2},{7,3},{8,12},{9,13},{10,... | collective-permute-start | bytes 393224 | tf_op jit(solution)/shard_map/ppermute | solution.py:342
  6.3 0.1 collective-permute-start.3
  6.4 6.2 %all-to-all-start = ((bf16[32,16,128]{2,1,0:T(8,128)(2,1)}), bf16[32,16,128]{2,1,0:T(8,128)(2,1)S(1)}, u32[]{:S(2)}, u32[]{:S(2)}) async-start(bf16[32,16,128]{2,1,0:T(8,128)(2,1)} %get-tuple-element.19), calls=%async_computation | async-start | bytes 262144 | tf_op jit(solution)/shard_map/all_to_all | solution.py:348
  12.7 0.0 collective-permute-done.1.refs_2_
  12.7 0.3 collective-permute-start.4
  13.0 0.0 collective-permute-done.2.refs_3_
  13.0 0.3 collective-permute-start.5
  13.3 0.0 collective-permute-done.3.refs_4_
  13.3 0.3 collective-permute-start.6
  13.6 0.3 collective-permute-start
  13.8 3.0 %suffix_attention.1 = (f32[4,64,128]{2,1,0:T(8,128)S(1)}, f32[4,64,128]{2,1,0:T(8,128)S(1)}) custom-call(s32[4]{0:T(128)} %len_in.1, f32[4,64,128]{2,1,0:T(8,128)S(1)} %get-tuple-element.20.rows_ref, bf16[4,2,1024]{2,1,0:T(2,128)(2,1)} %new_in.1, bf16[4,2,128,1024]{3,2,1,0:T(8,128)(2,1)} %kv_in.1), custom_call_target="tpu_custom_call" | custom-call | flops 134217728 | bytes 2097152 | tf_op jit(solution)/shard_map/suffix_attention/pallas_call | solution.py:352
  16.8 4.1 %all-to-all-done.q_ref = bf16[32,16,128]{2,1,0:T(8,128)(2,1)S(1)} async-done(((bf16[32,16,128]{2,1,0:T(8,128)(2,1)}), bf16[32,16,128]{2,1,0:T(8,128)(2,1)S(1)}, u32[]{:S(2)}, u32[]{:S(2)}) %all-to-all-start) | async-done | bytes 131104 | tf_op jit(solution)/shard_map/all_to_all | solution.py:348
  20.9 0.0 collective-permute-done.refs_1_
  20.9 0.0 collective-permute-done.4.refs_5_
  20.9 0.0 collective-permute-done.5.refs_6_
  20.9 0.0 collective-permute-done.6.refs_7_
  21.0 1.0 %prefix_attention.1 = bf16[288,2,128]{2,1,0:T(2,128)(2,1)S(1)} custom-call(bf16[32,16,128]{2,1,0:T(8,128)(2,1)S(1)} %all-to-all-done.q_ref, bf16[2,128,128]{2,1,0:T(8,128)(2,1)S(1)} %get-tuple-element.24.refs_0_, bf16[2,128,128]{2,1,0:T(8,128)(2,1)S(1)} %collective-permute-done.refs_1_, bf16[2,2,128,128]{3,2,1,0:T(8,128)(2,1)S(1)} %collective-permute-done.1.refs_2_, ...), custom_call_target="tpu_custom_call" | custom-call | tf_op jit(solution)/shard_map/prefix_attention/pallas_call | solution.py:378
  22.0 10.2 %all_to_all.10.back_ref = bf16[288,2,128]{2,1,0:T(2,128)(2,1)S(1)} all-to-all(bf16[288,2,128]{2,1,0:T(2,128)(2,1)S(1)} %prefix_attention.1), channel_id=1, replica_groups=mesh['grp'=4,'seq'=8] {'grp','seq'}, dimensions={0} | all-to-all | bytes 294912 | tf_op jit(solution)/shard_map/all_to_all | solution.py:387
  32.1 1.4 %join.1 = bf16[4,8192]{1,0:T(4,128)(2,1)} custom-call(s32[4]{0:T(128)S(4)} %get-tuple-element.18.routes_ref, bf16[288,2,128]{2,1,0:T(2,128)(2,1)S(1)} %all_to_all.10.back_ref, f32[4,64,128]{2,1,0:T(8,128)S(1)} %get-tuple-element.29.suffix_ref, f32[4,64,128]{2,1,0:T(8,128)S(1)} %get-tuple-element.30.stat_ref), custom_call_target="tpu_custom_call" | custom-call | tf_op jit(solution)/shard_map/join/pallas_call | solution.py:389
Async XLA Ops:
  1.8 10.9 %collective-permute-start.1 = (bf16[2,2,128,128]{3,2,1,0:T(8,128)(2,1)S(1)}, bf16[2,2,128,128]{3,2,1,0:T(8,128)(2,1)S(1)}, u32[]{:S(2)}, u32[]{:S(2)}) collective-permute-start(bf16[2,2,128,128]{3,2,1,0:T(8,128)(2,1)S(1)} %get-tuple-element.26), channel_id=1, source_target_pairs={{0,6},{1,7},{2,4},{3,5},{4,2},{5,3},{6,0},{7,1},{8,14},{9,15},{10,... | collective-permute-start | bytes 393224 | tf_op jit(solution)/shard_map/ppermute | solution.py:342
  5.8 7.2 %collective-permute-start.2 = (bf16[2,2,128,128]{3,2,1,0:T(8,128)(2,1)S(1)}, bf16[2,2,128,128]{3,2,1,0:T(8,128)(2,1)S(1)}, u32[]{:S(2)}, u32[]{:S(2)}) collective-permute-start(bf16[2,2,128,128]{3,2,1,0:T(8,128)(2,1)S(1)} %get-tuple-element.27), channel_id=1, source_target_pairs={{0,4},{1,5},{2,6},{3,7},{4,0},{5,1},{6,2},{7,3},{8,12},{9,13},{10,... | collective-permute-start | bytes 393224 | tf_op jit(solution)/shard_map/ppermute | solution.py:342
  6.3 7.0 %collective-permute-start.3 = (bf16[2,2,128,128]{3,2,1,0:T(8,128)(2,1)S(1)}, bf16[2,2,128,128]{3,2,1,0:T(8,128)(2,1)S(1)}, u32[]{:S(2)}, u32[]{:S(2)}) collective-permute-start(bf16[2,2,128,128]{3,2,1,0:T(8,128)(2,1)S(1)} %get-tuple-element.28), channel_id=1, source_target_pairs={{0,2},{1,3},{2,0},{3,1},{4,6},{5,7},{6,4},{7,5},{8,10},{9,11},{10,... | collective-permute-start | bytes 393224 | tf_op jit(solution)/shard_map/ppermute | solution.py:342
  6.4 14.5 %all-to-all-start = ((bf16[32,16,128]{2,1,0:T(8,128)(2,1)}), bf16[32,16,128]{2,1,0:T(8,128)(2,1)S(1)}, u32[]{:S(2)}, u32[]{:S(2)}) async-start(bf16[32,16,128]{2,1,0:T(8,128)(2,1)} %get-tuple-element.19), calls=%async_computation | async-start | bytes 262144 | tf_op jit(solution)/shard_map/all_to_all | solution.py:348
  12.7 8.2 %collective-permute-start.4 = (bf16[2,2,128,128]{3,2,1,0:T(8,128)(2,1)S(1)}, bf16[2,2,128,128]{3,2,1,0:T(8,128)(2,1)S(1)}, u32[]{:S(2)}, u32[]{:S(2)}) collective-permute-start(bf16[2,2,128,128]{3,2,1,0:T(8,128)(2,1)S(1)} %collective-permute-done.1.refs_2_), channel_id=1, source_target_pairs={{0,1},{1,0},{2,3},{3,2},{4,5},{5,4},{6,7},{7,6},{8,9},{9,8},{10,11... | collective-permute-start | bytes 393224 | tf_op jit(solution)/shard_map/ppermute | solution.py:342
  13.0 7.9 %collective-permute-start.5 = (bf16[2,2,128,128]{3,2,1,0:T(8,128)(2,1)S(1)}, bf16[2,2,128,128]{3,2,1,0:T(8,128)(2,1)S(1)}, u32[]{:S(2)}, u32[]{:S(2)}) collective-permute-start(bf16[2,2,128,128]{3,2,1,0:T(8,128)(2,1)S(1)} %collective-permute-done.2.refs_3_), channel_id=1, source_target_pairs={{0,1},{1,0},{2,3},{3,2},{4,5},{5,4},{6,7},{7,6},{8,9},{9,8},{10,11... | collective-permute-start | bytes 393224 | tf_op jit(solution)/shard_map/ppermute | solution.py:342
  13.3 7.7 %collective-permute-start.6 = (bf16[2,2,128,128]{3,2,1,0:T(8,128)(2,1)S(1)}, bf16[2,2,128,128]{3,2,1,0:T(8,128)(2,1)S(1)}, u32[]{:S(2)}, u32[]{:S(2)}) collective-permute-start(bf16[2,2,128,128]{3,2,1,0:T(8,128)(2,1)S(1)} %collective-permute-done.3.refs_4_), channel_id=1, source_target_pairs={{0,1},{1,0},{2,3},{3,2},{4,5},{5,4},{6,7},{7,6},{8,9},{9,8},{10,11... | collective-permute-start | bytes 393224 | tf_op jit(solution)/shard_map/ppermute | solution.py:342
  13.6 7.4 %collective-permute-start = (bf16[2,128,128]{2,1,0:T(8,128)(2,1)S(1)}, bf16[2,128,128]{2,1,0:T(8,128)(2,1)S(1)}, u32[]{:S(2)}, u32[]{:S(2)}) collective-permute-start(bf16[2,128,128]{2,1,0:T(8,128)(2,1)S(1)} %get-tuple-element.25), channel_id=1, source_target_pairs={{0,1},{1,0},{2,3},{3,2},{4,5},{5,4},{6,7},{7,6},{8,9},{9,8},{10,11... | collective-permute-start | bytes 196616 | tf_op jit(solution)/shard_map/ppermute | solution.py:342

commit v6 on v5

--- a/solution.py
+++ b/solution.py
@@ -40,7 +40,7 @@
     return routes, ranks
 
 
-def pack_queries(groups, splits, routes_ref, q_ref, out_ref, rows_ref, x_ref):
+def pack_queries(groups, splits, routes_ref, q_ref, out_ref, rows_ref, x_ref, sending):
     requests = q_ref.shape[0]
     routes, ranks = slots_of(routes_ref, requests)
     q = q_ref[...].astype(jnp.float32)
@@ -66,6 +66,7 @@
             tile = placed[g * ROWS:(g + 1) * ROWS, k * HEAD:(k + 1) * HEAD]
             for t in range(splits):
                 out_ref[(g * splits + t) * KVH + k] = tile
+    sending.start()
     mine = requests * PER
     row = lax.broadcasted_iota(jnp.int32, (mine, cols), 0)
     col = lax.broadcasted_iota(jnp.int32, (mine, cols), 1)
@@ -80,8 +81,8 @@
             ]
 
 
-def prepare(groups, splits, routes_in, q_in, kv_ref, out_ref, rows_ref, routes_ref, *refs):
-    blocks, (q_ref, x_ref, sems) = refs[:5], refs[5:]
+def prepare(groups, splits, routes_in, q_in, kv_ref, out_hbm, rows_ref, routes_ref, *refs):
+    blocks, (q_ref, x_ref, out_ref, sems) = refs[:5], refs[5:]
     mine = lax.axis_index("seq") % KVH
     first = [
         pltpu.make_async_copy(routes_in, routes_ref, sems.at[KVH]),
@@ -101,9 +102,11 @@
         copy.start()
     for copy in first:
         copy.wait()
-    pack_queries(groups, splits, routes_ref, q_ref, out_ref, rows_ref, x_ref)
+    sending = pltpu.make_async_copy(out_ref, out_hbm, sems.at[KVH + 2])
+    pack_queries(groups, splits, routes_ref, q_ref, out_ref, rows_ref, x_ref, sending)
     for copy in later:
         copy.wait()
+    sending.wait()
 
 
 def suffix_kernel(len_in, rows_ref, new_in, kv_in, out_ref, stat_ref, len_ref, new_ref, kv_ref, sems):
@@ -323,18 +326,19 @@
     outgoing, rows, routes, *blocks = pl.pallas_call(
         functools.partial(prepare, groups, splits),
         out_shape=[
-            pltpu.VMEM((groups * seq, ROWS, HEAD), jnp.bfloat16),
+            jax.ShapeDtypeStruct((groups * seq, ROWS, HEAD), jnp.bfloat16),
             pltpu.VMEM((requests, HEADS, HEAD), jnp.float32),
             pltpu.SMEM((requests,), jnp.int32),
         ]
         + [pltpu.VMEM((2, here, HEAD), jnp.bfloat16)] * 2
         + [pltpu.VMEM((2, 2, here, HEAD), jnp.bfloat16)] * 3,
         in_specs=[ANY, ANY, ANY],
-        out_specs=[VMEM, VMEM, SMEM] + [VMEM] * 5,
+        out_specs=[ANY, VMEM, SMEM] + [VMEM] * 5,
         scratch_shapes=[
             pltpu.VMEM((requests, HEADS * HEAD), jnp.bfloat16),
             pltpu.VMEM((PER * requests, KVH * HEAD), jnp.float32),
-            pltpu.SemaphoreType.DMA((KVH + 2,)),
+            pltpu.VMEM((groups * seq, ROWS, HEAD), jnp.bfloat16),
+            pltpu.SemaphoreType.DMA((KVH + 3,)),
         ],
         name="prepare",
     )(routes, queries, prefix_kv)
@@ -346,7 +350,7 @@
     parts += pairs + [swap(pair, 1) for pair in pairs]
 
     arrived = lax.all_to_all(
-        in_vmem(outgoing), everyone, split_axis=0, concat_axis=0, tiled=True
+        outgoing, everyone, split_axis=0, concat_axis=0, tiled=True
     )
 
     suffix_out, suffix_stat = pl.pallas_call(

time: 33.8 us -> 33.7 us (level)
  no operation moved by 1% of the time
where the time goes in v6:
time: 33.7 us; the launch traced here: 33.4 us
  starting transfers between devices  11.9 us (35%)
  blocking collectives  10.2 us (30%)
  Pallas kernels  7.13 us (21%)
  waiting for transfers between devices  4.12 us (12%)
    all_to_all x1, blocking collectives, on_device(): lax.all_to_all(back, everyone, split_axis=0, concat_axis=0, tiled=True)  10.2 us
    all_to_all x1, starting transfers between devices, on_device(): lax.all_to_all(outgoing, everyone, split_axis=0, concat_axis=0, tiled=True)  6.25 us
    ppermute x7, starting transfers between devices, swap(): return lax.ppermute(block, 'seq', [(s, s ^ j) for s in range(seq)])  5.68 us
    all_to_all x1, waiting for transfers between devices, on_device(): lax.all_to_all(outgoing, everyone, split_axis=0, concat_axis=0, tiled=True)  4.1 us
    pallas_call x1, Pallas kernels, on_device(): pl.pallas_call(suffix_kernel, out_shape=(pltpu.VMEM((requests, HEADS, HEA...  3.01 us
    pallas_call x1, Pallas kernels, on_device(): pl.pallas_call(functools.partial(prepare, groups, splits), out_shape=[jax...  1.75 us
    pallas_call x1, Pallas kernels, on_device(): pl.pallas_call(functools.partial(join_kernel, splits), out_shape=jax.Shap...  1.37 us
    pallas_call x1, Pallas kernels, on_device(): pl.pallas_call(prefix_kernel, out_shape=pltpu.VMEM((groups * seq * BACK,...  1 us
  transfers between devices with their start and end apart: 8, of which 1 were waited for; matrix products, arithmetic and copies ran while one was open for 0% of the time, Pallas kernels for 9%

profile of v6, /device:TPU:0, one launch (start us, length us, event | category | flops | bytes accessed | tf_op | source)
XLA Modules:
  0.0 33.4 jit_solution(10251105697163832616)
XLA Ops:
  0.0 1.8 %prepare.1 = (bf16[32,16,128]{2,1,0:T(8,128)(2,1)}, f32[4,64,128]{2,1,0:T(8,128)S(1)}, s32[4]{0:T(128)S(4)}, bf16[2,128,128]{2,1,0:T(8,128)(2,1)S(1)}, bf16[2,12...) custom-call(s32[4]{0:T(128)} %bitcast.1, ...), custom_call_target="tpu_custom_call" | custom-call | tf_op jit(solution)/shard_map/prepare/pallas_call | solution.py:326
  1.8 4.0 %collective-permute-start.1 = (bf16[2,2,128,128]{3,2,1,0:T(8,128)(2,1)S(1)}, bf16[2,2,128,128]{3,2,1,0:T(8,128)(2,1)S(1)}, u32[]{:S(2)}, u32[]{:S(2)}) collective-permute-start(bf16[2,2,128,128]{3,2,1,0:T(8,128)(2,1)S(1)} %get-tuple-element.26), channel_id=1, source_target_pairs={{0,6},{1,7},{2,4},{3,5},{4,2},{5,3},{6,0},{7,1},{8,14},{9,15},{10,... | collective-permute-start | bytes 393224 | tf_op jit(solution)/shard_map/ppermute | solution.py:346
  5.7 0.5 %collective-permute-start.2 = (bf16[2,2,128,128]{3,2,1,0:T(8,128)(2,1)S(1)}, bf16[2,2,128,128]{3,2,1,0:T(8,128)(2,1)S(1)}, u32[]{:S(2)}, u32[]{:S(2)}) collective-permute-start(bf16[2,2,128,128]{3,2,1,0:T(8,128)(2,1)S(1)} %get-tuple-element.27), channel_id=1, source_target_pairs={{0,4},{1,5},{2,6},{3,7},{4,0},{5,1},{6,2},{7,3},{8,12},{9,13},{10,... | collective-permute-start | bytes 393224 | tf_op jit(solution)/shard_map/ppermute | solution.py:346
  6.2 0.1 collective-permute-start.3
  6.4 6.3 %all-to-all-start = ((bf16[32,16,128]{2,1,0:T(8,128)(2,1)}), bf16[32,16,128]{2,1,0:T(8,128)(2,1)S(1)}, u32[]{:S(2)}, u32[]{:S(2)}) async-start(bf16[32,16,128]{2,1,0:T(8,128)(2,1)} %get-tuple-element.19), calls=%async_computation | async-start | bytes 262144 | tf_op jit(solution)/shard_map/all_to_all | solution.py:352
  12.6 0.0 collective-permute-done.1.refs_2_
  12.6 0.3 collective-permute-start.4
  12.9 0.0 collective-permute-done.2.refs_3_
  13.0 0.3 collective-permute-start.5
  13.2 0.0 collective-permute-done.3.refs_4_
  13.2 0.3 collective-permute-start.6
  13.5 0.3 collective-permute-start
  13.7 3.0 %suffix_attention.1 = (f32[4,64,128]{2,1,0:T(8,128)S(1)}, f32[4,64,128]{2,1,0:T(8,128)S(1)}) custom-call(s32[4]{0:T(128)} %len_in.1, f32[4,64,128]{2,1,0:T(8,128)S(1)} %get-tuple-element.20.rows_ref, bf16[4,2,1024]{2,1,0:T(2,128)(2,1)} %new_in.1, bf16[4,2,128,1024]{3,2,1,0:T(8,128)(2,1)} %kv_in.1), custom_call_target="tpu_custom_call" | custom-call | flops 134217728 | bytes 2097152 | tf_op jit(solution)/shard_map/suffix_attention/pallas_call | solution.py:356
  16.7 4.1 %all-to-all-done.q_ref = bf16[32,16,128]{2,1,0:T(8,128)(2,1)S(1)} async-done(((bf16[32,16,128]{2,1,0:T(8,128)(2,1)}), bf16[32,16,128]{2,1,0:T(8,128)(2,1)S(1)}, u32[]{:S(2)}, u32[]{:S(2)}) %all-to-all-start) | async-done | bytes 131104 | tf_op jit(solution)/shard_map/all_to_all | solution.py:352
  20.9 0.0 collective-permute-done.refs_1_
  20.9 0.0 collective-permute-done.4.refs_5_
  20.9 0.0 collective-permute-done.5.refs_6_
  20.9 0.0 collective-permute-done.6.refs_7_
  20.9 1.0 %prefix_attention.1 = bf16[288,2,128]{2,1,0:T(2,128)(2,1)S(1)} custom-call(bf16[32,16,128]{2,1,0:T(8,128)(2,1)S(1)} %all-to-all-done.q_ref, bf16[2,128,128]{2,1,0:T(8,128)(2,1)S(1)} %get-tuple-element.24.refs_0_, bf16[2,128,128]{2,1,0:T(8,128)(2,1)S(1)} %collective-permute-done.refs_1_, bf16[2,2,128,128]{3,2,1,0:T(8,128)(2,1)S(1)} %collective-permute-done.1.refs_2_, ...), custom_call_target="tpu_custom_call" | custom-call | tf_op jit(solution)/shard_map/prefix_attention/pallas_call | solution.py:382
  21.9 10.2 %all_to_all.10.back_ref = bf16[288,2,128]{2,1,0:T(2,128)(2,1)S(1)} all-to-all(bf16[288,2,128]{2,1,0:T(2,128)(2,1)S(1)} %prefix_attention.1), channel_id=1, replica_groups=mesh['grp'=4,'seq'=8] {'grp','seq'}, dimensions={0} | all-to-all | bytes 294912 | tf_op jit(solution)/shard_map/all_to_all | solution.py:391
  32.1 1.4 %join.1 = bf16[4,8192]{1,0:T(4,128)(2,1)} custom-call(s32[4]{0:T(128)S(4)} %get-tuple-element.18.routes_ref, bf16[288,2,128]{2,1,0:T(2,128)(2,1)S(1)} %all_to_all.10.back_ref, f32[4,64,128]{2,1,0:T(8,128)S(1)} %get-tuple-element.29.suffix_ref, f32[4,64,128]{2,1,0:T(8,128)S(1)} %get-tuple-element.30.stat_ref), custom_call_target="tpu_custom_call" | custom-call | tf_op jit(solution)/shard_map/join/pallas_call | solution.py:393
Async XLA Ops:
  1.8 10.9 %collective-permute-start.1 = (bf16[2,2,128,128]{3,2,1,0:T(8,128)(2,1)S(1)}, bf16[2,2,128,128]{3,2,1,0:T(8,128)(2,1)S(1)}, u32[]{:S(2)}, u32[]{:S(2)}) collective-permute-start(bf16[2,2,128,128]{3,2,1,0:T(8,128)(2,1)S(1)} %get-tuple-element.26), channel_id=1, source_target_pairs={{0,6},{1,7},{2,4},{3,5},{4,2},{5,3},{6,0},{7,1},{8,14},{9,15},{10,... | collective-permute-start | bytes 393224 | tf_op jit(solution)/shard_map/ppermute | solution.py:346
  5.7 7.2 %collective-permute-start.2 = (bf16[2,2,128,128]{3,2,1,0:T(8,128)(2,1)S(1)}, bf16[2,2,128,128]{3,2,1,0:T(8,128)(2,1)S(1)}, u32[]{:S(2)}, u32[]{:S(2)}) collective-permute-start(bf16[2,2,128,128]{3,2,1,0:T(8,128)(2,1)S(1)} %get-tuple-element.27), channel_id=1, source_target_pairs={{0,4},{1,5},{2,6},{3,7},{4,0},{5,1},{6,2},{7,3},{8,12},{9,13},{10,... | collective-permute-start | bytes 393224 | tf_op jit(solution)/shard_map/ppermute | solution.py:346
  6.2 7.0 %collective-permute-start.3 = (bf16[2,2,128,128]{3,2,1,0:T(8,128)(2,1)S(1)}, bf16[2,2,128,128]{3,2,1,0:T(8,128)(2,1)S(1)}, u32[]{:S(2)}, u32[]{:S(2)}) collective-permute-start(bf16[2,2,128,128]{3,2,1,0:T(8,128)(2,1)S(1)} %get-tuple-element.28), channel_id=1, source_target_pairs={{0,2},{1,3},{2,0},{3,1},{4,6},{5,7},{6,4},{7,5},{8,10},{9,11},{10,... | collective-permute-start | bytes 393224 | tf_op jit(solution)/shard_map/ppermute | solution.py:346
  6.4 14.5 %all-to-all-start = ((bf16[32,16,128]{2,1,0:T(8,128)(2,1)}), bf16[32,16,128]{2,1,0:T(8,128)(2,1)S(1)}, u32[]{:S(2)}, u32[]{:S(2)}) async-start(bf16[32,16,128]{2,1,0:T(8,128)(2,1)} %get-tuple-element.19), calls=%async_computation | async-start | bytes 262144 | tf_op jit(solution)/shard_map/all_to_all | solution.py:352
  12.6 8.2 %collective-permute-start.4 = (bf16[2,2,128,128]{3,2,1,0:T(8,128)(2,1)S(1)}, bf16[2,2,128,128]{3,2,1,0:T(8,128)(2,1)S(1)}, u32[]{:S(2)}, u32[]{:S(2)}) collective-permute-start(bf16[2,2,128,128]{3,2,1,0:T(8,128)(2,1)S(1)} %collective-permute-done.1.refs_2_), channel_id=1, source_target_pairs={{0,1},{1,0},{2,3},{3,2},{4,5},{5,4},{6,7},{7,6},{8,9},{9,8},{10,11... | collective-permute-start | bytes 393224 | tf_op jit(solution)/shard_map/ppermute | solution.py:346
  13.0 7.9 %collective-permute-start.5 = (bf16[2,2,128,128]{3,2,1,0:T(8,128)(2,1)S(1)}, bf16[2,2,128,128]{3,2,1,0:T(8,128)(2,1)S(1)}, u32[]{:S(2)}, u32[]{:S(2)}) collective-permute-start(bf16[2,2,128,128]{3,2,1,0:T(8,128)(2,1)S(1)} %collective-permute-done.2.refs_3_), channel_id=1, source_target_pairs={{0,1},{1,0},{2,3},{3,2},{4,5},{5,4},{6,7},{7,6},{8,9},{9,8},{10,11... | collective-permute-start | bytes 393224 | tf_op jit(solution)/shard_map/ppermute | solution.py:346
  13.2 7.7 %collective-permute-start.6 = (bf16[2,2,128,128]{3,2,1,0:T(8,128)(2,1)S(1)}, bf16[2,2,128,128]{3,2,1,0:T(8,128)(2,1)S(1)}, u32[]{:S(2)}, u32[]{:S(2)}) collective-permute-start(bf16[2,2,128,128]{3,2,1,0:T(8,128)(2,1)S(1)} %collective-permute-done.3.refs_4_), channel_id=1, source_target_pairs={{0,1},{1,0},{2,3},{3,2},{4,5},{5,4},{6,7},{7,6},{8,9},{9,8},{10,11... | collective-permute-start | bytes 393224 | tf_op jit(solution)/shard_map/ppermute | solution.py:346
  13.5 7.4 %collective-permute-start = (bf16[2,128,128]{2,1,0:T(8,128)(2,1)S(1)}, bf16[2,128,128]{2,1,0:T(8,128)(2,1)S(1)}, u32[]{:S(2)}, u32[]{:S(2)}) collective-permute-start(bf16[2,128,128]{2,1,0:T(8,128)(2,1)S(1)} %get-tuple-element.25), channel_id=1, source_target_pairs={{0,1},{1,0},{2,3},{3,2},{4,5},{5,4},{6,7},{7,6},{8,9},{9,8},{10,11... | collective-permute-start | bytes 196616 | tf_op jit(solution)/shard_map/ppermute | solution.py:346

commit v7 on v6

--- a/solution.py
+++ b/solution.py
@@ -29,6 +29,10 @@
 in_vmem = functools.partial(pltpu.with_memory_space_constraint, memory_space=pltpu.VMEM)
 
 
+def position(g, s, groups, seq):
+    return s * groups + (groups - 1 - g)
+
+
 def slots_of(routes_ref, requests):
     routes = [routes_ref[r] for r in range(requests)]
     ranks = []
@@ -65,7 +69,7 @@
         for k in range(KVH):
             tile = placed[g * ROWS:(g + 1) * ROWS, k * HEAD:(k + 1) * HEAD]
             for t in range(splits):
-                out_ref[(g * splits + t) * KVH + k] = tile
+                out_ref[position(g, t * KVH + k, groups, splits * KVH)] = tile
     sending.start()
     mine = requests * PER
     row = lax.broadcasted_iota(jnp.int32, (mine, cols), 0)
@@ -265,7 +269,7 @@
     requests = out_ref.shape[0]
     routes, ranks = slots_of(routes_ref, requests)
     step = HEAD // ROWS // 2
-    place = lax.axis_index("seq") % step * ROWS
+    place = position(lax.axis_index("grp"), lax.axis_index("seq"), lax.axis_size("grp"), lax.axis_size("seq")) % step * ROWS
     lane = lax.broadcasted_iota(jnp.int32, (PER, HEAD), 1)
     head = lax.broadcasted_iota(jnp.int32, (PER, HEAD), 0)
     pieces = [[None] * requests for _ in range(KVH)]
@@ -277,7 +281,7 @@
             rows = slice(k * PER, (k + 1) * PER)
             levels, parts = [], []
             for t in range(splits):
-                at = ((routes[r] * splits + t) * KVH + k) * BACK
+                at = position(routes[r], t * KVH + k, lax.axis_size("grp"), splits * KVH) * BACK
                 pair = back_ref[pl.ds(at + ranks[r] * (PER // 2), PER // 2)]
                 parts.append(pair.reshape(PER, HEAD).astype(jnp.float32))
                 stat = back_ref[at + PAIRS].astype(jnp.float32)
@@ -321,6 +325,10 @@
     span = suffix_kv.shape[2]
     here = prefix_kv.shape[2]
     everyone = ("grp", "seq")
+    order = [0] * (groups * seq)
+    for g in range(groups):
+        for s in range(seq):
+            order[position(g, s, groups, seq)] = g * seq + s
     routes = prefix_of.reshape(requests)
 
     outgoing, rows, routes, *blocks = pl.pallas_call(
@@ -350,7 +358,7 @@
     parts += pairs + [swap(pair, 1) for pair in pairs]
 
     arrived = lax.all_to_all(
-        outgoing, everyone, split_axis=0, concat_axis=0, tiled=True
+        outgoing, everyone, split_axis=0, concat_axis=0, tiled=True, axis_index_groups=[order]
     )
 
     suffix_out, suffix_stat = pl.pallas_call(
@@ -388,7 +396,11 @@
         name="prefix_attention",
     )(arrived, *parts)
 
-    home = in_vmem(lax.all_to_all(back, everyone, split_axis=0, concat_axis=0, tiled=True))
+    home = in_vmem(
+        lax.all_to_all(
+            back, everyone, split_axis=0, concat_axis=0, tiled=True, axis_index_groups=[order]
+        )
+    )
 
     return pl.pallas_call(
         functools.partial(join_kernel, splits),

time: 33.7 us -> 32.9 us (0.976)
  waiting for transfers between devices: 4.12 us -> 3.12 us
    all_to_all x1, waiting for transfers between devices: 4.1 us -> 3.1 us  [on_device(): lax.all_to_all(outgoing, everyone, split_axis=0, concat_axis=0, tiled=Tru...]
where the time goes in v7:
time: 32.9 us; the launch traced here: 32.6 us
  starting transfers between devices  11.9 us (36%)
  blocking collectives  10.3 us (31%)
  Pallas kernels  7.12 us (22%)
  waiting for transfers between devices  3.12 us (9%)
    all_to_all x1, blocking collectives, on_device(): lax.all_to_all(back, everyone, split_axis=0, concat_axis=0, tiled=True, a...  10.3 us
    all_to_all x1, starting transfers between devices, on_device(): lax.all_to_all(outgoing, everyone, split_axis=0, concat_axis=0, tiled=Tru...  6.25 us
    ppermute x7, starting transfers between devices, swap(): return lax.ppermute(block, 'seq', [(s, s ^ j) for s in range(seq)])  5.68 us
    all_to_all x1, waiting for transfers between devices, on_device(): lax.all_to_all(outgoing, everyone, split_axis=0, concat_axis=0, tiled=Tru...  3.1 us
    pallas_call x1, Pallas kernels, on_device(): pl.pallas_call(suffix_kernel, out_shape=(pltpu.VMEM((requests, HEADS, HEA...  3.01 us
    pallas_call x1, Pallas kernels, on_device(): pl.pallas_call(functools.partial(prepare, groups, splits), out_shape=[jax...  1.75 us
    pallas_call x1, Pallas kernels, on_device(): pl.pallas_call(functools.partial(join_kernel, splits), out_shape=jax.Shap...  1.35 us
    pallas_call x1, Pallas kernels, on_device(): pl.pallas_call(prefix_kernel, out_shape=pltpu.VMEM((groups * seq * BACK,...  1 us
  transfers between devices with their start and end apart: 8, of which 1 were waited for; matrix products, arithmetic and copies ran while one was open for 0% of the time, Pallas kernels for 9%

profile of v7, /device:TPU:0, one launch (start us, length us, event | category | flops | bytes accessed | tf_op | source)
XLA Modules:
  0.0 32.6 jit_solution(7526292611342141624)
XLA Ops:
  0.0 1.8 %prepare.1 = (bf16[32,16,128]{2,1,0:T(8,128)(2,1)}, f32[4,64,128]{2,1,0:T(8,128)S(1)}, s32[4]{0:T(128)S(4)}, bf16[2,128,128]{2,1,0:T(8,128)(2,1)S(1)}, bf16[2,12...) custom-call(s32[4]{0:T(128)} %bitcast.1, ...), custom_call_target="tpu_custom_call" | custom-call | tf_op jit(solution)/shard_map/prepare/pallas_call | solution.py:334
  1.8 4.0 %collective-permute-start.1 = (bf16[2,2,128,128]{3,2,1,0:T(8,128)(2,1)S(1)}, bf16[2,2,128,128]{3,2,1,0:T(8,128)(2,1)S(1)}, u32[]{:S(2)}, u32[]{:S(2)}) collective-permute-start(bf16[2,2,128,128]{3,2,1,0:T(8,128)(2,1)S(1)} %get-tuple-element.26), channel_id=1, source_target_pairs={{0,6},{1,7},{2,4},{3,5},{4,2},{5,3},{6,0},{7,1},{8,14},{9,15},{10,... | collective-permute-start | bytes 393224 | tf_op jit(solution)/shard_map/ppermute | solution.py:354
  5.7 0.5 %collective-permute-start.2 = (bf16[2,2,128,128]{3,2,1,0:T(8,128)(2,1)S(1)}, bf16[2,2,128,128]{3,2,1,0:T(8,128)(2,1)S(1)}, u32[]{:S(2)}, u32[]{:S(2)}) collective-permute-start(bf16[2,2,128,128]{3,2,1,0:T(8,128)(2,1)S(1)} %get-tuple-element.27), channel_id=1, source_target_pairs={{0,4},{1,5},{2,6},{3,7},{4,0},{5,1},{6,2},{7,3},{8,12},{9,13},{10,... | collective-permute-start | bytes 393224 | tf_op jit(solution)/shard_map/ppermute | solution.py:354
  6.2 0.1 collective-permute-start.3
  6.4 6.3 %all-to-all-start = ((bf16[32,16,128]{2,1,0:T(8,128)(2,1)}), bf16[32,16,128]{2,1,0:T(8,128)(2,1)S(1)}, u32[]{:S(2)}, u32[]{:S(2)}) async-start(bf16[32,16,128]{2,1,0:T(8,128)(2,1)} %get-tuple-element.19), calls=%async_computation | async-start | bytes 262144 | tf_op jit(solution)/shard_map/all_to_all | solution.py:360
  12.6 0.0 collective-permute-done.1.refs_2_
  12.6 0.3 collective-permute-start.4
  12.9 0.0 collective-permute-done.2.refs_3_
  13.0 0.3 collective-permute-start.5
  13.2 0.0 collective-permute-done.3.refs_4_
  13.2 0.3 collective-permute-start.6
  13.5 0.3 collective-permute-start
  13.7 3.0 %suffix_attention.1 = (f32[4,64,128]{2,1,0:T(8,128)S(1)}, f32[4,64,128]{2,1,0:T(8,128)S(1)}) custom-call(s32[4]{0:T(128)} %len_in.1, f32[4,64,128]{2,1,0:T(8,128)S(1)} %get-tuple-element.20.rows_ref, bf16[4,2,1024]{2,1,0:T(2,128)(2,1)} %new_in.1, bf16[4,2,128,1024]{3,2,1,0:T(8,128)(2,1)} %kv_in.1), custom_call_target="tpu_custom_call" | custom-call | flops 134217728 | bytes 2097152 | tf_op jit(solution)/shard_map/suffix_attention/pallas_call | solution.py:364
  16.7 3.1 %all-to-all-done.q_ref = bf16[32,16,128]{2,1,0:T(8,128)(2,1)S(1)} async-done(((bf16[32,16,128]{2,1,0:T(8,128)(2,1)}), bf16[32,16,128]{2,1,0:T(8,128)(2,1)S(1)}, u32[]{:S(2)}, u32[]{:S(2)}) %all-to-all-start) | async-done | bytes 131104 | tf_op jit(solution)/shard_map/all_to_all | solution.py:360
  19.9 0.0 collective-permute-done.refs_1_
  19.9 0.0 collective-permute-done.4.refs_5_
  19.9 0.0 collective-permute-done.5.refs_6_
  19.9 0.0 collective-permute-done.6.refs_7_
  19.9 1.0 %prefix_attention.1 = bf16[288,2,128]{2,1,0:T(2,128)(2,1)S(1)} custom-call(bf16[32,16,128]{2,1,0:T(8,128)(2,1)S(1)} %all-to-all-done.q_ref, bf16[2,128,128]{2,1,0:T(8,128)(2,1)S(1)} %get-tuple-element.24.refs_0_, bf16[2,128,128]{2,1,0:T(8,128)(2,1)S(1)} %collective-permute-done.refs_1_, bf16[2,2,128,128]{3,2,1,0:T(8,128)(2,1)S(1)} %collective-permute-done.1.refs_2_, ...), custom_call_target="tpu_custom_call" | custom-call | tf_op jit(solution)/shard_map/prefix_attention/pallas_call | solution.py:390
  20.9 10.3 %all_to_all.10.back_ref = bf16[288,2,128]{2,1,0:T(2,128)(2,1)S(1)} all-to-all(bf16[288,2,128]{2,1,0:T(2,128)(2,1)S(1)} %prefix_attention.1), channel_id=1, replica_groups={{24,16,8,0,25,17,9,1,26,18,10,2,27,19,11,3,28,20,12,4,29,21,13,5,30,22,..., dimensions={0} | all-to-all | bytes 294912 | tf_op jit(solution)/shard_map/all_to_all | solution.py:400
  31.2 1.4 %join.1 = bf16[4,8192]{1,0:T(4,128)(2,1)} custom-call(s32[4]{0:T(128)S(4)} %get-tuple-element.18.routes_ref, bf16[288,2,128]{2,1,0:T(2,128)(2,1)S(1)} %all_to_all.10.back_ref, f32[4,64,128]{2,1,0:T(8,128)S(1)} %get-tuple-element.29.suffix_ref, f32[4,64,128]{2,1,0:T(8,128)S(1)} %get-tuple-element.30.stat_ref), custom_call_target="tpu_custom_call" | custom-call | tf_op jit(solution)/shard_map/join/pallas_call | solution.py:405
Async XLA Ops:
  1.8 10.9 %collective-permute-start.1 = (bf16[2,2,128,128]{3,2,1,0:T(8,128)(2,1)S(1)}, bf16[2,2,128,128]{3,2,1,0:T(8,128)(2,1)S(1)}, u32[]{:S(2)}, u32[]{:S(2)}) collective-permute-start(bf16[2,2,128,128]{3,2,1,0:T(8,128)(2,1)S(1)} %get-tuple-element.26), channel_id=1, source_target_pairs={{0,6},{1,7},{2,4},{3,5},{4,2},{5,3},{6,0},{7,1},{8,14},{9,15},{10,... | collective-permute-start | bytes 393224 | tf_op jit(solution)/shard_map/ppermute | solution.py:354
  5.7 7.2 %collective-permute-start.2 = (bf16[2,2,128,128]{3,2,1,0:T(8,128)(2,1)S(1)}, bf16[2,2,128,128]{3,2,1,0:T(8,128)(2,1)S(1)}, u32[]{:S(2)}, u32[]{:S(2)}) collective-permute-start(bf16[2,2,128,128]{3,2,1,0:T(8,128)(2,1)S(1)} %get-tuple-element.27), channel_id=1, source_target_pairs={{0,4},{1,5},{2,6},{3,7},{4,0},{5,1},{6,2},{7,3},{8,12},{9,13},{10,... | collective-permute-start | bytes 393224 | tf_op jit(solution)/shard_map/ppermute | solution.py:354
  6.2 7.0 %collective-permute-start.3 = (bf16[2,2,128,128]{3,2,1,0:T(8,128)(2,1)S(1)}, bf16[2,2,128,128]{3,2,1,0:T(8,128)(2,1)S(1)}, u32[]{:S(2)}, u32[]{:S(2)}) collective-permute-start(bf16[2,2,128,128]{3,2,1,0:T(8,128)(2,1)S(1)} %get-tuple-element.28), channel_id=1, source_target_pairs={{0,2},{1,3},{2,0},{3,1},{4,6},{5,7},{6,4},{7,5},{8,10},{9,11},{10,... | collective-permute-start | bytes 393224 | tf_op jit(solution)/shard_map/ppermute | solution.py:354
  6.4 13.5 %all-to-all-start = ((bf16[32,16,128]{2,1,0:T(8,128)(2,1)}), bf16[32,16,128]{2,1,0:T(8,128)(2,1)S(1)}, u32[]{:S(2)}, u32[]{:S(2)}) async-start(bf16[32,16,128]{2,1,0:T(8,128)(2,1)} %get-tuple-element.19), calls=%async_computation | async-start | bytes 262144 | tf_op jit(solution)/shard_map/all_to_all | solution.py:360
  12.6 7.2 %collective-permute-start.4 = (bf16[2,2,128,128]{3,2,1,0:T(8,128)(2,1)S(1)}, bf16[2,2,128,128]{3,2,1,0:T(8,128)(2,1)S(1)}, u32[]{:S(2)}, u32[]{:S(2)}) collective-permute-start(bf16[2,2,128,128]{3,2,1,0:T(8,128)(2,1)S(1)} %collective-permute-done.1.refs_2_), channel_id=1, source_target_pairs={{0,1},{1,0},{2,3},{3,2},{4,5},{5,4},{6,7},{7,6},{8,9},{9,8},{10,11... | collective-permute-start | bytes 393224 | tf_op jit(solution)/shard_map/ppermute | solution.py:354
  13.0 6.9 %collective-permute-start.5 = (bf16[2,2,128,128]{3,2,1,0:T(8,128)(2,1)S(1)}, bf16[2,2,128,128]{3,2,1,0:T(8,128)(2,1)S(1)}, u32[]{:S(2)}, u32[]{:S(2)}) collective-permute-start(bf16[2,2,128,128]{3,2,1,0:T(8,128)(2,1)S(1)} %collective-permute-done.2.refs_3_), channel_id=1, source_target_pairs={{0,1},{1,0},{2,3},{3,2},{4,5},{5,4},{6,7},{7,6},{8,9},{9,8},{10,11... | collective-permute-start | bytes 393224 | tf_op jit(solution)/shard_map/ppermute | solution.py:354
  13.2 6.7 %collective-permute-start.6 = (bf16[2,2,128,128]{3,2,1,0:T(8,128)(2,1)S(1)}, bf16[2,2,128,128]{3,2,1,0:T(8,128)(2,1)S(1)}, u32[]{:S(2)}, u32[]{:S(2)}) collective-permute-start(bf16[2,2,128,128]{3,2,1,0:T(8,128)(2,1)S(1)} %collective-permute-done.3.refs_4_), channel_id=1, source_target_pairs={{0,1},{1,0},{2,3},{3,2},{4,5},{5,4},{6,7},{7,6},{8,9},{9,8},{10,11... | collective-permute-start | bytes 393224 | tf_op jit(solution)/shard_map/ppermute | solution.py:354
  13.5 6.4 %collective-permute-start = (bf16[2,128,128]{2,1,0:T(8,128)(2,1)S(1)}, bf16[2,128,128]{2,1,0:T(8,128)(2,1)S(1)}, u32[]{:S(2)}, u32[]{:S(2)}) collective-permute-start(bf16[2,128,128]{2,1,0:T(8,128)(2,1)S(1)} %get-tuple-element.25), channel_id=1, source_target_pairs={{0,1},{1,0},{2,3},{3,2},{4,5},{5,4},{6,7},{7,6},{8,9},{9,8},{10,11... | collective-permute-start | bytes 196616 | tf_op jit(solution)/shard_map/ppermute | solution.py:354

commit v8 on v7

--- a/solution.py
+++ b/solution.py
@@ -16,7 +16,6 @@
 SCALE = HEAD ** (-0.5)
 LOG2E = math.log2(math.e)
 LN2 = math.log(2.0)
-SEND = jnp.bfloat16
 ROWS = CAP * PER
 PAIRS = ROWS // 2
 BACK = PAIRS + 1
@@ -204,8 +203,9 @@
                 )
 
 
-def prefix_kernel(q_ref, *refs):
+def prefix_kernel(splits, q_ref, *refs):
     parts, out_ref = refs[:-1], refs[-1]
+    send = out_ref.dtype
     views = [part for part in parts[:2]]
     views += [part.at[0] for part in parts[2:5]] + [part.at[1] for part in parts[5:]]
     keys = jnp.concatenate([view[0] for view in views], axis=0)
@@ -224,21 +224,24 @@
         top = jnp.max(raw, axis=1, keepdims=True)
         weight = jnp.exp2((raw - top) * (SCALE * LOG2E))
         total = jnp.sum(weight, axis=1, keepdims=True)
-        return top, weight.astype(jnp.bfloat16), total
-
-    def store(i, top, weight, total):
-        out = jnp.dot(weight, values, preferred_element_type=jnp.float32)
-        out = (out / total).astype(SEND)
+        rounded = weight.astype(jnp.bfloat16)
+        if splits == 1:
+            return top, (rounded,), total
+        return top, (rounded, (weight - rounded.astype(jnp.float32)).astype(jnp.bfloat16)), total
+
+    def store(i, top, weights, total):
+        out = sum(jnp.dot(w, values, preferred_element_type=jnp.float32) for w in weights)
+        out = (out / total).astype(send)
         level = top * SCALE + jnp.log(total)
         level = jnp.sum(jnp.where(diagonal, level, 0.0), axis=0, keepdims=True)
-        first = level.astype(SEND).astype(jnp.float32)
+        first = level.astype(send).astype(jnp.float32)
         rest = level - first
-        second = rest.astype(SEND).astype(jnp.float32)
+        second = rest.astype(send).astype(jnp.float32)
         third = rest - second
         turned = [pltpu.roll(piece, HALF, 1) for piece in (first, second, third)]
         halves = [
-            jnp.concatenate([jnp.where(low, first, turned[1]), third], axis=0).astype(SEND),
-            jnp.concatenate([jnp.where(low, turned[0], second), turned[2]], axis=0).astype(SEND),
+            jnp.concatenate([jnp.where(low, first, turned[1]), third], axis=0).astype(send),
+            jnp.concatenate([jnp.where(low, turned[0], second), turned[2]], axis=0).astype(send),
         ]
         for s in range(step):
             at = (i * step + s) * BACK
@@ -387,9 +390,10 @@
         (arrived, suffix_out, suffix_stat)
     )
 
+    send = jnp.bfloat16 if splits == 1 else jnp.float32
     back = pl.pallas_call(
-        prefix_kernel,
-        out_shape=pltpu.VMEM((groups * seq * BACK, 2, HEAD), SEND),
+        functools.partial(prefix_kernel, splits),
+        out_shape=pltpu.VMEM((groups * seq * BACK, 2, HEAD), send),
         in_specs=[VMEM] * (1 + KVH),
         out_specs=VMEM,
         compiler_params=pltpu.CompilerParams(vmem_limit_bytes=32 * 1024 * 1024),

time: 32.9 us -> 32.9 us (level)
  no operation moved by 1% of the time
where the time goes in v8:
time: 32.9 us; the launch traced here: 32.6 us
  starting transfers between devices  11.9 us (36%)
  blocking collectives  10.3 us (31%)
  Pallas kernels  7.12 us (22%)
  waiting for transfers between devices  3.12 us (9%)
    all_to_all x1, blocking collectives, on_device(): lax.all_to_all(back, everyone, split_axis=0, concat_axis=0, tiled=True, a...  10.3 us
    all_to_all x1, starting transfers between devices, on_device(): lax.all_to_all(outgoing, everyone, split_axis=0, concat_axis=0, tiled=Tru...  6.25 us
    ppermute x7, starting transfers between devices, swap(): return lax.ppermute(block, 'seq', [(s, s ^ j) for s in range(seq)])  5.68 us
    all_to_all x1, waiting for transfers between devices, on_device(): lax.all_to_all(outgoing, everyone, split_axis=0, concat_axis=0, tiled=Tru...  3.1 us
    pallas_call x1, Pallas kernels, on_device(): pl.pallas_call(suffix_kernel, out_shape=(pltpu.VMEM((requests, HEADS, HEA...  3.01 us
    pallas_call x1, Pallas kernels, on_device(): pl.pallas_call(functools.partial(prepare, groups, splits), out_shape=[jax...  1.75 us
    pallas_call x1, Pallas kernels, on_device(): pl.pallas_call(functools.partial(join_kernel, splits), out_shape=jax.Shap...  1.35 us
    pallas_call x1, Pallas kernels, on_device(): pl.pallas_call(functools.partial(prefix_kernel, splits), out_shape=pltpu....  1 us
  transfers between devices with their start and end apart: 8, of which 1 were waited for; matrix products, arithmetic and copies ran while one was open for 0% of the time, Pallas kernels for 9%

profile of v8, /device:TPU:0, one launch (start us, length us, event | category | flops | bytes accessed | tf_op | source)
XLA Modules:
  0.0 32.6 jit_solution(7526292611342141624)
XLA Ops:
  0.0 1.8 %prepare.1 = (bf16[32,16,128]{2,1,0:T(8,128)(2,1)}, f32[4,64,128]{2,1,0:T(8,128)S(1)}, s32[4]{0:T(128)S(4)}, bf16[2,128,128]{2,1,0:T(8,128)(2,1)S(1)}, bf16[2,12...) custom-call(s32[4]{0:T(128)} %bitcast.1, ...), custom_call_target="tpu_custom_call" | custom-call | tf_op jit(solution)/shard_map/prepare/pallas_call | solution.py:337
  1.8 4.0 %collective-permute-start.1 = (bf16[2,2,128,128]{3,2,1,0:T(8,128)(2,1)S(1)}, bf16[2,2,128,128]{3,2,1,0:T(8,128)(2,1)S(1)}, u32[]{:S(2)}, u32[]{:S(2)}) collective-permute-start(bf16[2,2,128,128]{3,2,1,0:T(8,128)(2,1)S(1)} %get-tuple-element.26), channel_id=1, source_target_pairs={{0,6},{1,7},{2,4},{3,5},{4,2},{5,3},{6,0},{7,1},{8,14},{9,15},{10,... | collective-permute-start | bytes 393224 | tf_op jit(solution)/shard_map/ppermute | solution.py:357
  5.7 0.5 %collective-permute-start.2 = (bf16[2,2,128,128]{3,2,1,0:T(8,128)(2,1)S(1)}, bf16[2,2,128,128]{3,2,1,0:T(8,128)(2,1)S(1)}, u32[]{:S(2)}, u32[]{:S(2)}) collective-permute-start(bf16[2,2,128,128]{3,2,1,0:T(8,128)(2,1)S(1)} %get-tuple-element.27), channel_id=1, source_target_pairs={{0,4},{1,5},{2,6},{3,7},{4,0},{5,1},{6,2},{7,3},{8,12},{9,13},{10,... | collective-permute-start | bytes 393224 | tf_op jit(solution)/shard_map/ppermute | solution.py:357
  6.2 0.1 collective-permute-start.3
  6.4 6.3 %all-to-all-start = ((bf16[32,16,128]{2,1,0:T(8,128)(2,1)}), bf16[32,16,128]{2,1,0:T(8,128)(2,1)S(1)}, u32[]{:S(2)}, u32[]{:S(2)}) async-start(bf16[32,16,128]{2,1,0:T(8,128)(2,1)} %get-tuple-element.19), calls=%async_computation | async-start | bytes 262144 | tf_op jit(solution)/shard_map/all_to_all | solution.py:363
  12.6 0.0 collective-permute-done.1.refs_2_
  12.6 0.3 collective-permute-start.4
  12.9 0.0 collective-permute-done.2.refs_3_
  13.0 0.3 collective-permute-start.5
  13.2 0.0 collective-permute-done.3.refs_4_
  13.2 0.3 collective-permute-start.6
  13.5 0.3 collective-permute-start
  13.7 3.0 %suffix_attention.1 = (f32[4,64,128]{2,1,0:T(8,128)S(1)}, f32[4,64,128]{2,1,0:T(8,128)S(1)}) custom-call(s32[4]{0:T(128)} %len_in.1, f32[4,64,128]{2,1,0:T(8,128)S(1)} %get-tuple-element.20.rows_ref, bf16[4,2,1024]{2,1,0:T(2,128)(2,1)} %new_in.1, bf16[4,2,128,1024]{3,2,1,0:T(8,128)(2,1)} %kv_in.1), custom_call_target="tpu_custom_call" | custom-call | flops 134217728 | bytes 2097152 | tf_op jit(solution)/shard_map/suffix_attention/pallas_call | solution.py:367
  16.7 3.1 %all-to-all-done.q_ref = bf16[32,16,128]{2,1,0:T(8,128)(2,1)S(1)} async-done(((bf16[32,16,128]{2,1,0:T(8,128)(2,1)}), bf16[32,16,128]{2,1,0:T(8,128)(2,1)S(1)}, u32[]{:S(2)}, u32[]{:S(2)}) %all-to-all-start) | async-done | bytes 131104 | tf_op jit(solution)/shard_map/all_to_all | solution.py:363
  19.9 0.0 collective-permute-done.refs_1_
  19.9 0.0 collective-permute-done.4.refs_5_
  19.9 0.0 collective-permute-done.5.refs_6_
  19.9 0.0 collective-permute-done.6.refs_7_
  19.9 1.0 %prefix_attention.1 = bf16[288,2,128]{2,1,0:T(2,128)(2,1)S(1)} custom-call(bf16[32,16,128]{2,1,0:T(8,128)(2,1)S(1)} %all-to-all-done.q_ref, bf16[2,128,128]{2,1,0:T(8,128)(2,1)S(1)} %get-tuple-element.24.refs_0_, bf16[2,128,128]{2,1,0:T(8,128)(2,1)S(1)} %collective-permute-done.refs_1_, bf16[2,2,128,128]{3,2,1,0:T(8,128)(2,1)S(1)} %collective-permute-done.1.refs_2_, ...), custom_call_target="tpu_custom_call" | custom-call | tf_op jit(solution)/shard_map/prefix_attention/pallas_call | solution.py:394
  20.9 10.3 %all_to_all.10.back_ref = bf16[288,2,128]{2,1,0:T(2,128)(2,1)S(1)} all-to-all(bf16[288,2,128]{2,1,0:T(2,128)(2,1)S(1)} %prefix_attention.1), channel_id=1, replica_groups={{24,16,8,0,25,17,9,1,26,18,10,2,27,19,11,3,28,20,12,4,29,21,13,5,30,22,..., dimensions={0} | all-to-all | bytes 294912 | tf_op jit(solution)/shard_map/all_to_all | solution.py:404
  31.2 1.4 %join.1 = bf16[4,8192]{1,0:T(4,128)(2,1)} custom-call(s32[4]{0:T(128)S(4)} %get-tuple-element.18.routes_ref, bf16[288,2,128]{2,1,0:T(2,128)(2,1)S(1)} %all_to_all.10.back_ref, f32[4,64,128]{2,1,0:T(8,128)S(1)} %get-tuple-element.29.suffix_ref, f32[4,64,128]{2,1,0:T(8,128)S(1)} %get-tuple-element.30.stat_ref), custom_call_target="tpu_custom_call" | custom-call | tf_op jit(solution)/shard_map/join/pallas_call | solution.py:409
Async XLA Ops:
  1.8 10.9 %collective-permute-start.1 = (bf16[2,2,128,128]{3,2,1,0:T(8,128)(2,1)S(1)}, bf16[2,2,128,128]{3,2,1,0:T(8,128)(2,1)S(1)}, u32[]{:S(2)}, u32[]{:S(2)}) collective-permute-start(bf16[2,2,128,128]{3,2,1,0:T(8,128)(2,1)S(1)} %get-tuple-element.26), channel_id=1, source_target_pairs={{0,6},{1,7},{2,4},{3,5},{4,2},{5,3},{6,0},{7,1},{8,14},{9,15},{10,... | collective-permute-start | bytes 393224 | tf_op jit(solution)/shard_map/ppermute | solution.py:357
  5.7 7.2 %collective-permute-start.2 = (bf16[2,2,128,128]{3,2,1,0:T(8,128)(2,1)S(1)}, bf16[2,2,128,128]{3,2,1,0:T(8,128)(2,1)S(1)}, u32[]{:S(2)}, u32[]{:S(2)}) collective-permute-start(bf16[2,2,128,128]{3,2,1,0:T(8,128)(2,1)S(1)} %get-tuple-element.27), channel_id=1, source_target_pairs={{0,4},{1,5},{2,6},{3,7},{4,0},{5,1},{6,2},{7,3},{8,12},{9,13},{10,... | collective-permute-start | bytes 393224 | tf_op jit(solution)/shard_map/ppermute | solution.py:357
  6.2 7.0 %collective-permute-start.3 = (bf16[2,2,128,128]{3,2,1,0:T(8,128)(2,1)S(1)}, bf16[2,2,128,128]{3,2,1,0:T(8,128)(2,1)S(1)}, u32[]{:S(2)}, u32[]{:S(2)}) collective-permute-start(bf16[2,2,128,128]{3,2,1,0:T(8,128)(2,1)S(1)} %get-tuple-element.28), channel_id=1, source_target_pairs={{0,2},{1,3},{2,0},{3,1},{4,6},{5,7},{6,4},{7,5},{8,10},{9,11},{10,... | collective-permute-start | bytes 393224 | tf_op jit(solution)/shard_map/ppermute | solution.py:357
  6.4 13.5 %all-to-all-start = ((bf16[32,16,128]{2,1,0:T(8,128)(2,1)}), bf16[32,16,128]{2,1,0:T(8,128)(2,1)S(1)}, u32[]{:S(2)}, u32[]{:S(2)}) async-start(bf16[32,16,128]{2,1,0:T(8,128)(2,1)} %get-tuple-element.19), calls=%async_computation | async-start | bytes 262144 | tf_op jit(solution)/shard_map/all_to_all | solution.py:363
  12.6 7.2 %collective-permute-start.4 = (bf16[2,2,128,128]{3,2,1,0:T(8,128)(2,1)S(1)}, bf16[2,2,128,128]{3,2,1,0:T(8,128)(2,1)S(1)}, u32[]{:S(2)}, u32[]{:S(2)}) collective-permute-start(bf16[2,2,128,128]{3,2,1,0:T(8,128)(2,1)S(1)} %collective-permute-done.1.refs_2_), channel_id=1, source_target_pairs={{0,1},{1,0},{2,3},{3,2},{4,5},{5,4},{6,7},{7,6},{8,9},{9,8},{10,11... | collective-permute-start | bytes 393224 | tf_op jit(solution)/shard_map/ppermute | solution.py:357
  13.0 6.9 %collective-permute-start.5 = (bf16[2,2,128,128]{3,2,1,0:T(8,128)(2,1)S(1)}, bf16[2,2,128,128]{3,2,1,0:T(8,128)(2,1)S(1)}, u32[]{:S(2)}, u32[]{:S(2)}) collective-permute-start(bf16[2,2,128,128]{3,2,1,0:T(8,128)(2,1)S(1)} %collective-permute-done.2.refs_3_), channel_id=1, source_target_pairs={{0,1},{1,0},{2,3},{3,2},{4,5},{5,4},{6,7},{7,6},{8,9},{9,8},{10,11... | collective-permute-start | bytes 393224 | tf_op jit(solution)/shard_map/ppermute | solution.py:357
  13.2 6.7 %collective-permute-start.6 = (bf16[2,2,128,128]{3,2,1,0:T(8,128)(2,1)S(1)}, bf16[2,2,128,128]{3,2,1,0:T(8,128)(2,1)S(1)}, u32[]{:S(2)}, u32[]{:S(2)}) collective-permute-start(bf16[2,2,128,128]{3,2,1,0:T(8,128)(2,1)S(1)} %collective-permute-done.3.refs_4_), channel_id=1, source_target_pairs={{0,1},{1,0},{2,3},{3,2},{4,5},{5,4},{6,7},{7,6},{8,9},{9,8},{10,11... | collective-permute-start | bytes 393224 | tf_op jit(solution)/shard_map/ppermute | solution.py:357
  13.5 6.4 %collective-permute-start = (bf16[2,128,128]{2,1,0:T(8,128)(2,1)S(1)}, bf16[2,128,128]{2,1,0:T(8,128)(2,1)S(1)}, u32[]{:S(2)}, u32[]{:S(2)}) collective-permute-start(bf16[2,128,128]{2,1,0:T(8,128)(2,1)S(1)} %get-tuple-element.25), channel_id=1, source_target_pairs={{0,1},{1,0},{2,3},{3,2},{4,5},{5,4},{6,7},{7,6},{8,9},{9,8},{10,11... | collective-permute-start | bytes 196616 | tf_op jit(solution)/shard_map/ppermute | solution.py:357

commit v9 on v8

--- a/solution.py
+++ b/solution.py
@@ -127,7 +127,6 @@
     ]
     for copy in small + cached[0] + cached[1]:
         copy.start()
-    lane = lax.broadcasted_iota(jnp.int32, (HEADS, HEAD), 1)
     upper = lax.broadcasted_iota(jnp.int32, (2 * PER, HEAD), 0) < PER
     wides = []
     for r in range(requests):
@@ -176,13 +175,14 @@
         )
         live = lax.broadcasted_iota(jnp.int32, raw.shape, 1) < len_ref[r]
         raws.append(jnp.where(live, raw, -jnp.inf))
-    weights, own_weights = [], []
+    weights, own_weights, shares = [], [], []
     for r in range(requests):
         top = jnp.maximum(jnp.max(raws[r], axis=1, keepdims=True), owns[r])
         weight = jnp.exp2((raws[r] - top) * (SCALE * LOG2E))
         own_weight = jnp.exp2((owns[r] - top) * (SCALE * LOG2E))
         total = jnp.sum(weight, axis=1, keepdims=True) + own_weight
-        stat_ref[r] = jnp.where(lane == 0, top * SCALE, total)
+        stat_ref[r] = jnp.broadcast_to(top * SCALE + jnp.log(total), (HEADS, HEAD))
+        shares.append(1.0 / total)
         weights.append(weight.astype(jnp.bfloat16))
         own_weights.append(own_weight.astype(jnp.bfloat16).astype(jnp.float32))
     for r in range(requests):
@@ -197,7 +197,7 @@
                 k = 2 * pair + j
                 rows = slice(k * PER, (k + 1) * PER)
                 cols = slice(k * HEAD, (k + 1) * HEAD)
-                out_ref[r, rows, :] = (
+                out_ref[r, rows, :] = shares[r][rows] * (
                     both[j * PER:(j + 1) * PER, j * HEAD:(j + 1) * HEAD]
                     + own_weights[r][rows] * news[r][1:2, cols]
                 )
@@ -290,13 +290,23 @@
                 stat = back_ref[at + PAIRS].astype(jnp.float32)
                 stat = jnp.where(twice, stat[0:1], 0.0) + jnp.where(once, stat[1:2], 0.0)
                 levels.append(jnp.sum(stat, axis=1, keepdims=True))
-            suffix_top = stats[rows, 0:1]
-            top = suffix_top
+            base = stats[rows, :]
+            mixed = suffix_ref[r, rows, :]
+            if splits == 1:
+                ahead = levels[0] - base
+                less = jnp.exp(-jnp.abs(ahead))
+                more = 1.0 / (1.0 + less)
+                less = less * more
+                pieces[k][r] = (
+                    jnp.where(ahead >= 0.0, more, less) * parts[0]
+                    + jnp.where(ahead >= 0.0, less, more) * mixed
+                )
+                continue
+            top = base
             for level in levels:
                 top = jnp.maximum(top, level)
-            from_suffix = jnp.exp(suffix_top - top)
-            numer = from_suffix * suffix_ref[r, rows, :]
-            denom = from_suffix * stats[rows, 1:2]
+            denom = jnp.exp(base - top)
+            numer = denom * mixed
             for level, part in zip(levels, parts):
                 from_prefix = jnp.exp(level - top)
                 numer = numer + from_prefix * part

time: 32.9 us -> 32.5 us (0.988)
  Pallas kernels: 7.12 us -> 6.48 us
    pallas_call x1, Pallas kernels: 1.35 us -> 0.94 us  [on_device(): pl.pallas_call(functools.partial(join_kernel, splits), out_shape=jax.Shap...]
where the time goes in v9:
time: 32.5 us; the launch traced here: 32.1 us
  starting transfers between devices  11.9 us (37%)
  blocking collectives  10.3 us (32%)
  Pallas kernels  6.48 us (20%)
  waiting for transfers between devices  3.35 us (10%)
    all_to_all x1, blocking collectives, on_device(): lax.all_to_all(back, everyone, split_axis=0, concat_axis=0, tiled=True, a...  10.3 us
    all_to_all x1, starting transfers between devices, on_device(): lax.all_to_all(outgoing, everyone, split_axis=0, concat_axis=0, tiled=Tru...  6.25 us
    ppermute x7, starting transfers between devices, swap(): return lax.ppermute(block, 'seq', [(s, s ^ j) for s in range(seq)])  5.68 us
    all_to_all x1, waiting for transfers between devices, on_device(): lax.all_to_all(outgoing, everyone, split_axis=0, concat_axis=0, tiled=Tru...  3.33 us
    pallas_call x1, Pallas kernels, on_device(): pl.pallas_call(suffix_kernel, out_shape=(pltpu.VMEM((requests, HEADS, HEA...  2.79 us
    pallas_call x1, Pallas kernels, on_device(): pl.pallas_call(functools.partial(prepare, groups, splits), out_shape=[jax...  1.75 us
    pallas_call x1, Pallas kernels, on_device(): pl.pallas_call(functools.partial(prefix_kernel, splits), out_shape=pltpu....  1 us
    pallas_call x1, Pallas kernels, on_device(): pl.pallas_call(functools.partial(join_kernel, splits), out_shape=jax.Shap...  0.94 us
  transfers between devices with their start and end apart: 8, of which 1 were waited for; matrix products, arithmetic and copies ran while one was open for 0% of the time, Pallas kernels for 9%

profile of v9, /device:TPU:0, one launch (start us, length us, event | category | flops | bytes accessed | tf_op | source)
XLA Modules:
  0.0 32.1 jit_solution(6989837059232593404)
XLA Ops:
  0.0 1.8 %prepare.1 = (bf16[32,16,128]{2,1,0:T(8,128)(2,1)}, f32[4,64,128]{2,1,0:T(8,128)S(1)}, s32[4]{0:T(128)S(4)}, bf16[2,128,128]{2,1,0:T(8,128)(2,1)S(1)}, bf16[2,12...) custom-call(s32[4]{0:T(128)} %bitcast.1, ...), custom_call_target="tpu_custom_call" | custom-call | tf_op jit(solution)/shard_map/prepare/pallas_call | solution.py:347
  1.8 4.0 %collective-permute-start.1 = (bf16[2,2,128,128]{3,2,1,0:T(8,128)(2,1)S(1)}, bf16[2,2,128,128]{3,2,1,0:T(8,128)(2,1)S(1)}, u32[]{:S(2)}, u32[]{:S(2)}) collective-permute-start(bf16[2,2,128,128]{3,2,1,0:T(8,128)(2,1)S(1)} %get-tuple-element.26), channel_id=1, source_target_pairs={{0,6},{1,7},{2,4},{3,5},{4,2},{5,3},{6,0},{7,1},{8,14},{9,15},{10,... | collective-permute-start | bytes 393224 | tf_op jit(solution)/shard_map/ppermute | solution.py:367
  5.7 0.5 %collective-permute-start.2 = (bf16[2,2,128,128]{3,2,1,0:T(8,128)(2,1)S(1)}, bf16[2,2,128,128]{3,2,1,0:T(8,128)(2,1)S(1)}, u32[]{:S(2)}, u32[]{:S(2)}) collective-permute-start(bf16[2,2,128,128]{3,2,1,0:T(8,128)(2,1)S(1)} %get-tuple-element.27), channel_id=1, source_target_pairs={{0,4},{1,5},{2,6},{3,7},{4,0},{5,1},{6,2},{7,3},{8,12},{9,13},{10,... | collective-permute-start | bytes 393224 | tf_op jit(solution)/shard_map/ppermute | solution.py:367
  6.2 0.1 collective-permute-start.3
  6.4 6.3 %all-to-all-start = ((bf16[32,16,128]{2,1,0:T(8,128)(2,1)}), bf16[32,16,128]{2,1,0:T(8,128)(2,1)S(1)}, u32[]{:S(2)}, u32[]{:S(2)}) async-start(bf16[32,16,128]{2,1,0:T(8,128)(2,1)} %get-tuple-element.19), calls=%async_computation | async-start | bytes 262144 | tf_op jit(solution)/shard_map/all_to_all | solution.py:373
  12.6 0.0 collective-permute-done.1.refs_2_
  12.6 0.3 collective-permute-start.4
  12.9 0.0 collective-permute-done.2.refs_3_
  13.0 0.3 collective-permute-start.5
  13.2 0.0 collective-permute-done.3.refs_4_
  13.2 0.3 collective-permute-start.6
  13.5 0.3 collective-permute-start
  13.7 2.8 %suffix_attention.1 = (f32[4,64,128]{2,1,0:T(8,128)S(1)}, f32[4,64,128]{2,1,0:T(8,128)S(1)}) custom-call(s32[4]{0:T(128)} %len_in.1, f32[4,64,128]{2,1,0:T(8,128)S(1)} %get-tuple-element.20.rows_ref, bf16[4,2,1024]{2,1,0:T(2,128)(2,1)} %new_in.1, bf16[4,2,128,1024]{3,2,1,0:T(8,128)(2,1)} %kv_in.1), custom_call_target="tpu_custom_call" | custom-call | flops 134217728 | bytes 2097152 | tf_op jit(solution)/shard_map/suffix_attention/pallas_call | solution.py:377
  16.5 3.3 %all-to-all-done.q_ref = bf16[32,16,128]{2,1,0:T(8,128)(2,1)S(1)} async-done(((bf16[32,16,128]{2,1,0:T(8,128)(2,1)}), bf16[32,16,128]{2,1,0:T(8,128)(2,1)S(1)}, u32[]{:S(2)}, u32[]{:S(2)}) %all-to-all-start) | async-done | bytes 131104 | tf_op jit(solution)/shard_map/all_to_all | solution.py:373
  19.9 0.0 collective-permute-done.refs_1_
  19.9 0.0 collective-permute-done.4.refs_5_
  19.9 0.0 collective-permute-done.5.refs_6_
  19.9 0.0 collective-permute-done.6.refs_7_
  19.9 1.0 %prefix_attention.1 = bf16[288,2,128]{2,1,0:T(2,128)(2,1)S(1)} custom-call(bf16[32,16,128]{2,1,0:T(8,128)(2,1)S(1)} %all-to-all-done.q_ref, bf16[2,128,128]{2,1,0:T(8,128)(2,1)S(1)} %get-tuple-element.24.refs_0_, bf16[2,128,128]{2,1,0:T(8,128)(2,1)S(1)} %collective-permute-done.refs_1_, bf16[2,2,128,128]{3,2,1,0:T(8,128)(2,1)S(1)} %collective-permute-done.1.refs_2_, ...), custom_call_target="tpu_custom_call" | custom-call | tf_op jit(solution)/shard_map/prefix_attention/pallas_call | solution.py:404
  20.9 10.3 %all_to_all.10.back_ref = bf16[288,2,128]{2,1,0:T(2,128)(2,1)S(1)} all-to-all(bf16[288,2,128]{2,1,0:T(2,128)(2,1)S(1)} %prefix_attention.1), channel_id=1, replica_groups={{24,16,8,0,25,17,9,1,26,18,10,2,27,19,11,3,28,20,12,4,29,21,13,5,30,22,..., dimensions={0} | all-to-all | bytes 294912 | tf_op jit(solution)/shard_map/all_to_all | solution.py:414
  31.2 0.9 %join.1 = bf16[4,8192]{1,0:T(4,128)(2,1)} custom-call(s32[4]{0:T(128)S(4)} %get-tuple-element.18.routes_ref, bf16[288,2,128]{2,1,0:T(2,128)(2,1)S(1)} %all_to_all.10.back_ref, f32[4,64,128]{2,1,0:T(8,128)S(1)} %get-tuple-element.29.suffix_ref, f32[4,64,128]{2,1,0:T(8,128)S(1)} %get-tuple-element.30.stat_ref), custom_call_target="tpu_custom_call" | custom-call | tf_op jit(solution)/shard_map/join/pallas_call | solution.py:419
Async XLA Ops:
  1.8 10.9 %collective-permute-start.1 = (bf16[2,2,128,128]{3,2,1,0:T(8,128)(2,1)S(1)}, bf16[2,2,128,128]{3,2,1,0:T(8,128)(2,1)S(1)}, u32[]{:S(2)}, u32[]{:S(2)}) collective-permute-start(bf16[2,2,128,128]{3,2,1,0:T(8,128)(2,1)S(1)} %get-tuple-element.26), channel_id=1, source_target_pairs={{0,6},{1,7},{2,4},{3,5},{4,2},{5,3},{6,0},{7,1},{8,14},{9,15},{10,... | collective-permute-start | bytes 393224 | tf_op jit(solution)/shard_map/ppermute | solution.py:367
  5.7 7.2 %collective-permute-start.2 = (bf16[2,2,128,128]{3,2,1,0:T(8,128)(2,1)S(1)}, bf16[2,2,128,128]{3,2,1,0:T(8,128)(2,1)S(1)}, u32[]{:S(2)}, u32[]{:S(2)}) collective-permute-start(bf16[2,2,128,128]{3,2,1,0:T(8,128)(2,1)S(1)} %get-tuple-element.27), channel_id=1, source_target_pairs={{0,4},{1,5},{2,6},{3,7},{4,0},{5,1},{6,2},{7,3},{8,12},{9,13},{10,... | collective-permute-start | bytes 393224 | tf_op jit(solution)/shard_map/ppermute | solution.py:367
  6.2 7.0 %collective-permute-start.3 = (bf16[2,2,128,128]{3,2,1,0:T(8,128)(2,1)S(1)}, bf16[2,2,128,128]{3,2,1,0:T(8,128)(2,1)S(1)}, u32[]{:S(2)}, u32[]{:S(2)}) collective-permute-start(bf16[2,2,128,128]{3,2,1,0:T(8,128)(2,1)S(1)} %get-tuple-element.28), channel_id=1, source_target_pairs={{0,2},{1,3},{2,0},{3,1},{4,6},{5,7},{6,4},{7,5},{8,10},{9,11},{10,... | collective-permute-start | bytes 393224 | tf_op jit(solution)/shard_map/ppermute | solution.py:367
  6.4 13.5 %all-to-all-start = ((bf16[32,16,128]{2,1,0:T(8,128)(2,1)}), bf16[32,16,128]{2,1,0:T(8,128)(2,1)S(1)}, u32[]{:S(2)}, u32[]{:S(2)}) async-start(bf16[32,16,128]{2,1,0:T(8,128)(2,1)} %get-tuple-element.19), calls=%async_computation | async-start | bytes 262144 | tf_op jit(solution)/shard_map/all_to_all | solution.py:373
  12.6 7.2 %collective-permute-start.4 = (bf16[2,2,128,128]{3,2,1,0:T(8,128)(2,1)S(1)}, bf16[2,2,128,128]{3,2,1,0:T(8,128)(2,1)S(1)}, u32[]{:S(2)}, u32[]{:S(2)}) collective-permute-start(bf16[2,2,128,128]{3,2,1,0:T(8,128)(2,1)S(1)} %collective-permute-done.1.refs_2_), channel_id=1, source_target_pairs={{0,1},{1,0},{2,3},{3,2},{4,5},{5,4},{6,7},{7,6},{8,9},{9,8},{10,11... | collective-permute-start | bytes 393224 | tf_op jit(solution)/shard_map/ppermute | solution.py:367
  13.0 6.9 %collective-permute-start.5 = (bf16[2,2,128,128]{3,2,1,0:T(8,128)(2,1)S(1)}, bf16[2,2,128,128]{3,2,1,0:T(8,128)(2,1)S(1)}, u32[]{:S(2)}, u32[]{:S(2)}) collective-permute-start(bf16[2,2,128,128]{3,2,1,0:T(8,128)(2,1)S(1)} %collective-permute-done.2.refs_3_), channel_id=1, source_target_pairs={{0,1},{1,0},{2,3},{3,2},{4,5},{5,4},{6,7},{7,6},{8,9},{9,8},{10,11... | collective-permute-start | bytes 393224 | tf_op jit(solution)/shard_map/ppermute | solution.py:367
  13.2 6.7 %collective-permute-start.6 = (bf16[2,2,128,128]{3,2,1,0:T(8,128)(2,1)S(1)}, bf16[2,2,128,128]{3,2,1,0:T(8,128)(2,1)S(1)}, u32[]{:S(2)}, u32[]{:S(2)}) collective-permute-start(bf16[2,2,128,128]{3,2,1,0:T(8,128)(2,1)S(1)} %collective-permute-done.3.refs_4_), channel_id=1, source_target_pairs={{0,1},{1,0},{2,3},{3,2},{4,5},{5,4},{6,7},{7,6},{8,9},{9,8},{10,11... | collective-permute-start | bytes 393224 | tf_op jit(solution)/shard_map/ppermute | solution.py:367
  13.5 6.4 %collective-permute-start = (bf16[2,128,128]{2,1,0:T(8,128)(2,1)S(1)}, bf16[2,128,128]{2,1,0:T(8,128)(2,1)S(1)}, u32[]{:S(2)}, u32[]{:S(2)}) collective-permute-start(bf16[2,128,128]{2,1,0:T(8,128)(2,1)S(1)} %get-tuple-element.25), channel_id=1, source_target_pairs={{0,1},{1,0},{2,3},{3,2},{4,5},{5,4},{6,7},{7,6},{8,9},{9,8},{10,11... | collective-permute-start | bytes 196616 | tf_op jit(solution)/shard_map/ppermute | solution.py:367

commit v10 on v9

--- a/solution.py
+++ b/solution.py
@@ -149,10 +149,13 @@
         owns.append(
             jnp.concatenate(
                 [
-                    jnp.sum(
-                        q[k * PER:(k + 1) * PER] * new[0:1, k * HEAD:(k + 1) * HEAD],
-                        axis=1,
-                        keepdims=True,
+                    jnp.broadcast_to(
+                        jnp.sum(
+                            q[k * PER:(k + 1) * PER] * new[0:1, k * HEAD:(k + 1) * HEAD],
+                            axis=1,
+                            keepdims=True,
+                        ),
+                        (PER, HEAD),
                     )
                     for k in range(KVH)
                 ],
@@ -178,10 +181,10 @@
     weights, own_weights, shares = [], [], []
     for r in range(requests):
         top = jnp.maximum(jnp.max(raws[r], axis=1, keepdims=True), owns[r])
-        weight = jnp.exp2((raws[r] - top) * (SCALE * LOG2E))
+        weight = jnp.exp2((raws[r] - top[:, :raws[r].shape[1]]) * (SCALE * LOG2E))
         own_weight = jnp.exp2((owns[r] - top) * (SCALE * LOG2E))
         total = jnp.sum(weight, axis=1, keepdims=True) + own_weight
-        stat_ref[r] = jnp.broadcast_to(top * SCALE + jnp.log(total), (HEADS, HEAD))
+        stat_ref[r] = top * SCALE + jnp.log(total)
         shares.append(1.0 / total)
         weights.append(weight.astype(jnp.bfloat16))
         own_weights.append(own_weight.astype(jnp.bfloat16).astype(jnp.float32))

time: 32.5 us -> 32.5 us (level)
  transfers between devices with their start and end apart: 8 -> 8, of which waited for: 1 -> 1; matrix products, arithmetic and copies ran while one was open for 0% -> 0% of each run, Pallas kernels for 9% -> 8%
where the time goes in v10:
time: 32.5 us; the launch traced here: 32.1 us
  starting transfers between devices  11.9 us (37%)
  blocking collectives  10.3 us (32%)
  Pallas kernels  6.28 us (19%)
  waiting for transfers between devices  3.55 us (11%)
    all_to_all x1, blocking collectives, on_device(): lax.all_to_all(back, everyone, split_axis=0, concat_axis=0, tiled=True, a...  10.3 us
    all_to_all x1, starting transfers between devices, on_device(): lax.all_to_all(outgoing, everyone, split_axis=0, concat_axis=0, tiled=Tru...  6.25 us
    ppermute x7, starting transfers between devices, swap(): return lax.ppermute(block, 'seq', [(s, s ^ j) for s in range(seq)])  5.68 us
    all_to_all x1, waiting for transfers between devices, on_device(): lax.all_to_all(outgoing, everyone, split_axis=0, concat_axis=0, tiled=Tru...  3.53 us
    pallas_call x1, Pallas kernels, on_device(): pl.pallas_call(suffix_kernel, out_shape=(pltpu.VMEM((requests, HEADS, HEA...  2.58 us
    pallas_call x1, Pallas kernels, on_device(): pl.pallas_call(functools.partial(prepare, groups, splits), out_shape=[jax...  1.75 us
    pallas_call x1, Pallas kernels, on_device(): pl.pallas_call(functools.partial(prefix_kernel, splits), out_shape=pltpu....  1 us
    pallas_call x1, Pallas kernels, on_device(): pl.pallas_call(functools.partial(join_kernel, splits), out_shape=jax.Shap...  0.94 us
  transfers between devices with their start and end apart: 8, of which 1 were waited for; matrix products, arithmetic and copies ran while one was open for 0% of the time, Pallas kernels for 8%

profile of v10, /device:TPU:0, one launch (start us, length us, event | category | flops | bytes accessed | tf_op | source)
XLA Modules:
  0.0 32.1 jit_solution(12444166564456555497)
XLA Ops:
  0.0 1.8 %prepare.1 = (bf16[32,16,128]{2,1,0:T(8,128)(2,1)}, f32[4,64,128]{2,1,0:T(8,128)S(1)}, s32[4]{0:T(128)S(4)}, bf16[2,128,128]{2,1,0:T(8,128)(2,1)S(1)}, bf16[2,12...) custom-call(s32[4]{0:T(128)} %bitcast.1, ...), custom_call_target="tpu_custom_call" | custom-call | tf_op jit(solution)/shard_map/prepare/pallas_call | solution.py:350
  1.8 4.0 %collective-permute-start.1 = (bf16[2,2,128,128]{3,2,1,0:T(8,128)(2,1)S(1)}, bf16[2,2,128,128]{3,2,1,0:T(8,128)(2,1)S(1)}, u32[]{:S(2)}, u32[]{:S(2)}) collective-permute-start(bf16[2,2,128,128]{3,2,1,0:T(8,128)(2,1)S(1)} %get-tuple-element.26), channel_id=1, source_target_pairs={{0,6},{1,7},{2,4},{3,5},{4,2},{5,3},{6,0},{7,1},{8,14},{9,15},{10,... | collective-permute-start | bytes 393224 | tf_op jit(solution)/shard_map/ppermute | solution.py:370
  5.7 0.5 %collective-permute-start.2 = (bf16[2,2,128,128]{3,2,1,0:T(8,128)(2,1)S(1)}, bf16[2,2,128,128]{3,2,1,0:T(8,128)(2,1)S(1)}, u32[]{:S(2)}, u32[]{:S(2)}) collective-permute-start(bf16[2,2,128,128]{3,2,1,0:T(8,128)(2,1)S(1)} %get-tuple-element.27), channel_id=1, source_target_pairs={{0,4},{1,5},{2,6},{3,7},{4,0},{5,1},{6,2},{7,3},{8,12},{9,13},{10,... | collective-permute-start | bytes 393224 | tf_op jit(solution)/shard_map/ppermute | solution.py:370
  6.2 0.1 collective-permute-start.3
  6.4 6.3 %all-to-all-start = ((bf16[32,16,128]{2,1,0:T(8,128)(2,1)}), bf16[32,16,128]{2,1,0:T(8,128)(2,1)S(1)}, u32[]{:S(2)}, u32[]{:S(2)}) async-start(bf16[32,16,128]{2,1,0:T(8,128)(2,1)} %get-tuple-element.19), calls=%async_computation | async-start | bytes 262144 | tf_op jit(solution)/shard_map/all_to_all | solution.py:376
  12.6 0.0 collective-permute-done.1.refs_2_
  12.6 0.3 collective-permute-start.4
  12.9 0.0 collective-permute-done.2.refs_3_
  13.0 0.3 collective-permute-start.5
  13.2 0.0 collective-permute-done.3.refs_4_
  13.2 0.3 collective-permute-start.6
  13.5 0.3 collective-permute-start
  13.7 2.6 %suffix_attention.1 = (f32[4,64,128]{2,1,0:T(8,128)S(1)}, f32[4,64,128]{2,1,0:T(8,128)S(1)}) custom-call(s32[4]{0:T(128)} %len_in.1, f32[4,64,128]{2,1,0:T(8,128)S(1)} %get-tuple-element.20.rows_ref, bf16[4,2,1024]{2,1,0:T(2,128)(2,1)} %new_in.1, bf16[4,2,128,1024]{3,2,1,0:T(8,128)(2,1)} %kv_in.1), custom_call_target="tpu_custom_call" | custom-call | flops 134217728 | bytes 2097152 | tf_op jit(solution)/shard_map/suffix_attention/pallas_call | solution.py:380
  16.3 3.5 %all-to-all-done.q_ref = bf16[32,16,128]{2,1,0:T(8,128)(2,1)S(1)} async-done(((bf16[32,16,128]{2,1,0:T(8,128)(2,1)}), bf16[32,16,128]{2,1,0:T(8,128)(2,1)S(1)}, u32[]{:S(2)}, u32[]{:S(2)}) %all-to-all-start) | async-done | bytes 131104 | tf_op jit(solution)/shard_map/all_to_all | solution.py:376
  19.9 0.0 collective-permute-done.refs_1_
  19.9 0.0 collective-permute-done.4.refs_5_
  19.9 0.0 collective-permute-done.5.refs_6_
  19.9 0.0 collective-permute-done.6.refs_7_
  19.9 1.0 %prefix_attention.1 = bf16[288,2,128]{2,1,0:T(2,128)(2,1)S(1)} custom-call(bf16[32,16,128]{2,1,0:T(8,128)(2,1)S(1)} %all-to-all-done.q_ref, bf16[2,128,128]{2,1,0:T(8,128)(2,1)S(1)} %get-tuple-element.24.refs_0_, bf16[2,128,128]{2,1,0:T(8,128)(2,1)S(1)} %collective-permute-done.refs_1_, bf16[2,2,128,128]{3,2,1,0:T(8,128)(2,1)S(1)} %collective-permute-done.1.refs_2_, ...), custom_call_target="tpu_custom_call" | custom-call | tf_op jit(solution)/shard_map/prefix_attention/pallas_call | solution.py:407
  20.9 10.3 %all_to_all.10.back_ref = bf16[288,2,128]{2,1,0:T(2,128)(2,1)S(1)} all-to-all(bf16[288,2,128]{2,1,0:T(2,128)(2,1)S(1)} %prefix_attention.1), channel_id=1, replica_groups={{24,16,8,0,25,17,9,1,26,18,10,2,27,19,11,3,28,20,12,4,29,21,13,5,30,22,..., dimensions={0} | all-to-all | bytes 294912 | tf_op jit(solution)/shard_map/all_to_all | solution.py:417
  31.2 0.9 %join.1 = bf16[4,8192]{1,0:T(4,128)(2,1)} custom-call(s32[4]{0:T(128)S(4)} %get-tuple-element.18.routes_ref, bf16[288,2,128]{2,1,0:T(2,128)(2,1)S(1)} %all_to_all.10.back_ref, f32[4,64,128]{2,1,0:T(8,128)S(1)} %get-tuple-element.29.suffix_ref, f32[4,64,128]{2,1,0:T(8,128)S(1)} %get-tuple-element.30.stat_ref), custom_call_target="tpu_custom_call" | custom-call | tf_op jit(solution)/shard_map/join/pallas_call | solution.py:422
Async XLA Ops:
  1.8 10.9 %collective-permute-start.1 = (bf16[2,2,128,128]{3,2,1,0:T(8,128)(2,1)S(1)}, bf16[2,2,128,128]{3,2,1,0:T(8,128)(2,1)S(1)}, u32[]{:S(2)}, u32[]{:S(2)}) collective-permute-start(bf16[2,2,128,128]{3,2,1,0:T(8,128)(2,1)S(1)} %get-tuple-element.26), channel_id=1, source_target_pairs={{0,6},{1,7},{2,4},{3,5},{4,2},{5,3},{6,0},{7,1},{8,14},{9,15},{10,... | collective-permute-start | bytes 393224 | tf_op jit(solution)/shard_map/ppermute | solution.py:370
  5.7 7.2 %collective-permute-start.2 = (bf16[2,2,128,128]{3,2,1,0:T(8,128)(2,1)S(1)}, bf16[2,2,128,128]{3,2,1,0:T(8,128)(2,1)S(1)}, u32[]{:S(2)}, u32[]{:S(2)}) collective-permute-start(bf16[2,2,128,128]{3,2,1,0:T(8,128)(2,1)S(1)} %get-tuple-element.27), channel_id=1, source_target_pairs={{0,4},{1,5},{2,6},{3,7},{4,0},{5,1},{6,2},{7,3},{8,12},{9,13},{10,... | collective-permute-start | bytes 393224 | tf_op jit(solution)/shard_map/ppermute | solution.py:370
  6.2 7.0 %collective-permute-start.3 = (bf16[2,2,128,128]{3,2,1,0:T(8,128)(2,1)S(1)}, bf16[2,2,128,128]{3,2,1,0:T(8,128)(2,1)S(1)}, u32[]{:S(2)}, u32[]{:S(2)}) collective-permute-start(bf16[2,2,128,128]{3,2,1,0:T(8,128)(2,1)S(1)} %get-tuple-element.28), channel_id=1, source_target_pairs={{0,2},{1,3},{2,0},{3,1},{4,6},{5,7},{6,4},{7,5},{8,10},{9,11},{10,... | collective-permute-start | bytes 393224 | tf_op jit(solution)/shard_map/ppermute | solution.py:370
  6.4 13.5 %all-to-all-start = ((bf16[32,16,128]{2,1,0:T(8,128)(2,1)}), bf16[32,16,128]{2,1,0:T(8,128)(2,1)S(1)}, u32[]{:S(2)}, u32[]{:S(2)}) async-start(bf16[32,16,128]{2,1,0:T(8,128)(2,1)} %get-tuple-element.19), calls=%async_computation | async-start | bytes 262144 | tf_op jit(solution)/shard_map/all_to_all | solution.py:376
  12.6 7.2 %collective-permute-start.4 = (bf16[2,2,128,128]{3,2,1,0:T(8,128)(2,1)S(1)}, bf16[2,2,128,128]{3,2,1,0:T(8,128)(2,1)S(1)}, u32[]{:S(2)}, u32[]{:S(2)}) collective-permute-start(bf16[2,2,128,128]{3,2,1,0:T(8,128)(2,1)S(1)} %collective-permute-done.1.refs_2_), channel_id=1, source_target_pairs={{0,1},{1,0},{2,3},{3,2},{4,5},{5,4},{6,7},{7,6},{8,9},{9,8},{10,11... | collective-permute-start | bytes 393224 | tf_op jit(solution)/shard_map/ppermute | solution.py:370
  13.0 6.9 %collective-permute-start.5 = (bf16[2,2,128,128]{3,2,1,0:T(8,128)(2,1)S(1)}, bf16[2,2,128,128]{3,2,1,0:T(8,128)(2,1)S(1)}, u32[]{:S(2)}, u32[]{:S(2)}) collective-permute-start(bf16[2,2,128,128]{3,2,1,0:T(8,128)(2,1)S(1)} %collective-permute-done.2.refs_3_), channel_id=1, source_target_pairs={{0,1},{1,0},{2,3},{3,2},{4,5},{5,4},{6,7},{7,6},{8,9},{9,8},{10,11... | collective-permute-start | bytes 393224 | tf_op jit(solution)/shard_map/ppermute | solution.py:370
  13.2 6.7 %collective-permute-start.6 = (bf16[2,2,128,128]{3,2,1,0:T(8,128)(2,1)S(1)}, bf16[2,2,128,128]{3,2,1,0:T(8,128)(2,1)S(1)}, u32[]{:S(2)}, u32[]{:S(2)}) collective-permute-start(bf16[2,2,128,128]{3,2,1,0:T(8,128)(2,1)S(1)} %collective-permute-done.3.refs_4_), channel_id=1, source_target_pairs={{0,1},{1,0},{2,3},{3,2},{4,5},{5,4},{6,7},{7,6},{8,9},{9,8},{10,11... | collective-permute-start | bytes 393224 | tf_op jit(solution)/shard_map/ppermute | solution.py:370
  13.5 6.4 %collective-permute-start = (bf16[2,128,128]{2,1,0:T(8,128)(2,1)S(1)}, bf16[2,128,128]{2,1,0:T(8,128)(2,1)S(1)}, u32[]{:S(2)}, u32[]{:S(2)}) collective-permute-start(bf16[2,128,128]{2,1,0:T(8,128)(2,1)S(1)} %get-tuple-element.25), channel_id=1, source_target_pairs={{0,1},{1,0},{2,3},{3,2},{4,5},{5,4},{6,7},{7,6},{8,9},{9,8},{10,11... | collective-permute-start | bytes 196616 | tf_op jit(solution)/shard_map/ppermute | solution.py:370
